TPU v7x, 256 devices: a whole 4x4x8 slice. The times are simulated.
256 devices in a mesh: row: 16 (over x_lo, y, core), col: 16 (over z, x_hi).
Axes of the slice: x: 4 (x_hi: 2, x_lo: 2; x = x_hi * 2 + x_lo), y: 4, z: 8, core: 2. Of those that a mesh axis runs over, the one named last changes fastest.
Arguments:
- tokens: bfloat16 [6144, 16384], P('row', 'col'), may hold values from -6 to 6
- gate_weight: bfloat16 [16384, 26624], P('row', 'col'), may hold values from -0.046875 to 0.046875
Outputs:
- gate_partial: float32 [6144, 26624], P('row', 'col')
All inputs are finite; a program needn't handle non-finite values.
Results may differ from a plain program's by a relative error of at most 0.0003.
Values may be sent and summed in bfloat16 or wider, within the bound.
No kernel may reach another device: no remote copies, remote signals or barrier semaphores. Data moves between devices by JAX's collectives and lax.ppermute only.
A program may use at most 64 MiB of HBM per device.

v0:
```python
import jax
import jax.numpy as jnp
from jax import lax
from jax.sharding import PartitionSpec as P

STEPS = 4


def passed_along(x, axis, by):
    peers = lax.axis_size(axis)
    return lax.ppermute(x, axis, [(i, (i + by) % peers) for i in range(peers)])


def skew_tokens(tile, offset, bit_count):
    for level in range(bit_count):
        arrived = passed_along(tile, "col", -(1 << level))
        tile = jnp.where(offset >> level & 1 == 1, arrived, tile)
    return tile


def skew_weights(weights, offset, bit_count):
    for level in range(bit_count):
        arrived = passed_along(weights, "row", -(1 << level))
        weights = jnp.where(offset >> level & 1 == 1, arrived, weights)
    return weights


def on_device(tokens, gate_weight):
    row_index = lax.axis_index("row")
    col_index = lax.axis_index("col")
    rows_count = lax.axis_size("row")
    cols_count = lax.axis_size("col")
    ratio = rows_count // cols_count
    row_bits = rows_count.bit_length() - 1
    col_bits = cols_count.bit_length() - 1
    block_rows = gate_weight.shape[0]
    tile_count = (ratio + STEPS - 2) // ratio + 1
    tile = skew_tokens(tokens, row_index // ratio, col_bits)
    tiles = [tile]
    for number in range(1, tile_count):
        tile = passed_along(tile, "col", -1)
        tiles.append(tile)
    slab = jnp.concatenate(tiles, axis=1)
    lead = row_index % ratio
    first = skew_weights(gate_weight, ratio * col_index % rows_count, row_bits)
    moving = [first]
    current = first
    for advance in range(1, STEPS):
        current = passed_along(current, "row", -1)
        moving.append(current)
    running = None
    for advance in range(STEPS):
        operand = lax.dynamic_slice_in_dim(slab, (lead + advance) * block_rows, block_rows, 1)
        partial_value = jnp.dot(operand, moving[advance], preferred_element_type=jnp.float32)
        running = partial_value if running is None else running + partial_value
    return running


def solution(mesh):
    placed = (P("row", "col"), P("row", "col"))
    return jax.shard_map(
        on_device, mesh=mesh, in_specs=placed, out_specs=P("row", "col"), check_vma=False
    )
```

profile of v0, /device:TPU:2, one launch (start us, length us, event | category | flops | bytes accessed | tf_op | source)
XLA Modules:
  0.0 511.4 jit_solution(1949435123548365820)
XLA Ops:
  0.0 2.4 collective-permute-start.4
  2.4 37.9 %collective-permute-done.4 = bf16[1024,1664]{1,0:T(8,128)(2,1)} collective-permute-done((bf16[1024,1664]{1,0:T(8,128)(2,1)}, bf16[1024,1664]{1,0:T(8,128)(2,1)}, u32[]{:S(2)}, u32[]{:S(2)}) %collective-permute-start.4) | collective-permute-done | bytes 3407904 | tf_op jit(solution)/shard_map/ppermute | solution.py:11
  40.3 2.3 broadcast_select_fusion
  43.5 0.9 copy-done.1
  44.4 73.5 %collective-permute-done.5 = bf16[1024,1664]{1,0:T(8,128)(2,1)} collective-permute-done((bf16[1024,1664]{1,0:T(8,128)(2,1)S(1)}, bf16[1024,1664]{1,0:T(8,128)(2,1)}, u32[]{:S(2)}, u32[]{:S(2)}) %collective-permute-start.5) | collective-permute-done | bytes 3407904 | tf_op jit(solution)/shard_map/ppermute | solution.py:11
  117.9 2.3 broadcast_select_fusion.1
  120.4 1.7 copy-done
  122.0 75.4 %collective-permute-done.6 = bf16[1024,1664]{1,0:T(8,128)(2,1)} collective-permute-done((bf16[1024,1664]{1,0:T(8,128)(2,1)S(1)}, bf16[1024,1664]{1,0:T(8,128)(2,1)}, u32[]{:S(2)}, u32[]{:S(2)}) %collective-permute-start.6) | collective-permute-done | bytes 3407904 | tf_op jit(solution)/shard_map/ppermute | solution.py:11
  197.4 2.3 broadcast_select_fusion.2
  199.7 1.6 collective-permute-start.7
  201.3 73.9 %collective-permute-done.7 = bf16[1024,1664]{1,0:T(8,128)(2,1)} collective-permute-done((bf16[1024,1664]{1,0:T(8,128)(2,1)S(1)}, bf16[1024,1664]{1,0:T(8,128)(2,1)}, u32[]{:S(2)}, u32[]{:S(2)}) %collective-permute-start.7) | collective-permute-done | bytes 3407904 | tf_op jit(solution)/shard_map/ppermute | solution.py:11
  275.6 1.7 copy-done.2
  277.3 2.7 collective-permute-start.9
  280.0 9.7 %collective-permute-start = (bf16[384,1024]{1,0:T(8,128)(2,1)}, bf16[384,1024]{1,0:T(8,128)(2,1)S(1)}, u32[]{:S(2)}, u32[]{:S(2)}) collective-permute-start(bf16[384,1024]{1,0:T(8,128)(2,1)} %param.2), channel_id=1, source_target_pairs={{0,15},{1,0},{2,1},{3,2},{4,3},{5,4},{6,5},{7,6},{8,7},{9,8},{10,9... | collective-permute-start | bytes 2359304 | tf_op jit(solution)/shard_map/ppermute | solution.py:11
  289.7 44.7 %collective-permute-done.9 = bf16[1024,1664]{1,0:T(8,128)(2,1)} collective-permute-done((bf16[1024,1664]{1,0:T(8,128)(2,1)S(1)}, bf16[1024,1664]{1,0:T(8,128)(2,1)}, u32[]{:S(2)}, u32[]{:S(2)}) %collective-permute-start.9) | collective-permute-done | bytes 3407904 | tf_op jit(solution)/shard_map/ppermute | solution.py:11
  334.4 4.1 collective-permute-start.11
  338.5 1.2 broadcast_select_fusion.4
  339.8 7.9 %collective-permute-start.1 = (bf16[384,1024]{1,0:T(8,128)(2,1)S(1)}, bf16[384,1024]{1,0:T(8,128)(2,1)S(1)}, u32[]{:S(2)}, u32[]{:S(2)}) collective-permute-start(bf16[384,1024]{1,0:T(8,128)(2,1)S(1)} %broadcast_select_fusion.4), channel_id=1, source_target_pairs={{0,14},{1,15},{2,0},{3,1},{4,2},{5,3},{6,4},{7,5},{8,6},{9,7},{10,... | collective-permute-start | bytes 2359304 | tf_op jit(solution)/shard_map/ppermute | solution.py:11
  347.7 22.0 %collective-permute-done.1 = bf16[384,1024]{1,0:T(8,128)(2,1)S(1)} collective-permute-done((bf16[384,1024]{1,0:T(8,128)(2,1)S(1)}, bf16[384,1024]{1,0:T(8,128)(2,1)S(1)}, u32[]{:S(2)}, u32[]{:S(2)}) %collective-permute-start.1) | collective-permute-done | bytes 786464 | tf_op jit(solution)/shard_map/ppermute | solution.py:11
  369.9 17.7 %collective-permute-done.2 = bf16[384,1024]{1,0:T(8,128)(2,1)S(1)} collective-permute-done((bf16[384,1024]{1,0:T(8,128)(2,1)S(1)}, bf16[384,1024]{1,0:T(8,128)(2,1)S(1)}, u32[]{:S(2)}, u32[]{:S(2)}) %collective-permute-start.2) | collective-permute-done | bytes 786464 | tf_op jit(solution)/shard_map/ppermute | solution.py:11
  387.8 2.1 collective-permute-start.3
  389.8 14.8 %collective-permute-start.13 = (bf16[1024,1664]{1,0:T(8,128)(2,1)}, bf16[1024,1664]{1,0:T(8,128)(2,1)}, u32[]{:S(2)}, u32[]{:S(2)}) collective-permute-start(bf16[1024,1664]{1,0:T(8,128)(2,1)} %collective-permute-done.11), channel_id=1, source_target_pairs={{0,240},{16,0},{32,16},{48,32},{64,48},{80,64},{96,80},{112,96},{1... | collective-permute-start | bytes 10223624 | tf_op jit(solution)/shard_map/ppermute | solution.py:11
  404.6 6.4 %collective-permute-done.3 = bf16[384,1024]{1,0:T(8,128)(2,1)S(1)} collective-permute-done((bf16[384,1024]{1,0:T(8,128)(2,1)S(1)}, bf16[384,1024]{1,0:T(8,128)(2,1)S(1)}, u32[]{:S(2)}, u32[]{:S(2)}) %collective-permute-start.3) | collective-permute-done | bytes 786464 | tf_op jit(solution)/shard_map/ppermute | solution.py:11
  411.1 20.9 %collective-permute-start.8 = (bf16[384,1024]{1,0:T(8,128)(2,1)S(1)}, bf16[384,1024]{1,0:T(8,128)(2,1)S(1)}, u32[]{:S(2)}, u32[]{:S(2)}) collective-permute-start(bf16[384,1024]{1,0:T(8,128)(2,1)S(1)} %broadcast_select_fusion.7), channel_id=1, source_target_pairs={{0,15},{1,0},{2,1},{3,2},{4,3},{5,4},{6,5},{7,6},{8,7},{9,8},{10,9... | collective-permute-start | bytes 2359304 | tf_op jit(solution)/shard_map/ppermute | solution.py:11
  432.0 47.3 %collective-permute-done.8 = bf16[384,1024]{1,0:T(8,128)(2,1)S(1)} collective-permute-done((bf16[384,1024]{1,0:T(8,128)(2,1)S(1)}, bf16[384,1024]{1,0:T(8,128)(2,1)S(1)}, u32[]{:S(2)}, u32[]{:S(2)}) %collective-permute-start.8) | collective-permute-done | bytes 786464 | tf_op jit(solution)/shard_map/ppermute | solution.py:11
  479.4 13.5 %collective-permute-done.10 = bf16[384,1024]{1,0:T(8,128)(2,1)S(1)} collective-permute-done((bf16[384,1024]{1,0:T(8,128)(2,1)S(1)}, bf16[384,1024]{1,0:T(8,128)(2,1)S(1)}, u32[]{:S(2)}, u32[]{:S(2)}) %collective-permute-start.10) | collective-permute-done | bytes 786464 | tf_op jit(solution)/shard_map/ppermute | solution.py:11
  492.9 2.2 collective-permute-start.12
  495.1 3.6 fusion
  498.6 1.6 convolution_add_fusion.2
  500.3 3.6 convolution_add_fusion.1
  503.8 2.5 collective-permute-done.12
  506.4 5.1 convolution_add_fusion
  (16 shorter events, 1.6 us)
Async XLA Ops:
  0.0 40.3 %collective-permute-start.4 = (bf16[1024,1664]{1,0:T(8,128)(2,1)}, bf16[1024,1664]{1,0:T(8,128)(2,1)}, u32[]{:S(2)}, u32[]{:S(2)}) collective-permute-start(bf16[1024,1664]{1,0:T(8,128)(2,1)} %param.3), channel_id=1, source_target_pairs={{0,240},{16,0},{32,16},{48,32},{64,48},{80,64},{96,80},{112,96},{1... | collective-permute-start | bytes 10223624 | tf_op jit(solution)/shard_map/ppermute | solution.py:11
  42.7 1.8 copy-start.1
  42.7 75.2 %collective-permute-start.5 = (bf16[1024,1664]{1,0:T(8,128)(2,1)S(1)}, bf16[1024,1664]{1,0:T(8,128)(2,1)}, u32[]{:S(2)}, u32[]{:S(2)}) collective-permute-start(bf16[1024,1664]{1,0:T(8,128)(2,1)S(1)} %broadcast_select_fusion), channel_id=1, source_target_pairs={{0,224},{16,240},{32,0},{48,16},{64,32},{80,48},{96,64},{112,80},{... | collective-permute-start | bytes 10223624 | tf_op jit(solution)/shard_map/ppermute | solution.py:11
  120.3 1.8 copy-start
  120.3 77.1 %collective-permute-start.6 = (bf16[1024,1664]{1,0:T(8,128)(2,1)S(1)}, bf16[1024,1664]{1,0:T(8,128)(2,1)}, u32[]{:S(2)}, u32[]{:S(2)}) collective-permute-start(bf16[1024,1664]{1,0:T(8,128)(2,1)S(1)} %broadcast_select_fusion.1), channel_id=1, source_target_pairs={{0,192},{16,208},{32,224},{48,240},{64,0},{80,16},{96,32},{112,48}... | collective-permute-start | bytes 10223624 | tf_op jit(solution)/shard_map/ppermute | solution.py:11
  199.7 75.5 %collective-permute-start.7 = (bf16[1024,1664]{1,0:T(8,128)(2,1)S(1)}, bf16[1024,1664]{1,0:T(8,128)(2,1)}, u32[]{:S(2)}, u32[]{:S(2)}) collective-permute-start(bf16[1024,1664]{1,0:T(8,128)(2,1)S(1)} %broadcast_select_fusion.2), channel_id=1, source_target_pairs={{0,128},{16,144},{32,160},{48,176},{64,192},{80,208},{96,224},{112... | collective-permute-start | bytes 10223624 | tf_op jit(solution)/shard_map/ppermute | solution.py:11
  275.6 1.7 copy-start.2
  277.3 57.1 %collective-permute-start.9 = (bf16[1024,1664]{1,0:T(8,128)(2,1)S(1)}, bf16[1024,1664]{1,0:T(8,128)(2,1)}, u32[]{:S(2)}, u32[]{:S(2)}) collective-permute-start(bf16[1024,1664]{1,0:T(8,128)(2,1)S(1)} %broadcast_select_fusion.3), channel_id=1, source_target_pairs={{0,240},{16,0},{32,16},{48,32},{64,48},{80,64},{96,80},{112,96},{1... | collective-permute-start | bytes 10223624 | tf_op jit(solution)/shard_map/ppermute | solution.py:11
  280.0 58.5 %collective-permute-start = (bf16[384,1024]{1,0:T(8,128)(2,1)}, bf16[384,1024]{1,0:T(8,128)(2,1)S(1)}, u32[]{:S(2)}, u32[]{:S(2)}) collective-permute-start(bf16[384,1024]{1,0:T(8,128)(2,1)} %param.2), channel_id=1, source_target_pairs={{0,15},{1,0},{2,1},{3,2},{4,3},{5,4},{6,5},{7,6},{8,7},{9,8},{10,9... | collective-permute-start | bytes 2359304 | tf_op jit(solution)/shard_map/ppermute | solution.py:11
  334.4 55.4 %collective-permute-start.11 = (bf16[1024,1664]{1,0:T(8,128)(2,1)}, bf16[1024,1664]{1,0:T(8,128)(2,1)}, u32[]{:S(2)}, u32[]{:S(2)}) collective-permute-start(bf16[1024,1664]{1,0:T(8,128)(2,1)} %collective-permute-done.9), channel_id=1, source_target_pairs={{0,240},{16,0},{32,16},{48,32},{64,48},{80,64},{96,80},{112,96},{1... | collective-permute-start | bytes 10223624 | tf_op jit(solution)/shard_map/ppermute | solution.py:11
  339.8 30.0 %collective-permute-start.1 = (bf16[384,1024]{1,0:T(8,128)(2,1)S(1)}, bf16[384,1024]{1,0:T(8,128)(2,1)S(1)}, u32[]{:S(2)}, u32[]{:S(2)}) collective-permute-start(bf16[384,1024]{1,0:T(8,128)(2,1)S(1)} %broadcast_select_fusion.4), channel_id=1, source_target_pairs={{0,14},{1,15},{2,0},{3,1},{4,2},{5,3},{6,4},{7,5},{8,6},{9,7},{10,... | collective-permute-start | bytes 2359304 | tf_op jit(solution)/shard_map/ppermute | solution.py:11
  369.8 17.8 %collective-permute-start.2 = (bf16[384,1024]{1,0:T(8,128)(2,1)S(1)}, bf16[384,1024]{1,0:T(8,128)(2,1)S(1)}, u32[]{:S(2)}, u32[]{:S(2)}) collective-permute-start(bf16[384,1024]{1,0:T(8,128)(2,1)S(1)} %broadcast_select_fusion.5), channel_id=1, source_target_pairs={{0,12},{1,13},{2,14},{3,15},{4,0},{5,1},{6,2},{7,3},{8,4},{9,5},{1... | collective-permute-start | bytes 2359304 | tf_op jit(solution)/shard_map/ppermute | solution.py:11
  387.8 23.3 %collective-permute-start.3 = (bf16[384,1024]{1,0:T(8,128)(2,1)S(1)}, bf16[384,1024]{1,0:T(8,128)(2,1)S(1)}, u32[]{:S(2)}, u32[]{:S(2)}) collective-permute-start(bf16[384,1024]{1,0:T(8,128)(2,1)S(1)} %broadcast_select_fusion.6), channel_id=1, source_target_pairs={{0,8},{1,9},{2,10},{3,11},{4,12},{5,13},{6,14},{7,15},{8,0},{9,1},... | collective-permute-start | bytes 2359304 | tf_op jit(solution)/shard_map/ppermute | solution.py:11
  389.8 116.5 %collective-permute-start.13 = (bf16[1024,1664]{1,0:T(8,128)(2,1)}, bf16[1024,1664]{1,0:T(8,128)(2,1)}, u32[]{:S(2)}, u32[]{:S(2)}) collective-permute-start(bf16[1024,1664]{1,0:T(8,128)(2,1)} %collective-permute-done.11), channel_id=1, source_target_pairs={{0,240},{16,0},{32,16},{48,32},{64,48},{80,64},{96,80},{112,96},{1... | collective-permute-start | bytes 10223624 | tf_op jit(solution)/shard_map/ppermute | solution.py:11
  411.1 87.5 %copy-start.3 = (bf16[1024,1664]{1,0:T(8,128)(2,1)S(1)}, bf16[1024,1664]{1,0:T(8,128)(2,1)}, u32[]{:S(2)}) copy-start(bf16[1024,1664]{1,0:T(8,128)(2,1)} %copy-done.2) | copy-start | bytes 10223620
  411.1 68.2 %collective-permute-start.8 = (bf16[384,1024]{1,0:T(8,128)(2,1)S(1)}, bf16[384,1024]{1,0:T(8,128)(2,1)S(1)}, u32[]{:S(2)}, u32[]{:S(2)}) collective-permute-start(bf16[384,1024]{1,0:T(8,128)(2,1)S(1)} %broadcast_select_fusion.7), channel_id=1, source_target_pairs={{0,15},{1,0},{2,1},{3,2},{4,3},{5,4},{6,5},{7,6},{8,7},{9,8},{10,9... | collective-permute-start | bytes 2359304 | tf_op jit(solution)/shard_map/ppermute | solution.py:11
  479.4 13.5 %collective-permute-start.10 = (bf16[384,1024]{1,0:T(8,128)(2,1)S(1)}, bf16[384,1024]{1,0:T(8,128)(2,1)S(1)}, u32[]{:S(2)}, u32[]{:S(2)}) collective-permute-start(bf16[384,1024]{1,0:T(8,128)(2,1)S(1)} %collective-permute-done.8), channel_id=1, source_target_pairs={{0,15},{1,0},{2,1},{3,2},{4,3},{5,4},{6,5},{7,6},{8,7},{9,8},{10,9... | collective-permute-start | bytes 2359304 | tf_op jit(solution)/shard_map/ppermute | solution.py:11
  492.9 13.5 %collective-permute-start.12 = (bf16[384,1024]{1,0:T(8,128)(2,1)S(1)}, bf16[384,1024]{1,0:T(8,128)(2,1)S(1)}, u32[]{:S(2)}, u32[]{:S(2)}) collective-permute-start(bf16[384,1024]{1,0:T(8,128)(2,1)S(1)} %collective-permute-done.10), channel_id=1, source_target_pairs={{0,15},{1,0},{2,1},{3,2},{4,3},{5,4},{6,5},{7,6},{8,7},{9,8},{10,9... | collective-permute-start | bytes 2359304 | tf_op jit(solution)/shard_map/ppermute | solution.py:11
where the time goes:
time: 512 us; the launch traced here: 511 us
  waiting for transfers between devices  415 us (81%)
  starting transfers between devices  69.5 us (14%)
  matrix products  13.8 us (3%)
  other arithmetic  8.83 us (2%)
    ppermute x14, waiting for transfers between devices, passed_along(): return lax.ppermute(x, axis, [(i, (i + by) % peers) for i in range(peers)])  415 us
    ppermute x14, starting transfers between devices, passed_along(): return lax.ppermute(x, axis, [(i, (i + by) % peers) for i in range(peers)])  69.5 us
    dot_general x4, matrix products, on_device(): jnp.dot(operand, moving[advance], preferred_element_type=jnp.float32)  13.8 us
  transfers between devices with their start and end apart: 14, of which 11 were waited for; matrix products, arithmetic and copies ran while one was open for 2% of the time, Pallas kernels for 0%

commit v1 on v0

v1 whole, which is shorter than its diff:
```python
import functools

import jax
import jax.numpy as jnp
import numpy as np
from jax import lax
from jax.experimental import pallas as pl
from jax.experimental.pallas import tpu as pltpu
from jax.sharding import PartitionSpec as P

XS, YS, ZS = 2, 4, 8
BOTH = ("row", "col")
PARTS = 2

ROUTES = {
    (0, 0, 3): (
        (((0, 3, 7, 6),), ((1, 1, 6, 7),)),
        (((2, 0), (1, 6, 7)), ((0, 0, 3, 7),)),
        (((1, 0), (0, 1)), ((2, 0), (0, 1))),
        (((0, 0, 1), (2, 2)), ((1, 0, 1, 2),)),
    ),
    (0, 0, 2): (
        (((2, 7),), ((2, 7),)),
        (((2, 0),), ((2, 0),)),
        (((2, 1),), ((2, 1),)),
        (((2, 2),), ((2, 2),)),
    ),
    (0, 1, 3): (
        (((1, 7, 6),), ((0, 1, 6), (2, 7))),
        (((1, 0, 3, 7),), ((1, 6, 7, 0),)),
        (((0, 0), (1, 1)), ((1, 1, 0),)),
        (((0, 2, 1),), ((1, 0, 1), (2, 2))),
    ),
    (0, 1, 2): (
        (((1, 2, 6, 7),), ((1, 3, 7, 6),)),
        (((2, 0), (0, 6, 7)), ((0, 0, 7),)),
        (((1, 1, 0),), ((1, 0, 1),)),
        (((1, 0, 1, 2),), ((0, 2, 1),)),
    ),
    (1, 0, 3): (
        (((0, 1, 5, 6), (1, 7)), ((0, 5, 6, 7),)),
        (((2, 0), (1, 6, 7)), ((1, 6, 7, 0),)),
        (((1, 1), (0, 7, 0)), ((0, 7, 0, 1),)),
        (((1, 0, 1), (0, 2)), ((0, 0, 1, 2),)),
    ),
    (1, 0, 2): (
        (((0, 7, 6),), ((0, 7, 6),)),
        (((0, 0, 7),), ((1, 0, 3, 7),)),
        (((0, 1, 0),), ((1, 1, 0),)),
        (((1, 2, 1),), ((0, 2, 1),)),
    ),
    (1, 1, 3): (
        (((0, 7, 6, 5),), ((0, 7, 6, 5),)),
        (((1, 0, 7, 6),), ((0, 0, 3, 7), (2, 6))),
        (((0, 1, 0, 7),), ((0, 1, 0), (1, 6, 7))),
        (((0, 0, 1), (2, 2)), ((0, 2, 1, 0),)),
    ),
    (1, 1, 2): (
        (((1, 1, 5, 6),), ((0, 1, 5, 6),)),
        (((0, 6, 7),), ((0, 2, 6, 7),)),
        (((1, 7, 0),), ((0, 7, 0),)),
        (((0, 0, 1),), ((1, 0, 1),)),
    ),
    (2, 0, 3): (
        (((1, 4, 5, 6),), ((0, 4, 5, 6),)),
        (((0, 5, 6, 7),), ((1, 5, 7, 6),)),
        (((1, 1, 0), (0, 6, 7)), ((0, 6), (1, 7, 0))),
        (((0, 0), (2, 1), (1, 7)), ((1, 0, 1), (0, 7))),
    ),
    (2, 0, 2): (
        (((0, 1, 5, 6),), ((0, 3, 6, 5),)),
        (((0, 2, 6, 7),), ((1, 7, 6),)),
        (((0, 0, 7),), ((1, 1, 0, 7),)),
        (((1, 0, 1),), ((0, 1, 0),)),
    ),
    (2, 1, 3): (
        (((0, 4, 5, 6),), ((1, 4, 5, 6),)),
        (((1, 7, 6, 5),), ((1, 5, 6, 7),)),
        (((0, 1, 0), (1, 6, 7)), ((0, 1, 0), (1, 6, 7))),
        (((1, 0), (2, 1), (0, 7)), ((0, 0), (2, 1), (1, 7))),
    ),
    (2, 1, 2): (
        (((1, 4, 5),), ((0, 4, 5),)),
        (((0, 5, 6),), ((1, 5, 6),)),
        (((1, 6, 7),), ((1, 6, 7),)),
        (((0, 0), (2, 7)), ((1, 0), (2, 7))),
    ),
    (3, 0, 3): (
        (((1, 4, 5), (2, 3)), ((0, 4, 5), (1, 3))),
        (((0, 6, 5, 4),), ((1, 6, 5, 4),)),
        (((1, 7, 6, 5),), ((0, 6, 7, 5),)),
        (((2, 0), (0, 7, 6)), ((1, 0), (0, 7, 6))),
    ),
    (3, 0, 2): (
        (((0, 4, 5),), ((0, 4, 5),)),
        (((1, 5, 6),), ((1, 5, 6),)),
        (((1, 6, 7),), ((1, 6, 7),)),
        (((2, 0), (1, 7)), ((2, 0), (1, 7))),
    ),
    (3, 1, 3): (
        (((1, 4, 5), (0, 3)), ((1, 4, 5), (2, 3))),
        (((1, 5, 4, 6),), ((0, 5, 4, 6),)),
        (((0, 5, 6, 7),), ((1, 5, 6, 7),)),
        (((0, 0), (1, 7, 6)), ((2, 0), (0, 7, 6))),
    ),
    (3, 1, 2): (
        (((1, 4), (2, 3)), ((1, 4), (0, 3))),
        (((1, 5, 4),), ((0, 5, 4),)),
        (((1, 6, 5),), ((1, 6, 5),)),
        (((0, 7, 6),), ((1, 7, 6),)),
    ),
    (4, 0, 3): (
        (((0, 4), (2, 2), (1, 3)), ((0, 4), (2, 2), (1, 3))),
        (((1, 4, 5), (0, 2, 3)), ((1, 5, 4), (0, 2, 3))),
        (((1, 6, 4, 5),), ((1, 6, 5, 4),)),
        (((0, 7, 6, 5),), ((0, 7, 6, 5),)),
    ),
    (4, 0, 2): (
        (((0, 4), (2, 3)), ((2, 4), (0, 3))),
        (((0, 5, 4),), ((0, 5, 4),)),
        (((1, 6, 5),), ((1, 6, 5),)),
        (((1, 7, 6),), ((1, 7, 6),)),
    ),
    (4, 1, 3): (
        (((0, 4), (1, 3, 2)), ((2, 4), (0, 3, 2))),
        (((1, 4, 3), (0, 5)), ((1, 5, 4), (0, 2, 3))),
        (((1, 6, 4, 5),), ((1, 6, 5, 4),)),
        (((0, 7, 6, 5),), ((1, 7, 6, 5),)),
    ),
    (4, 1, 2): (
        (((2, 2), (0, 3)), ((0, 2, 3),)),
        (((1, 2, 3, 4),), ((0, 3, 4),)),
        (((0, 4, 5),), ((0, 1, 5, 4),)),
        (((1, 0, 5, 6),), ((1, 2, 6, 5),)),
    ),
    (5, 0, 3): (
        (((1, 1, 2, 3),), ((1, 1), (0, 3, 2))),
        (((0, 2, 3, 4),), ((2, 4), (1, 2, 3))),
        (((1, 3, 4, 5),), ((2, 5), (1, 3, 0, 4))),
        (((1, 4, 5, 6),), ((1, 4, 5, 6),)),
    ),
    (5, 0, 2): (
        (((1, 3, 2),), ((0, 3, 2),)),
        (((1, 4, 3),), ((1, 4, 3),)),
        (((1, 5, 4),), ((1, 1, 5, 4),)),
        (((0, 2, 6, 5),), ((1, 2, 6, 5),)),
    ),
    (5, 1, 3): (
        (((2, 1), (1, 3, 2)), ((1, 3, 2, 1),)),
        (((0, 4, 3, 2),), ((0, 4, 3), (2, 2))),
        (((0, 5, 4, 3),), ((0, 5, 4), (2, 3))),
        (((1, 6, 5, 4),), ((2, 4), (0, 2, 6, 5))),
    ),
    (5, 1, 2): (
        (((1, 1, 2),), ((1, 1, 2),)),
        (((1, 2, 3),), ((1, 2, 3),)),
        (((0, 3, 4),), ((0, 3, 0, 4),)),
        (((1, 4, 5),), ((1, 4, 5),)),
    ),
    (6, 0, 3): (
        (((0, 1, 2),), ((0, 3, 2, 1),)),
        (((0, 2, 3),), ((1, 2, 3),)),
        (((0, 3, 4),), ((1, 3, 4),)),
        (((1, 2, 5, 4),), ((0, 2, 5, 4),)),
    ),
    (6, 0, 2): (
        (((2, 1), (0, 3, 2)), ((1, 1, 2),)),
        (((1, 2), (2, 3)), ((0, 3, 2),)),
        (((0, 1, 4, 3),), ((1, 3, 4),)),
        (((1, 0, 4, 5),), ((0, 0, 4, 5),)),
    ),
    (6, 1, 3): (
        (((0, 1), (1, 3, 2)), ((2, 1), (1, 3, 2))),
        (((0, 2), (2, 3)), ((1, 2), (2, 3))),
        (((0, 3, 0, 4),), ((1, 5, 4), (0, 3))),
        (((1, 1, 5, 4),), ((1, 4), (0, 1, 5))),
    ),
    (6, 1, 2): (
        (((2, 1),), ((2, 1),)),
        (((2, 2),), ((2, 2),)),
        (((2, 3),), ((2, 3),)),
        (((2, 4),), ((0, 0, 4),)),
    ),
    (7, 0, 3): (
        (((1, 1), (2, 7)), ((2, 1), (0, 7))),
        (((0, 0), (2, 2)), ((0, 0), (1, 2))),
        (((0, 1), (1, 3)), ((0, 1), (1, 3))),
        (((2, 4), (0, 2)), ((1, 4), (2, 2))),
    ),
    (7, 0, 2): (
        (((2, 1),), ((2, 1),)),
        (((2, 2),), ((2, 2),)),
        (((2, 3),), ((2, 3),)),
        (((1, 1, 4),), ((0, 1, 4),)),
    ),
    (7, 1, 3): (
        (((2, 1), (0, 2, 7)), ((0, 1), (1, 2, 7))),
        (((0, 0), (1, 2)), ((0, 0), (2, 2))),
        (((1, 1), (2, 3)), ((1, 1), (0, 3))),
        (((1, 4), (2, 2)), ((1, 4), (0, 2))),
    ),
    (7, 1, 2): (
        (((2, 7),), ((2, 7),)),
        (((2, 0),), ((2, 0),)),
        (((2, 1),), ((2, 1),)),
        (((2, 2),), ((2, 2),)),
    ),
}


def place(x, y, core, z, half):
    return (x % XS * 8 + y % YS * 2 + core) * 16 + z % ZS * 2 + half


def everywhere():
    for x in range(XS):
        for y in range(YS):
            for core in range(2):
                for z in range(ZS):
                    for half in range(2):
                        yield x, y, core, z, half


def weight_plan():
    moves = {}
    found = {}
    for (z, half, kept), by_y in ROUTES.items():
        core = half if kept == 3 else 1 - half
        for x in range(XS):
            for y in range(YS):
                for part in range(PARTS):
                    for chain, *chips in by_y[y][part]:
                        at = place(x, y, core, z, half)
                        for step, chip in enumerate(chips):
                            to = place(x + chip // 4, chip % 4, core, z, half)
                            moves.setdefault((step, chain, part), []).append((at, to))
                            found[to, part, (x * 4 + y)] = (step, chain)
                            at = to
    order = sorted(moves)
    names = sorted({(step, chain) for step, chain, _ in order})
    table = np.zeros((256, PARTS, 3), np.int32)
    for x, y, core, z, half in everywhere():
        me = place(x, y, core, z, half)
        chip = 4 * x + y
        first = 2 if (half, core) == (1, 0) else 0
        second = 0 if (half, core) == (0, 1) else 2
        ends = (first, second) if core == 0 else (second, first)
        for part in range(PARTS):
            for slot, offset in enumerate((1,) + ends):
                source = (chip + z + offset) % 8
                if source != chip:
                    table[me, part, slot] = 1 + names.index(found[me, part, source])
    return {key: moves[key] for key in order}, names, table


def token_plan():
    shift = ([], [])
    flip = []
    near = ([], [])
    for x, y, core, z, half in everywhere():
        me = place(x, y, core, z, half)
        chip = 4 * x + y
        shift[core].append((me, place(x, y, half, z - chip - 1, half)))
        if core == half:
            flip.append((me, place(x, y, core, z, 1 - half)))
        first = 1 if (half, core) == (1, 0) else -1
        second = -1 if (half, core) == (0, 1) else 1
        near[0].append((place(x, y, core, z + first, half), me))
        near[1].append((place(x, y, core, z + second, half), me))
    return shift, flip, near


def product_kernel(slots, names, index, *refs):
    buffers = refs[: 1 + len(names) * PARTS]
    mid, end, out, held, sems = refs[1 + len(names) * PARTS :]
    rows = held.shape[2]

    def fetch(side, part, source):
        return pltpu.make_async_copy(source, held.at[side, part], sems.at[side, part])

    for part in range(PARTS):
        for side, slot in enumerate(slots):
            which = index[part * 3 + slot]

            @pl.when(which == 0)
            def _():
                fetch(side, part, buffers[0].at[pl.ds(part * rows, rows)]).start()

            for number in range(len(names)):

                @pl.when(which == 1 + number)
                def _():
                    fetch(side, part, buffers[1 + number * PARTS + part]).start()

    for part in range(PARTS):
        for side in range(2):
            fetch(side, part, buffers[0].at[pl.ds(part * rows, rows)]).wait()
    width = out.shape[1]
    for low in range(0, width, 256):
        high = min(low + 256, width)
        total = None
        for side, tokens in enumerate((mid, end)):
            for part in range(PARTS):
                term = jnp.dot(
                    tokens[:, part * rows : (part + 1) * rows],
                    held[side, part, :, low:high],
                    preferred_element_type=jnp.float32,
                )
                total = term if total is None else total + term
        out[:, low:high] = total


def product(slots, names, index, buffers, mid, end):
    count, (depth, width) = mid.shape[0], buffers[0].shape
    anywhere = pl.BlockSpec(memory_space=pl.ANY)
    whole = pl.BlockSpec(memory_space=pltpu.VMEM)
    return pl.pallas_call(
        functools.partial(product_kernel, slots, names),
        out_shape=jax.ShapeDtypeStruct((count, width), jnp.float32),
        in_specs=[pl.BlockSpec(memory_space=pltpu.SMEM)] + [anywhere] * len(buffers) + [whole] * 2,
        out_specs=whole,
        scratch_shapes=[
            pltpu.VMEM((2, PARTS, depth // PARTS, width), jnp.bfloat16),
            pltpu.SemaphoreType.DMA((2, PARTS)),
        ],
        compiler_params=pltpu.CompilerParams(vmem_limit_bytes=40 * 2**20),
        cost_estimate=pl.CostEstimate(
            flops=4 * count * depth * width, bytes_accessed=4 * depth * width + 4 * count * width, transcendentals=0
        ),
    )(index, *buffers, mid, end)


def on_device(tokens, gate_weight):
    me = lax.axis_index("row") * 16 + lax.axis_index("col")
    core = lax.axis_index("row") % 2
    half = lax.axis_index("col") % 2
    moves, names, table = weight_plan()
    index = lax.dynamic_index_in_dim(jnp.asarray(table.reshape(256, -1)), me, 0, keepdims=False)
    rows = gate_weight.shape[0] // PARTS
    parts = [gate_weight[part * rows : (part + 1) * rows] for part in range(PARTS)]

    shift, flip, near = token_plan()
    base = [lax.ppermute(tokens, BOTH, pairs) for pairs in shift]
    base = [jnp.where(core == half, own, lax.ppermute(own, BOTH, flip)) for own in base]
    ends = [lax.ppermute(own, BOTH, pairs) for own, pairs in zip(base, near)]

    got = {}
    for (step, chain, part), pairs in moves.items():
        source = parts[part] if step == 0 else got[step - 1, chain, part]
        got[step, chain, part] = lax.ppermute(source, BOTH, pairs)
    buffers = [gate_weight] + [got[name + (part,)] for name in names for part in range(PARTS)]

    keep_mid, send_mid = jnp.where(core == 0, base[0], base[1]), jnp.where(core == 0, base[1], base[0])
    keep_end, send_end = jnp.where(core == 0, ends[0], ends[1]), jnp.where(core == 0, ends[1], ends[0])
    send = product((0, 2), names, index, buffers, send_mid, send_end)
    swap = [(place(x, y, c, z, h), place(x, y, 1 - c, z, h)) for x, y, c, z, h in everywhere()]
    arrived = lax.ppermute(send, BOTH, swap)
    keep = product((0, 1), names, index, buffers, keep_mid, keep_end)
    return keep + arrived


def solution(mesh):
    placed = (P("row", "col"), P("row", "col"))
    return jax.shard_map(
        on_device, mesh=mesh, in_specs=placed, out_specs=P("row", "col"), check_vma=False
    )
```

time: 512 us -> 269 us (0.53)
  the two profiles are of different devices: /device:TPU:2 before, /device:TPU:193 now
where the time goes in v1:
time: 269 us
  waiting for transfers between devices  145 us (54%)
  starting transfers between devices  94.6 us (35%)
  Pallas kernels  16.3 us (6%)
  other arithmetic  7.57 us (3%)
  local copies, waits for them, and re-layouts  4.8 us (2%)
    ppermute x14, waiting for transfers between devices, on_device(): got[step, chain, part] = lax.ppermute(source, BOTH, pairs)  105 us
    ppermute x14, starting transfers between devices, on_device(): got[step, chain, part] = lax.ppermute(source, BOTH, pairs)  85.7 us
    ppermute x2, waiting for transfers between devices, on_device(): ends = [lax.ppermute(own, BOTH, pairs) for own, pairs in zip(base, near)]  25.5 us
    pallas_call x2, Pallas kernels, product(): pl.pallas_call(functools.partial(product_kernel, slots, names), out_shape...  16.3 us
    ppermute x2, waiting for transfers between devices, on_device(): base = [lax.ppermute(tokens, BOTH, pairs) for pairs in shift]  15 us
  transfers between devices with their start and end apart: 21, of which 9 were waited for; matrix products, arithmetic and copies ran while one was open for 3% of the time, Pallas kernels for 3%

profile of v1, /device:TPU:193, one launch (start us, length us, event | category | flops | bytes accessed | tf_op | source)
XLA Modules:
  0.0 268.8 jit_solution(10827597831748698364)
XLA Ops:
  0.0 3.2 %collective-permute-start.16 = (bf16[384,1024]{1,0:T(8,128)(2,1)}, bf16[384,1024]{1,0:T(8,128)(2,1)S(1)}, u32[]{:S(2)}, u32[]{:S(2)}) collective-permute-start(bf16[384,1024]{1,0:T(8,128)(2,1)} %param.3), channel_id=1, source_target_pairs={{16,14},{17,31},{18,0},{19,17},{20,2},{21,19},{22,4},{23,21},{24,6... | collective-permute-start | bytes 2359304 | tf_op jit(solution)/shard_map/ppermute | solution.py:343
  4.0 14.9 %collective-permute-done.16 = bf16[384,1024]{1,0:T(8,128)(2,1)S(1)} collective-permute-done((bf16[384,1024]{1,0:T(8,128)(2,1)}, bf16[384,1024]{1,0:T(8,128)(2,1)S(1)}, u32[]{:S(2)}, u32[]{:S(2)}) %collective-permute-start.16) | collective-permute-done | bytes 786464 | tf_op jit(solution)/shard_map/ppermute | solution.py:343
  18.9 1.3 collective-permute-start.17
  20.2 1.3 collective-permute-start.15
  21.5 4.0 %fusion = (bf16[512,1664]{1,0:T(8,128)(2,1)}, bf16[512,1664]{1,0:T(8,128)(2,1)}) fusion(bf16[1024,1664]{1,0:T(8,128)(2,1)} %refs_0_.3), kind=kLoop, calls=%fused_computation.7 | loop fusion | bytes 6815744 | tf_op jit(solution)/shard_map/slice | solution.py:340
  25.5 20.9 %collective-permute-start.3 = (bf16[512,1664]{1,0:T(8,128)(2,1)}, bf16[512,1664]{1,0:T(8,128)(2,1)S(1)}, u32[]{:S(2)}, u32[]{:S(2)}) collective-permute-start(bf16[512,1664]{1,0:T(8,128)(2,1)} %get-tuple-element.8), channel_id=1, source_target_pairs={{0,32},{96,0},{128,160},{224,128},{49,209},{81,49},{113,17},{177,8... | collective-permute-start | bytes 5111816 | tf_op jit(solution)/shard_map/ppermute | solution.py:350
  46.5 1.3 collective-permute-start.1
  47.8 1.3 collective-permute-start.2
  49.1 11.0 %collective-permute-start = (bf16[512,1664]{1,0:T(8,128)(2,1)}, bf16[512,1664]{1,0:T(8,128)(2,1)}, u32[]{:S(2)}, u32[]{:S(2)}) collective-permute-start(bf16[512,1664]{1,0:T(8,128)(2,1)} %get-tuple-element.9), channel_id=1, source_target_pairs={{0,96},{64,32},{96,0},{128,224},{192,160},{224,128},{81,17},{113,8... | collective-permute-start | bytes 5111816 | tf_op jit(solution)/shard_map/ppermute | solution.py:350
  60.0 1.9 collective-permute-start.5
  61.9 3.5 %collective-permute-done.3.refs_4_ = bf16[512,1664]{1,0:T(8,128)(2,1)S(1)} collective-permute-done((bf16[512,1664]{1,0:T(8,128)(2,1)}, bf16[512,1664]{1,0:T(8,128)(2,1)S(1)}, u32[]{:S(2)}, u32[]{:S(2)}) %collective-permute-start.3) | collective-permute-done | bytes 1703968 | tf_op jit(solution)/shard_map/ppermute | solution.py:350
  66.7 3.7 %collective-permute-done.1.refs_2_ = bf16[512,1664]{1,0:T(8,128)(2,1)S(1)} collective-permute-done((bf16[512,1664]{1,0:T(8,128)(2,1)}, bf16[512,1664]{1,0:T(8,128)(2,1)S(1)}, u32[]{:S(2)}, u32[]{:S(2)}) %collective-permute-start.1) | collective-permute-done | bytes 1703968 | tf_op jit(solution)/shard_map/ppermute | solution.py:350
  70.4 18.2 %collective-permute-start.7 = (bf16[512,1664]{1,0:T(8,128)(2,1)S(1)}, bf16[512,1664]{1,0:T(8,128)(2,1)}, u32[]{:S(2)}, u32[]{:S(2)}) collective-permute-start(bf16[512,1664]{1,0:T(8,128)(2,1)S(1)} %collective-permute-done.1.refs_2_), channel_id=1, source_target_pairs={{0,96},{128,224},{49,209},{177,81},{1,225},{65,33},{129,97},{193,1... | collective-permute-start | bytes 5111816 | tf_op jit(solution)/shard_map/ppermute | solution.py:350
  88.6 54.9 %collective-permute-done.2.refs_3_ = bf16[512,1664]{1,0:T(8,128)(2,1)} collective-permute-done((bf16[512,1664]{1,0:T(8,128)(2,1)}, bf16[512,1664]{1,0:T(8,128)(2,1)}, u32[]{:S(2)}, u32[]{:S(2)}) %collective-permute-start.2) | collective-permute-done | bytes 1703968 | tf_op jit(solution)/shard_map/ppermute | solution.py:350
  143.6 14.1 %collective-permute-start.8 = (bf16[512,1664]{1,0:T(8,128)(2,1)}, bf16[512,1664]{1,0:T(8,128)(2,1)}, u32[]{:S(2)}, u32[]{:S(2)}) collective-permute-start(bf16[512,1664]{1,0:T(8,128)(2,1)} %collective-permute-done.2.refs_3_), channel_id=1, source_target_pairs={{192,224},{64,96},{241,209},{17,113},{113,81},{145,241},{65,193},{... | collective-permute-start | bytes 5111816 | tf_op jit(solution)/shard_map/ppermute | solution.py:350
  157.7 1.3 collective-permute-start.6
  159.0 2.4 broadcast_select_fusion.3
  161.6 15.5 %collective-permute-done.19 = bf16[384,1024]{1,0:T(8,128)(2,1)S(1)} collective-permute-done((bf16[384,1024]{1,0:T(8,128)(2,1)S(1)}, bf16[384,1024]{1,0:T(8,128)(2,1)S(1)}, u32[]{:S(2)}, u32[]{:S(2)}) %collective-permute-start.19) | collective-permute-done | bytes 786464 | tf_op jit(solution)/shard_map/ppermute | solution.py:345
  177.0 2.2 collective-permute-start.18
  179.2 10.0 %collective-permute-done.18 = bf16[384,1024]{1,0:T(8,128)(2,1)S(1)} collective-permute-done((bf16[384,1024]{1,0:T(8,128)(2,1)S(1)}, bf16[384,1024]{1,0:T(8,128)(2,1)S(1)}, u32[]{:S(2)}, u32[]{:S(2)}) %collective-permute-start.18) | collective-permute-done | bytes 786464 | tf_op jit(solution)/shard_map/ppermute | solution.py:345
  189.2 5.1 %collective-permute-start.4 = (bf16[512,1664]{1,0:T(8,128)(2,1)}, bf16[512,1664]{1,0:T(8,128)(2,1)}, u32[]{:S(2)}, u32[]{:S(2)}) collective-permute-start(bf16[512,1664]{1,0:T(8,128)(2,1)} %get-tuple-element.9), channel_id=1, source_target_pairs={{32,0},{96,64},{160,128},{224,192},{16,240},{48,16},{80,48},{112,8... | collective-permute-start | bytes 5111816 | tf_op jit(solution)/shard_map/ppermute | solution.py:350
  194.4 1.9 collective-permute-start.13
  196.3 2.5 collective-permute-start.11
  198.7 2.5 collective-permute-start.12
  201.2 2.5 collective-permute-start.10
  204.5 1.5 broadcast_select_fusion.2
  206.0 6.2 %collective-permute-done.4.refs_5_ = bf16[512,1664]{1,0:T(8,128)(2,1)} collective-permute-done((bf16[512,1664]{1,0:T(8,128)(2,1)}, bf16[512,1664]{1,0:T(8,128)(2,1)}, u32[]{:S(2)}, u32[]{:S(2)}) %collective-permute-start.4) | collective-permute-done | bytes 1703968 | tf_op jit(solution)/shard_map/ppermute | solution.py:350
  212.2 18.3 %collective-permute-done.11.refs_12_ = bf16[512,1664]{1,0:T(8,128)(2,1)} collective-permute-done((bf16[512,1664]{1,0:T(8,128)(2,1)}, bf16[512,1664]{1,0:T(8,128)(2,1)}, u32[]{:S(2)}, u32[]{:S(2)}) %collective-permute-start.11) | collective-permute-done | bytes 1703968 | tf_op jit(solution)/shard_map/ppermute | solution.py:350
  230.5 18.3 %collective-permute-done.12.refs_13_ = bf16[512,1664]{1,0:T(8,128)(2,1)} collective-permute-done((bf16[512,1664]{1,0:T(8,128)(2,1)}, bf16[512,1664]{1,0:T(8,128)(2,1)}, u32[]{:S(2)}, u32[]{:S(2)}) %collective-permute-start.12) | collective-permute-done | bytes 1703968 | tf_op jit(solution)/shard_map/ppermute | solution.py:350
  248.7 8.2 %shard_map.38 = f32[384,1664]{1,0:T(8,128)} custom-call(s32[6]{0:T(128)S(1)} %dynamic-slice_bitcast_fusion.index, bf16[1024,1664]{1,0:T(8,128)(2,1)} %refs_0_.3, bf16[512,1664]{1,0:T(8,128)(2,1)} %collective-permute-done.refs_1_, bf16[512,1664]{1,0:T(8,128)(2,1)S(1)} %collective-permute-done.1.refs_2_, bf16[512,1664]{1,0:T(8,128)(2,1)} %collective-permute-done.2.refs_3_, ...), custom_call_target="tpu_custom_call" | custom-call | flops 2617245696 | bytes 9371648 | tf_op jit(solution)/shard_map/pallas_call | solution.py:317
  257.1 8.1 %shard_map.37 = f32[384,1664]{1,0:T(8,128)} custom-call(s32[6]{0:T(128)S(1)} %dynamic-slice_bitcast_fusion.index, bf16[1024,1664]{1,0:T(8,128)(2,1)} %refs_0_.3, bf16[512,1664]{1,0:T(8,128)(2,1)} %collective-permute-done.refs_1_, bf16[512,1664]{1,0:T(8,128)(2,1)S(1)} %collective-permute-done.1.refs_2_, bf16[512,1664]{1,0:T(8,128)(2,1)} %collective-permute-done.2.refs_3_, ...), custom_call_target="tpu_custom_call" | custom-call | flops 2617245696 | bytes 9371648 | tf_op jit(solution)/shard_map/pallas_call | solution.py:317
  265.3 3.6 %add.21 = f32[384,1664]{1,0:T(8,128)} add(f32[384,1664]{1,0:T(8,128)} %shard_map.37, f32[384,1664]{1,0:T(8,128)S(1)} %collective-permute-done.20) | non-fusion elementwise | flops 638976 | bytes 7667712 | tf_op jit(solution)/shard_map/add | solution.py:359
  (40 shorter events, 3.1 us)
Async XLA Ops:
  0.0 18.9 %collective-permute-start.16 = (bf16[384,1024]{1,0:T(8,128)(2,1)}, bf16[384,1024]{1,0:T(8,128)(2,1)S(1)}, u32[]{:S(2)}, u32[]{:S(2)}) collective-permute-start(bf16[384,1024]{1,0:T(8,128)(2,1)} %param.3), channel_id=1, source_target_pairs={{16,14},{17,31},{18,0},{19,17},{20,2},{21,19},{22,4},{23,21},{24,6... | collective-permute-start | bytes 2359304 | tf_op jit(solution)/shard_map/ppermute | solution.py:343
  3.2 17.0 %collective-permute-start.14 = (bf16[384,1024]{1,0:T(8,128)(2,1)}, bf16[384,1024]{1,0:T(8,128)(2,1)S(1)}, u32[]{:S(2)}, u32[]{:S(2)}) collective-permute-start(bf16[384,1024]{1,0:T(8,128)(2,1)} %param.3), channel_id=1, source_target_pairs={{0,14},{1,31},{2,0},{3,17},{4,2},{5,19},{6,4},{7,21},{8,6},{9,23},... | collective-permute-start | bytes 2359304 | tf_op jit(solution)/shard_map/ppermute | solution.py:343
  18.9 6.6 %copy-start.5 = (bf16[384,1024]{1,0:T(8,128)(2,1)}, bf16[384,1024]{1,0:T(8,128)(2,1)S(1)}, u32[]{:S(2)}) copy-start(bf16[384,1024]{1,0:T(8,128)(2,1)S(1)} %collective-permute-done.16) | copy-start | bytes 2359300
  18.9 30.2 %collective-permute-start.17 = (bf16[384,1024]{1,0:T(8,128)(2,1)S(1)}, bf16[384,1024]{1,0:T(8,128)(2,1)S(1)}, u32[]{:S(2)}, u32[]{:S(2)}) collective-permute-start(bf16[384,1024]{1,0:T(8,128)(2,1)S(1)} %collective-permute-done.16), channel_id=1, source_target_pairs={{0,1},{2,3},{4,5},{6,7},{8,9},{10,11},{12,13},{14,15},{17,16},{19,... | collective-permute-start | bytes 2359304 | tf_op jit(solution)/shard_map/ppermute | solution.py:344
  20.2 5.3 %copy-start.6 = (bf16[384,1024]{1,0:T(8,128)(2,1)}, bf16[384,1024]{1,0:T(8,128)(2,1)S(1)}, u32[]{:S(2)}) copy-start(bf16[384,1024]{1,0:T(8,128)(2,1)S(1)} %collective-permute-done.14) | copy-start | bytes 2359300
  20.2 39.8 %collective-permute-start.15 = (bf16[384,1024]{1,0:T(8,128)(2,1)S(1)}, bf16[384,1024]{1,0:T(8,128)(2,1)S(1)}, u32[]{:S(2)}, u32[]{:S(2)}) collective-permute-start(bf16[384,1024]{1,0:T(8,128)(2,1)S(1)} %collective-permute-done.14), channel_id=1, source_target_pairs={{0,1},{2,3},{4,5},{6,7},{8,9},{10,11},{12,13},{14,15},{17,16},{19,... | collective-permute-start | bytes 2359304 | tf_op jit(solution)/shard_map/ppermute | solution.py:344
  25.5 39.9 %collective-permute-start.3 = (bf16[512,1664]{1,0:T(8,128)(2,1)}, bf16[512,1664]{1,0:T(8,128)(2,1)S(1)}, u32[]{:S(2)}, u32[]{:S(2)}) collective-permute-start(bf16[512,1664]{1,0:T(8,128)(2,1)} %get-tuple-element.8), channel_id=1, source_target_pairs={{0,32},{96,0},{128,160},{224,128},{49,209},{81,49},{113,17},{177,8... | collective-permute-start | bytes 5111816 | tf_op jit(solution)/shard_map/ppermute | solution.py:350
  46.5 24.0 %collective-permute-start.1 = (bf16[512,1664]{1,0:T(8,128)(2,1)}, bf16[512,1664]{1,0:T(8,128)(2,1)S(1)}, u32[]{:S(2)}, u32[]{:S(2)}) collective-permute-start(bf16[512,1664]{1,0:T(8,128)(2,1)} %get-tuple-element.8), channel_id=1, source_target_pairs={{32,0},{64,32},{160,128},{192,160},{17,49},{145,177},{33,1},{97,65... | collective-permute-start | bytes 5111816 | tf_op jit(solution)/shard_map/ppermute | solution.py:350
  47.8 95.8 %collective-permute-start.2 = (bf16[512,1664]{1,0:T(8,128)(2,1)}, bf16[512,1664]{1,0:T(8,128)(2,1)}, u32[]{:S(2)}, u32[]{:S(2)}) collective-permute-start(bf16[512,1664]{1,0:T(8,128)(2,1)} %get-tuple-element.9), channel_id=1, source_target_pairs={{32,192},{64,0},{160,64},{192,128},{17,241},{49,17},{81,49},{145,1... | collective-permute-start | bytes 5111816 | tf_op jit(solution)/shard_map/ppermute | solution.py:350
  49.1 11.0 %copy-start.7 = (bf16[384,1024]{1,0:T(8,128)(2,1)}, bf16[384,1024]{1,0:T(8,128)(2,1)S(1)}, u32[]{:S(2)}) copy-start(bf16[384,1024]{1,0:T(8,128)(2,1)S(1)} %collective-permute-done.17) | copy-start | bytes 2359300
  49.1 108.6 %collective-permute-start = (bf16[512,1664]{1,0:T(8,128)(2,1)}, bf16[512,1664]{1,0:T(8,128)(2,1)}, u32[]{:S(2)}, u32[]{:S(2)}) collective-permute-start(bf16[512,1664]{1,0:T(8,128)(2,1)} %get-tuple-element.9), channel_id=1, source_target_pairs={{0,96},{64,32},{96,0},{128,224},{192,160},{224,128},{81,17},{113,8... | collective-permute-start | bytes 5111816 | tf_op jit(solution)/shard_map/ppermute | solution.py:350
  60.0 1.9 copy-start.8
  60.0 101.4 %collective-permute-start.5 = (bf16[512,1664]{1,0:T(8,128)(2,1)}, bf16[512,1664]{1,0:T(8,128)(2,1)}, u32[]{:S(2)}, u32[]{:S(2)}) collective-permute-start(bf16[512,1664]{1,0:T(8,128)(2,1)} %get-tuple-element.8), channel_id=1, source_target_pairs={{64,0},{192,128},{16,240},{48,16},{80,48},{112,80},{144,112},{176,... | collective-permute-start | bytes 5111816 | tf_op jit(solution)/shard_map/ppermute | solution.py:350
  65.4 128.9 %collective-permute-start.9 = (bf16[512,1664]{1,0:T(8,128)(2,1)S(1)}, bf16[512,1664]{1,0:T(8,128)(2,1)}, u32[]{:S(2)}, u32[]{:S(2)}) collective-permute-start(bf16[512,1664]{1,0:T(8,128)(2,1)S(1)} %collective-permute-done.3.refs_4_), channel_id=1, source_target_pairs={{32,192},{0,32},{160,64},{128,160},{209,241},{49,17},{17,49},{81,1... | collective-permute-start | bytes 5111816 | tf_op jit(solution)/shard_map/ppermute | solution.py:350
  70.4 125.8 %collective-permute-start.7 = (bf16[512,1664]{1,0:T(8,128)(2,1)S(1)}, bf16[512,1664]{1,0:T(8,128)(2,1)}, u32[]{:S(2)}, u32[]{:S(2)}) collective-permute-start(bf16[512,1664]{1,0:T(8,128)(2,1)S(1)} %collective-permute-done.1.refs_2_), channel_id=1, source_target_pairs={{0,96},{128,224},{49,209},{177,81},{1,225},{65,33},{129,97},{193,1... | collective-permute-start | bytes 5111816 | tf_op jit(solution)/shard_map/ppermute | solution.py:350
  143.6 55.2 %collective-permute-start.8 = (bf16[512,1664]{1,0:T(8,128)(2,1)}, bf16[512,1664]{1,0:T(8,128)(2,1)}, u32[]{:S(2)}, u32[]{:S(2)}) collective-permute-start(bf16[512,1664]{1,0:T(8,128)(2,1)} %collective-permute-done.2.refs_3_), channel_id=1, source_target_pairs={{192,224},{64,96},{241,209},{17,113},{113,81},{145,241},{65,193},{... | collective-permute-start | bytes 5111816 | tf_op jit(solution)/shard_map/ppermute | solution.py:350
  157.7 43.5 %collective-permute-start.6 = (bf16[512,1664]{1,0:T(8,128)(2,1)}, bf16[512,1664]{1,0:T(8,128)(2,1)}, u32[]{:S(2)}, u32[]{:S(2)}) collective-permute-start(bf16[512,1664]{1,0:T(8,128)(2,1)} %collective-permute-done.refs_1_), channel_id=1, source_target_pairs={{96,224},{0,32},{224,96},{128,160},{81,49},{209,177},{193,225},{65... | collective-permute-start | bytes 5111816 | tf_op jit(solution)/shard_map/ppermute | solution.py:350
  161.5 34.8 %copy-start.1 = (bf16[384,1024]{1,0:T(8,128)(2,1)}, bf16[384,1024]{1,0:T(8,128)(2,1)S(1)}, u32[]{:S(2)}) copy-start(bf16[384,1024]{1,0:T(8,128)(2,1)S(1)} %get-tuple-element.6) | copy-start | bytes 2359300
  161.5 37.3 %copy-start.3 = (bf16[384,1024]{1,0:T(8,128)(2,1)}, bf16[384,1024]{1,0:T(8,128)(2,1)S(1)}, u32[]{:S(2)}) copy-start(bf16[384,1024]{1,0:T(8,128)(2,1)S(1)} %get-tuple-element.7) | copy-start | bytes 2359300
  161.5 15.6 %collective-permute-start.19 = (bf16[384,1024]{1,0:T(8,128)(2,1)S(1)}, bf16[384,1024]{1,0:T(8,128)(2,1)S(1)}, u32[]{:S(2)}, u32[]{:S(2)}) collective-permute-start(bf16[384,1024]{1,0:T(8,128)(2,1)S(1)} %get-tuple-element.6), channel_id=1, source_target_pairs={{2,0},{3,1},{4,2},{5,3},{6,4},{7,5},{8,6},{9,7},{10,8},{11,9},{12,... | collective-permute-start | bytes 2359304 | tf_op jit(solution)/shard_map/ppermute | solution.py:345
  177.0 21.7 %copy-start.9 = (bf16[384,1024]{1,0:T(8,128)(2,1)}, bf16[384,1024]{1,0:T(8,128)(2,1)S(1)}, u32[]{:S(2)}) copy-start(bf16[384,1024]{1,0:T(8,128)(2,1)S(1)} %collective-permute-done.19) | copy-start | bytes 2359300
  177.0 12.2 %collective-permute-start.18 = (bf16[384,1024]{1,0:T(8,128)(2,1)S(1)}, bf16[384,1024]{1,0:T(8,128)(2,1)S(1)}, u32[]{:S(2)}, u32[]{:S(2)}) collective-permute-start(bf16[384,1024]{1,0:T(8,128)(2,1)S(1)} %get-tuple-element.7), channel_id=1, source_target_pairs={{14,0},{3,1},{0,2},{5,3},{2,4},{7,5},{4,6},{9,7},{6,8},{11,9},{8,1... | collective-permute-start | bytes 2359304 | tf_op jit(solution)/shard_map/ppermute | solution.py:345
  189.2 12.0 %copy-start.10 = (bf16[384,1024]{1,0:T(8,128)(2,1)}, bf16[384,1024]{1,0:T(8,128)(2,1)S(1)}, u32[]{:S(2)}) copy-start(bf16[384,1024]{1,0:T(8,128)(2,1)S(1)} %collective-permute-done.18) | copy-start | bytes 2359300
  189.2 22.9 %collective-permute-start.4 = (bf16[512,1664]{1,0:T(8,128)(2,1)}, bf16[512,1664]{1,0:T(8,128)(2,1)}, u32[]{:S(2)}, u32[]{:S(2)}) collective-permute-start(bf16[512,1664]{1,0:T(8,128)(2,1)} %get-tuple-element.9), channel_id=1, source_target_pairs={{32,0},{96,64},{160,128},{224,192},{16,240},{48,16},{80,48},{112,8... | collective-permute-start | bytes 5111816 | tf_op jit(solution)/shard_map/ppermute | solution.py:350
  194.4 17.8 %collective-permute-start.13 = (bf16[512,1664]{1,0:T(8,128)(2,1)}, bf16[512,1664]{1,0:T(8,128)(2,1)}, u32[]{:S(2)}, u32[]{:S(2)}) collective-permute-start(bf16[512,1664]{1,0:T(8,128)(2,1)} %collective-permute-done.9.refs_10_), channel_id=1, source_target_pairs={{192,224},{32,64},{64,96},{160,192},{241,17},{113,145},{225,193},{... | collective-permute-start | bytes 5111816 | tf_op jit(solution)/shard_map/ppermute | solution.py:350
  196.3 34.2 %collective-permute-start.11 = (bf16[512,1664]{1,0:T(8,128)(2,1)}, bf16[512,1664]{1,0:T(8,128)(2,1)}, u32[]{:S(2)}, u32[]{:S(2)}) collective-permute-start(bf16[512,1664]{1,0:T(8,128)(2,1)} %collective-permute-done.7.refs_8_), channel_id=1, source_target_pairs={{96,224},{224,96},{194,226},{2,34},{34,66},{66,98},{130,162},{162,... | collective-permute-start | bytes 5111816 | tf_op jit(solution)/shard_map/ppermute | solution.py:350
  198.7 50.0 %collective-permute-start.12 = (bf16[512,1664]{1,0:T(8,128)(2,1)}, bf16[512,1664]{1,0:T(8,128)(2,1)}, u32[]{:S(2)}, u32[]{:S(2)}) collective-permute-start(bf16[512,1664]{1,0:T(8,128)(2,1)} %collective-permute-done.8.refs_9_), channel_id=1, source_target_pairs={{113,241},{241,113},{193,225},{33,65},{65,97},{161,193},{243,211},... | collective-permute-start | bytes 5111816 | tf_op jit(solution)/shard_map/ppermute | solution.py:350
  201.2 47.5 %collective-permute-start.10 = (bf16[512,1664]{1,0:T(8,128)(2,1)}, bf16[512,1664]{1,0:T(8,128)(2,1)}, u32[]{:S(2)}, u32[]{:S(2)}) collective-permute-start(bf16[512,1664]{1,0:T(8,128)(2,1)} %collective-permute-done.6.refs_7_), channel_id=1, source_target_pairs={{224,192},{96,64},{162,194},{34,66},{211,179},{19,243},{83,51},{14... | collective-permute-start | bytes 5111816 | tf_op jit(solution)/shard_map/ppermute | solution.py:350
  203.7 45.0 %copy-start = (bf16[384,1024]{1,0:T(8,128)(2,1)S(1)}, bf16[384,1024]{1,0:T(8,128)(2,1)}, u32[]{:S(2)}) copy-start(bf16[384,1024]{1,0:T(8,128)(2,1)} %get-tuple-element.5.refs_15_) | copy-start | bytes 2359300
  248.7 8.3 %copy-start.2 = (bf16[384,1024]{1,0:T(8,128)(2,1)S(1)}, bf16[384,1024]{1,0:T(8,128)(2,1)}, u32[]{:S(2)}) copy-start(bf16[384,1024]{1,0:T(8,128)(2,1)} %copy-done.1) | copy-start | bytes 2359300
  248.7 8.3 %copy-start.4 = (bf16[384,1024]{1,0:T(8,128)(2,1)S(1)}, bf16[384,1024]{1,0:T(8,128)(2,1)}, u32[]{:S(2)}) copy-start(bf16[384,1024]{1,0:T(8,128)(2,1)} %copy-done.3) | copy-start | bytes 2359300
  256.9 8.4 %collective-permute-start.20 = (f32[384,1664]{1,0:T(8,128)}, f32[384,1664]{1,0:T(8,128)S(1)}, u32[]{:S(2)}, u32[]{:S(2)}) collective-permute-start(f32[384,1664]{1,0:T(8,128)} %shard_map.38), channel_id=1, source_target_pairs={{0,16},{1,17},{2,18},{3,19},{4,20},{5,21},{6,22},{7,23},{8,24},{9,... | collective-permute-start | bytes 7667720 | tf_op jit(solution)/shard_map/ppermute | solution.py:357

commit v2 on v0

v2 whole, which is shorter than its diff:
```python
import functools

import jax
import jax.numpy as jnp
import numpy as np
from jax import lax
from jax.experimental import pallas as pl
from jax.experimental.pallas import tpu as pltpu
from jax.sharding import PartitionSpec as P

XS, YS, ZS = 2, 4, 8
BOTH = ("row", "col")
ROUNDS = 3
PARTS = 4

FIRST = (0,)
ROUTES = {
    (0, 0, 3): (
        (((0, 1, 7, 6),), ((0, 5, 6, 7),), ((0, 1, 6, 7),), ((0, 7, 6),)),
        (((0, 2, 0, 7),), ((0, 0, 7),), ((0, 2, 7, 0),), ((0, 2, 7, 0),)),
        (((0, 3, 1, 0),), ((0, 3, 0, 1),), ((0, 3, 0, 1),), ((0, 1, 0),)),
        (((0, 0, 2, 1),), ((0, 2, 1),), ((0, 0, 1, 2),), ((0, 0, 1, 2),)),
    ),
    (0, 0, 2): (
        (((0, 7),), ((0, 3, 7),), ((0, 3, 7),), ((0, 4, 7),)),
        (((0, 0),), ((0, 0),), ((0, 0),), ((0, 5, 0),)),
        (((0, 1),), ((0, 1),), ((0, 1),), ((0, 6, 1),)),
        (((0, 2),), ((0, 2),), ((0, 2),), ((0, 7, 2),)),
    ),
    (0, 1, 3): (
        (((0, 6, 7),), ((0, 6, 7),), ((0, 3, 7, 6),), ((0, 3, 7, 6),)),
        (((0, 7, 0),), ((0, 7, 0),), ((0, 0, 4, 7),), ((0, 0, 4, 7),)),
        (((0, 0, 1),), ((0, 0, 1),), ((0, 5, 1, 0),), ((0, 5, 1, 0),)),
        (((0, 1, 2),), ((0, 1, 2),), ((0, 2, 6, 1),), ((0, 2, 6, 1),)),
    ),
    (0, 1, 2): (
        (((0, 1, 6, 7),), ((0, 1, 6, 7),), ((0, 7, 6),), ((0, 7, 6),)),
        (((0, 0, 7),), ((0, 6, 7, 0),), ((0, 6, 7, 0),), ((0, 0, 7),)),
        (((0, 3, 0, 1),), ((0, 3, 0, 1),), ((0, 1, 0),), ((0, 1, 0),)),
        (((0, 2, 1),), ((0, 0, 1, 2),), ((0, 0, 1, 2),), ((0, 2, 1),)),
    ),
    (1, 0, 3): (
        (((0, 7, 6, 5),), ((0, 5, 6, 7),), ((0, 5, 6, 7),), ((0, 7, 6, 5),)),
        (((0, 0, 7, 6),), ((0, 6, 7, 0),), ((0, 6, 7, 0),), ((0, 6, 7, 0),)),
        (((0, 1, 0, 7),), ((0, 7, 0, 1),), ((0, 7, 0, 1),), ((0, 1, 0, 7),)),
        (((0, 2, 1, 0),), ((0, 0, 1, 2),), ((0, 0, 1, 2),), ((0, 0, 1, 2),)),
    ),
    (1, 0, 2): (
        (((0, 3, 7, 6),), ((0, 2, 6, 7),), ((0, 3, 7, 6),), ((0, 3, 7, 6),)),
        (((0, 0, 2, 7),), ((0, 5, 7, 0),), ((0, 0, 4, 7),), ((0, 0, 4, 7),)),
        (((0, 1, 0),), ((0, 3, 0, 1),), ((0, 5, 1, 0),), ((0, 1, 5, 0),)),
        (((0, 2, 1),), ((0, 0, 1, 2),), ((0, 2, 6, 1),), ((0, 2, 6, 1),)),
    ),
    (1, 1, 3): (
        (((0, 5, 6, 7),), ((0, 7, 6, 5),), ((0, 5, 6, 7),), ((0, 5, 6, 7),)),
        (((0, 0, 7, 6),), ((0, 0, 7, 6),), ((0, 6, 7, 0),), ((0, 0, 7, 6),)),
        (((0, 7, 0, 1),), ((0, 1, 0, 7),), ((0, 7, 0, 1),), ((0, 7, 0, 1),)),
        (((0, 2, 1, 0),), ((0, 2, 1, 0),), ((0, 0, 1, 2),), ((0, 2, 1, 0),)),
    ),
    (1, 1, 2): (
        (((0, 3, 6, 5),), ((0, 2, 5, 6),), ((0, 4, 5, 6),), ((0, 1, 6, 5),)),
        (((0, 6, 7),), ((0, 7, 6),), ((0, 7, 6),), ((0, 6, 7),)),
        (((0, 1, 0, 7),), ((0, 0, 3, 7),), ((0, 6, 7, 0),), ((0, 7, 0),)),
        (((0, 0, 1),), ((0, 1, 0),), ((0, 1, 0),), ((0, 0, 1),)),
    ),
    (2, 0, 3): (
        (((0, 4, 5, 6),), ((0, 4, 5, 6),), ((0, 4, 5, 6),), ((0, 4, 5, 6),)),
        (((0, 7, 6, 5),), ((0, 7, 6, 5),), ((0, 7, 6, 5),), ((0, 5, 6, 7),)),
        (((0, 6, 7, 0),), ((0, 6, 7, 0),), ((0, 6, 7, 0),), ((0, 6, 7, 0),)),
        (((0, 1, 0, 7),), ((0, 1, 0, 7),), ((0, 1, 0, 7),), ((0, 7, 0, 1),)),
    ),
    (2, 0, 2): (
        (((0, 5, 7, 6),), ((0, 2, 5, 6),), ((0, 1, 6, 5),), ((0, 1, 6, 5),)),
        (((0, 2, 6, 7),), ((0, 7, 6),), ((0, 6, 7),), ((0, 4, 7, 6),)),
        (((0, 7, 0),), ((0, 0, 7),), ((0, 7, 0),), ((0, 7, 0),)),
        (((0, 0, 1),), ((0, 1, 0),), ((0, 0, 1),), ((0, 2, 1, 0),)),
    ),
    (2, 1, 3): (
        (((0, 4, 5, 6),), ((0, 4, 5, 6),), ((0, 6, 5, 4),), ((0, 4, 5, 6),)),
        (((0, 7, 6, 5),), ((0, 5, 6, 7),), ((0, 7, 6, 5),), ((0, 7, 6, 5),)),
        (((0, 6, 7, 0),), ((0, 6, 7, 0),), ((0, 0, 7, 6),), ((0, 6, 7, 0),)),
        (((0, 1, 0, 7),), ((0, 7, 0, 1),), ((0, 1, 0, 7),), ((0, 1, 0, 7),)),
    ),
    (2, 1, 2): (
        (((0, 1, 4, 5),), ((0, 4, 5),), ((0, 3, 4, 5),), ((0, 1, 5, 4),)),
        (((0, 2, 5, 6),), ((0, 5, 6),), ((0, 6, 5),), ((0, 2, 6, 5),)),
        (((0, 7, 6),), ((0, 6, 7),), ((0, 1, 7, 6),), ((0, 4, 7, 6),)),
        (((0, 0, 7),), ((0, 7, 0),), ((0, 0, 2, 7),), ((0, 7, 0),)),
    ),
    (3, 0, 3): (
        (((0, 3, 4, 5),), ((0, 4, 5, 3),), ((0, 3, 4, 5),), ((0, 3, 4, 5),)),
        (((0, 6, 5, 4),), ((0, 5, 4, 6),), ((0, 4, 5, 6),), ((0, 6, 5, 4),)),
        (((0, 5, 6, 7),), ((0, 6, 7, 5),), ((0, 5, 6, 7),), ((0, 5, 6, 7),)),
        (((0, 0, 7, 6),), ((0, 7, 6, 0),), ((0, 6, 7, 0),), ((0, 0, 7, 6),)),
    ),
    (3, 0, 2): (
        (((0, 4, 5),), ((0, 5, 4),), ((0, 1, 5, 4),), ((0, 4, 5),)),
        (((0, 5, 6),), ((0, 6, 5),), ((0, 7, 6, 5),), ((0, 2, 6, 5),)),
        (((0, 6, 7),), ((0, 7, 6),), ((0, 6, 7),), ((0, 3, 7, 6),)),
        (((0, 7, 0),), ((0, 0, 7),), ((0, 0, 4, 7),), ((0, 1, 0, 7),)),
    ),
    (3, 1, 3): (
        (((0, 3, 4, 5),), ((0, 3, 4, 5),), ((0, 5, 4, 3),), ((0, 4, 5, 3),)),
        (((0, 6, 5, 4),), ((0, 6, 5, 4),), ((0, 6, 5, 4),), ((0, 5, 4, 6),)),
        (((0, 5, 6, 7),), ((0, 5, 6, 7),), ((0, 7, 6, 5),), ((0, 6, 7, 5),)),
        (((0, 0, 7, 6),), ((0, 0, 7, 6),), ((0, 0, 7, 6),), ((0, 7, 6, 0),)),
    ),
    (3, 1, 2): (
        (((0, 2, 3, 4),), ((0, 4, 3),), ((0, 3, 4),), ((0, 3, 7, 4),)),
        (((0, 0, 4, 5),), ((0, 5, 4),), ((0, 4, 5),), ((0, 5, 4),)),
        (((0, 1, 5, 6),), ((0, 6, 5),), ((0, 5, 6),), ((0, 4, 5, 6),)),
        (((0, 7, 6),), ((0, 7, 6),), ((0, 6, 7),), ((0, 2, 6, 7),)),
    ),
    (4, 0, 3): (
        (((0, 2, 3, 4),), ((0, 2, 3, 4),), ((0, 4, 3, 2),), ((0, 2, 3, 4),)),
        (((0, 5, 4, 3),), ((0, 3, 4, 5),), ((0, 5, 4, 3),), ((0, 5, 4, 3),)),
        (((0, 4, 5, 6),), ((0, 4, 5, 6),), ((0, 6, 5, 4),), ((0, 4, 5, 6),)),
        (((0, 7, 6, 5),), ((0, 5, 6, 7),), ((0, 7, 6, 5),), ((0, 7, 6, 5),)),
    ),
    (4, 0, 2): (
        (((0, 3, 1, 4),), ((0, 3, 4),), ((0, 4, 3),), ((0, 3, 7, 4),)),
        (((0, 0, 4, 5),), ((0, 4, 5),), ((0, 7, 4, 5),), ((0, 5, 4),)),
        (((0, 5, 6),), ((0, 1, 6, 5),), ((0, 1, 5, 6),), ((0, 6, 5),)),
        (((0, 2, 7, 6),), ((0, 2, 7, 6),), ((0, 2, 6, 7),), ((0, 0, 6, 7),)),
    ),
    (4, 1, 3): (
        (((0, 4, 3, 2),), ((0, 2, 3, 4),), ((0, 2, 3, 4),), ((0, 2, 3, 4),)),
        (((0, 5, 4, 3),), ((0, 5, 4, 3),), ((0, 5, 4, 3),), ((0, 5, 4, 3),)),
        (((0, 6, 5, 4),), ((0, 4, 5, 6),), ((0, 4, 5, 6),), ((0, 4, 5, 6),)),
        (((0, 7, 6, 5),), ((0, 7, 6, 5),), ((0, 7, 6, 5),), ((0, 7, 6, 5),)),
    ),
    (4, 1, 2): (
        (((0, 1, 2, 3),), ((0, 3, 2),), ((0, 2, 3),), ((0, 3, 2),)),
        (((0, 4, 3),), ((0, 4, 3),), ((0, 3, 4),), ((0, 4, 3),)),
        (((0, 7, 4, 5),), ((0, 1, 5, 4),), ((0, 4, 5),), ((0, 5, 4),)),
        (((0, 2, 5, 6),), ((0, 6, 4, 5),), ((0, 1, 6, 5),), ((0, 2, 5, 6),)),
    ),
    (5, 0, 3): (
        (((0, 1, 2, 3),), ((0, 1, 2, 3),), ((0, 3, 2, 1),), ((0, 1, 2, 3),)),
        (((0, 2, 3, 4),), ((0, 4, 3, 2),), ((0, 2, 3, 4),), ((0, 4, 3, 2),)),
        (((0, 3, 4, 5),), ((0, 3, 4, 5),), ((0, 5, 4, 3),), ((0, 3, 4, 5),)),
        (((0, 4, 5, 6),), ((0, 6, 5, 4),), ((0, 4, 5, 6),), ((0, 6, 5, 4),)),
    ),
    (5, 0, 2): (
        (((0, 3, 2),), ((0, 3, 2),), ((0, 2, 3),), ((0, 2, 3),)),
        (((0, 4, 3),), ((0, 4, 3),), ((0, 3, 0, 4),), ((0, 5, 4, 3),)),
        (((0, 5, 4),), ((0, 5, 4),), ((0, 4, 5),), ((0, 7, 5, 4),)),
        (((0, 2, 5, 6),), ((0, 6, 5),), ((0, 1, 6, 5),), ((0, 0, 6, 5),)),
    ),
    (5, 1, 3): (
        (((0, 1, 2, 3),), ((0, 3, 2, 1),), ((0, 3, 2, 1),), ((0, 3, 2, 1),)),
        (((0, 2, 3, 4),), ((0, 2, 3, 4),), ((0, 4, 3, 2),), ((0, 4, 3, 2),)),
        (((0, 3, 4, 5),), ((0, 5, 4, 3),), ((0, 5, 4, 3),), ((0, 5, 4, 3),)),
        (((0, 4, 5, 6),), ((0, 4, 5, 6),), ((0, 6, 5, 4),), ((0, 6, 5, 4),)),
    ),
    (5, 1, 2): (
        (((0, 1, 2),), ((0, 1, 5, 2),), ((0, 3, 2, 1),), ((0, 1, 5, 2),)),
        (((0, 2, 3),), ((0, 6, 2, 3),), ((0, 0, 3, 2),), ((0, 2, 6, 3),)),
        (((0, 3, 1, 4),), ((0, 3, 7, 4),), ((0, 6, 4, 3),), ((0, 3, 7, 4),)),
        (((0, 0, 4, 5),), ((0, 0, 4, 5),), ((0, 1, 5, 4),), ((0, 0, 4, 5),)),
    ),
    (6, 0, 3): (
        (((0, 1, 2),), ((0, 3, 2, 1),), ((0, 2, 1),), ((0, 2, 1),)),
        (((0, 2, 3),), ((0, 2, 3),), ((0, 3, 2),), ((0, 3, 2),)),
        (((0, 3, 4),), ((0, 1, 4, 3),), ((0, 4, 3),), ((0, 4, 3),)),
        (((0, 4, 5),), ((0, 4, 5),), ((0, 5, 4),), ((0, 5, 4),)),
    ),
    (6, 0, 2): (
        (((0, 3, 2, 1),), ((0, 1, 2),), ((0, 1, 5, 2),), ((0, 5, 1, 2),)),
        (((0, 0, 3, 2),), ((0, 0, 3, 2),), ((0, 6, 2, 3),), ((0, 2, 6, 3),)),
        (((0, 5, 4, 3),), ((0, 3, 4),), ((0, 3, 7, 4),), ((0, 3, 7, 4),)),
        (((0, 2, 5, 4),), ((0, 2, 5, 4),), ((0, 0, 4, 5),), ((0, 0, 4, 5),)),
    ),
    (6, 1, 3): (
        (((0, 3, 1, 2),), ((0, 3, 2, 1),), ((0, 1, 2),), ((0, 3, 2, 1),)),
        (((0, 0, 2, 3),), ((0, 0, 3, 2),), ((0, 0, 3, 2),), ((0, 2, 3),)),
        (((0, 1, 3, 4),), ((0, 5, 4, 3),), ((0, 3, 4),), ((0, 5, 4, 3),)),
        (((0, 6, 4, 5),), ((0, 2, 5, 4),), ((0, 2, 5, 4),), ((0, 4, 5),)),
    ),
    (6, 1, 2): (
        (((0, 1),), ((0, 1),), ((0, 1),), ((0, 4, 1),)),
        (((0, 2),), ((0, 2),), ((0, 2),), ((0, 5, 2),)),
        (((0, 3),), ((0, 3),), ((0, 3),), ((0, 6, 3),)),
        (((0, 0, 4),), ((0, 0, 4),), ((0, 4),), ((0, 7, 4),)),
    ),
    (7, 0, 3): (
        (((0, 7, 1),), ((0, 7, 1),), ((0, 7, 1),), ((0, 7, 1),)),
        (((0, 0, 2),), ((0, 0, 2),), ((0, 0, 2),), ((0, 0, 2),)),
        (((0, 1, 3),), ((0, 1, 3),), ((0, 1, 3),), ((0, 1, 3),)),
        (((0, 2, 4),), ((0, 2, 4),), ((0, 2, 4),), ((0, 2, 4),)),
    ),
    (7, 0, 2): (
        (((0, 1),), ((0, 1),), ((0, 1),), ((0, 1),)),
        (((0, 2),), ((0, 2),), ((0, 2),), ((0, 2),)),
        (((0, 3),), ((0, 3),), ((0, 3),), ((0, 3),)),
        (((0, 0, 4),), ((0, 0, 4),), ((0, 4),), ((0, 4),)),
    ),
    (7, 1, 3): (
        (((0, 1, 7),), ((0, 1, 7),), ((0, 1, 7),), ((0, 1, 7),)),
        (((0, 2, 0),), ((0, 2, 0),), ((0, 2, 0),), ((0, 2, 0),)),
        (((0, 3, 1),), ((0, 3, 1),), ((0, 3, 1),), ((0, 3, 1),)),
        (((0, 4, 2),), ((0, 4, 2),), ((0, 4, 2),), ((0, 4, 2),)),
    ),
    (7, 1, 2): (
        (((0, 3, 7),), ((0, 3, 7),), ((0, 7),), ((0, 7),)),
        (((0, 0),), ((0, 0),), ((0, 0),), ((0, 0),)),
        (((0, 1),), ((0, 1),), ((0, 1),), ((0, 1),)),
        (((0, 2),), ((0, 2),), ((0, 2),), ((0, 2),)),
    ),
}


def place(x, y, core, z, half):
    return (x % XS * 8 + y % YS * 2 + core) * 16 + z % ZS * 2 + half


def everywhere():
    for x in range(XS):
        for y in range(YS):
            for core in range(2):
                for z in range(ZS):
                    for half in range(2):
                        yield x, y, core, z, half


def weight_plan():
    moves = {}
    found = {}
    for (z, half, kept), by_y in ROUTES.items():
        core = half if kept == 3 else 1 - half
        for x in range(XS):
            for y in range(YS):
                for part in range(PARTS):
                    for chain, *chips in by_y[y][part]:
                        at = place(x, y, core, z, half)
                        for step, chip in enumerate(chips, FIRST[chain]):
                            to = place(x + chip // 4, chip % 4, core, z, half)
                            moves.setdefault((step, chain, part), []).append((at, to))
                            found[to, part, (x * 4 + y)] = (step, chain)
                            at = to
    keys = sorted(moves)
    table = np.zeros((256, PARTS, 3), np.int32)
    for x, y, core, z, half in everywhere():
        me = place(x, y, core, z, half)
        chip = 4 * x + y
        first = 2 if (half, core) == (1, 0) else 0
        second = 0 if (half, core) == (0, 1) else 2
        ends = (first, second) if core == 0 else (second, first)
        for part in range(PARTS):
            for slot, offset in enumerate((1,) + ends):
                source = (chip + z + offset) % 8
                if source != chip:
                    table[me, part, slot] = 1 + keys.index(found[me, part, source] + (part,))
    return {key: moves[key] for key in keys}, table


def token_plan():
    shift, first, second, keep, send = [], [], [], [], []
    for x, y, core, z, half in everywhere():
        me = place(x, y, core, z, half)
        shift.append((me, place(x, y, core, z - 4 * x - y - 1, half)))
        if core == half:
            first.append((me, place(x, y, core, z, 1 - half)))
        else:
            first.append((me, place(x, y, 1 - core, z, half)))
            second.append((me, place(x, y, 1 - core, z, 1 - half)))
        keep.append((place(x, y, core, z + (1 if half else -1), half), me))
        send.append((place(x, y, core, z + (-1 if core else 1), half), me))
    return shift, first, second, keep, send


def product_kernel(slots, last, rows, held_at, index, *refs):
    buffers = refs[: 1 + len(held_at)]
    tokens, out, held, sems = refs[1 + len(held_at) : -3 - last], refs[-3], refs[-2], refs[-1]
    jobs = [(part, side) for part in range(PARTS) for side in range(1 + last)]
    early = sum(step < ROUNDS - 1 for step, _, _ in held_at)

    def fetch(part, side, source):
        return pltpu.make_async_copy(source, held.at[side, part], sems.at[side, part])

    def own(part):
        return buffers[0].at[pl.ds(part * rows, rows)]

    def due(part, side):
        which = index[part * 3 + slots[side]]
        came_late = which > early
        if side:
            return which, which >= 0
        return which, came_late if last else jnp.logical_not(came_late)

    for part, side in jobs:
        which, wanted = due(part, side)
        if not last or side:

            @pl.when(which == 0)
            def _():
                fetch(part, side, own(part)).start()

        for number, (step, _, of) in enumerate(held_at, 1):
            if of == part and (side or last == (step == ROUNDS - 1)):

                @pl.when(which == number)
                def _():
                    fetch(part, side, buffers[number]).start()

    if not last:
        out[...] = jnp.zeros_like(out)
    width = out.shape[1]
    for part, side in jobs:

        @pl.when(due(part, side)[1])
        def _():
            fetch(part, side, own(part)).wait()
            for low in range(0, width, 256):
                high = min(low + 256, width)
                out[:, low:high] += jnp.dot(
                    tokens[side][:, part * rows : (part + 1) * rows],
                    held[side, part, :, low:high],
                    preferred_element_type=jnp.float32,
                )


def product(slots, index, own, got, mid, *more):
    last = bool(more)
    rows = own.shape[0] // PARTS
    held_at = sorted(key for key in got if last or key[0] < ROUNDS - 1)
    buffers = [own] + [got[key] for key in held_at]
    tokens, width = mid.shape[0], own.shape[1]
    anywhere = pl.BlockSpec(memory_space=pl.ANY)
    whole = pl.BlockSpec(memory_space=pltpu.VMEM)
    return pl.pallas_call(
        functools.partial(product_kernel, slots, last, rows, held_at),
        out_shape=jax.ShapeDtypeStruct((tokens, width), jnp.float32),
        in_specs=[pl.BlockSpec(memory_space=pltpu.SMEM)] + [anywhere] * len(buffers) + [whole] * (1 + len(more)),
        out_specs=whole,
        input_output_aliases={len(buffers) + 3: 0} if last else {},
        scratch_shapes=[
            pltpu.VMEM((1 + last, PARTS, rows, width), jnp.bfloat16),
            pltpu.SemaphoreType.DMA((1 + last, PARTS)),
        ],
        compiler_params=pltpu.CompilerParams(vmem_limit_bytes=40 * 2**20),
        cost_estimate=pl.CostEstimate(
            flops=2 * tokens * own.shape[0] * width,
            bytes_accessed=2 * own.shape[0] * width + 8 * tokens * width,
            transcendentals=0,
        ),
    )(index, *buffers, mid, *more)


def on_device(tokens, gate_weight):
    me = lax.axis_index("row") * 16 + lax.axis_index("col")
    core = lax.axis_index("row") % 2
    half = lax.axis_index("col") % 2
    moves, table = weight_plan()
    index = lax.dynamic_index_in_dim(jnp.asarray(table.reshape(256, -1)), me, 0, keepdims=False)
    rows = gate_weight.shape[0] // PARTS
    parts = [gate_weight[part * rows : (part + 1) * rows] for part in range(PARTS)]

    shift, first, second, near_keep, near_send = token_plan()

    def after(value, *others):
        return lax.optimization_barrier((value,) + others)[0]

    def send(value, pairs):
        return lax.ppermute(value, BOTH, pairs)

    got = {}

    def weights(step, part, *others):
        value = parts[part] if step == 0 else got[step - 1, 0, part]
        value = after(value, *others) if others else value
        got[step, 0, part] = send(value, moves[step, 0, part])
        return got[step, 0, part]

    def product_of(slots, *operands):
        return product(slots, index, gate_weight, *operands)

    shifted = send(tokens, shift)
    parts = [after(value, tokens) for value in parts]
    for part in range(PARTS):
        weights(0, part)
    weights(1, 0)
    weights(1, 1)
    weights(1, 2, shifted)
    shifted = after(shifted, got[0, 0, 0], got[0, 0, 1])
    crossed, also = send(shifted, first), send(shifted, second)
    weights(1, 3)
    weights(2, 0)
    weights(2, 1, crossed, also)
    keep_mid = jnp.where(core == half, shifted, crossed)
    send_mid = jnp.where(core == half, crossed, also)
    keep_end, send_end = send(keep_mid, near_keep), send(send_mid, near_send)
    weights(2, 2)
    weights(2, 3)
    early = {key: value for key, value in got.items() if key[0] < 2}
    sent = product_of((0, 2), early, send_mid)
    kept = product_of((0, 1), early, keep_mid)
    keep_end, send_end, sent, kept = lax.optimization_barrier((keep_end, send_end, sent, kept))
    sent = product_of((0, 2), got, send_mid, send_end, sent)
    swap = [(place(x, y, c, z, h), place(x, y, 1 - c, z, h)) for x, y, c, z, h in everywhere()]
    arrived = send(sent, swap)
    kept = product_of((0, 1), got, keep_mid, keep_end, kept)
    return kept + arrived

def solution(mesh):
    placed = (P("row", "col"), P("row", "col"))
    return jax.shard_map(
        on_device, mesh=mesh, in_specs=placed, out_specs=P("row", "col"), check_vma=False
    )
```

time: 512 us -> 184 us (0.36)
  the two profiles are of different devices: /device:TPU:2 before, /device:TPU:108 now
where the time goes in v2:
time: 184 us; the launch traced here: 183 us
  starting transfers between devices  92.9 us (50%)
  waiting for transfers between devices  61.4 us (33%)
  Pallas kernels  17.4 us (9%)
  local copies, waits for them, and re-layouts  7.02 us (4%)
  other arithmetic  4.11 us (2%)
    ppermute x18, starting transfers between devices, send(): return lax.ppermute(value, BOTH, pairs)  92.9 us
    ppermute x18, waiting for transfers between devices, send(): return lax.ppermute(value, BOTH, pairs)  61.4 us
    pallas_call x4, Pallas kernels, product(): pl.pallas_call(functools.partial(product_kernel, slots, last, rows, held_...  17.4 us
  transfers between devices with their start and end apart: 18, of which 5 were waited for; matrix products, arithmetic and copies ran while one was open for 2% of the time, Pallas kernels for 7%

profile of v2, /device:TPU:108, one launch (start us, length us, event | category | flops | bytes accessed | tf_op | source)
XLA Modules:
  0.0 183.0 jit_solution(5636690343891157897)
XLA Ops:
  0.0 3.4 %fusion = (bf16[256,1664]{1,0:T(8,128)(2,1)}, bf16[256,1664]{1,0:T(8,128)(2,1)}, bf16[256,1664]{1,0:T(8,128)(2,1)S(1)}, bf16[256,1664]{1,0:T(8,128)(2,1)S(1)}) fusion(bf16[1024,1664]{1,0:T(8,128)(2,1)} %refs_0_.7), kind=kLoop, calls=%fused_computation.3 | loop fusion | bytes 6815744 | tf_op jit(solution)/shard_map/slice | solution.py:357
  3.4 0.4 collective-permute-start
  3.9 1.2 collective-permute-start.1
  5.1 3.1 %collective-permute-start.6 = (bf16[384,1024]{1,0:T(8,128)(2,1)S(1)}, bf16[384,1024]{1,0:T(8,128)(2,1)}, u32[]{:S(2)}, u32[]{:S(2)}) collective-permute-start(bf16[384,1024]{1,0:T(8,128)(2,1)S(1)} %copy-done.5), channel_id=1, source_target_pairs={{0,14},{1,15},{2,0},{3,1},{4,2},{5,3},{6,4},{7,5},{8,6},{9,7},{10,... | collective-permute-start | bytes 2359304 | tf_op jit(solution)/shard_map/ppermute | solution.py:365
  8.1 5.5 %collective-permute-start.2 = (bf16[256,1664]{1,0:T(8,128)(2,1)}, bf16[256,1664]{1,0:T(8,128)(2,1)}, u32[]{:S(2)}, u32[]{:S(2)}) collective-permute-start(bf16[256,1664]{1,0:T(8,128)(2,1)} %get-tuple-element.18), channel_id=1, source_target_pairs={{0,32},{32,64},{64,96},{96,0},{128,160},{160,192},{192,224},{224,1... | collective-permute-start | bytes 2555912 | tf_op jit(solution)/shard_map/ppermute | solution.py:365
  13.7 23.5 %collective-permute-done.6 = bf16[384,1024]{1,0:T(8,128)(2,1)} collective-permute-done((bf16[384,1024]{1,0:T(8,128)(2,1)S(1)}, bf16[384,1024]{1,0:T(8,128)(2,1)}, u32[]{:S(2)}, u32[]{:S(2)}) %collective-permute-start.6) | collective-permute-done | bytes 786464 | tf_op jit(solution)/shard_map/ppermute | solution.py:365
  37.2 4.1 %collective-permute-start.11 = (bf16[384,1024]{1,0:T(8,128)(2,1)}, bf16[384,1024]{1,0:T(8,128)(2,1)}, u32[]{:S(2)}, u32[]{:S(2)}) collective-permute-start(bf16[384,1024]{1,0:T(8,128)(2,1)} %collective-permute-done.6), channel_id=1, source_target_pairs={{1,16},{3,18},{5,20},{7,22},{9,24},{11,26},{13,28},{15,30},{16,1},... | collective-permute-start | bytes 2359304 | tf_op jit(solution)/shard_map/ppermute | solution.py:365
  41.3 2.0 %collective-permute-start.10 = (bf16[384,1024]{1,0:T(8,128)(2,1)}, bf16[384,1024]{1,0:T(8,128)(2,1)}, u32[]{:S(2)}, u32[]{:S(2)}) collective-permute-start(bf16[384,1024]{1,0:T(8,128)(2,1)} %collective-permute-done.6), channel_id=1, source_target_pairs={{0,1},{1,17},{2,3},{3,19},{4,5},{5,21},{6,7},{7,23},{8,9},{9,25},{... | collective-permute-start | bytes 2359304 | tf_op jit(solution)/shard_map/ppermute | solution.py:365
  43.4 1.8 collective-permute-done.2.refs_3_
  45.1 23.6 %collective-permute-start.7 = (bf16[256,1664]{1,0:T(8,128)(2,1)}, bf16[256,1664]{1,0:T(8,128)(2,1)}, u32[]{:S(2)}, u32[]{:S(2)}) collective-permute-start(bf16[256,1664]{1,0:T(8,128)(2,1)} %collective-permute-done.2.refs_3_), channel_id=1, source_target_pairs={{32,192},{64,224},{96,0},{0,32},{160,64},{192,96},{224,128},{128,1... | collective-permute-start | bytes 2555912 | tf_op jit(solution)/shard_map/ppermute | solution.py:365
  68.7 1.9 %collective-permute-start.4 = (bf16[256,1664]{1,0:T(8,128)(2,1)}, bf16[256,1664]{1,0:T(8,128)(2,1)}, u32[]{:S(2)}, u32[]{:S(2)}) collective-permute-start(bf16[256,1664]{1,0:T(8,128)(2,1)} %collective-permute-done.refs_1_), channel_id=1, source_target_pairs={{32,224},{64,0},{96,32},{0,64},{160,96},{192,128},{224,160},{128,1... | collective-permute-start | bytes 2555912 | tf_op jit(solution)/shard_map/ppermute | solution.py:365
  70.7 2.1 %collective-permute-start.5 = (bf16[256,1664]{1,0:T(8,128)(2,1)}, bf16[256,1664]{1,0:T(8,128)(2,1)}, u32[]{:S(2)}, u32[]{:S(2)}) collective-permute-start(bf16[256,1664]{1,0:T(8,128)(2,1)} %collective-permute-done.1.refs_2_), channel_id=1, source_target_pairs={{160,192},{0,224},{96,0},{64,32},{32,64},{128,96},{224,128},{192,1... | collective-permute-start | bytes 2555912 | tf_op jit(solution)/shard_map/ppermute | solution.py:365
  72.8 5.1 %collective-permute-done.11 = bf16[384,1024]{1,0:T(8,128)(2,1)} collective-permute-done((bf16[384,1024]{1,0:T(8,128)(2,1)}, bf16[384,1024]{1,0:T(8,128)(2,1)}, u32[]{:S(2)}, u32[]{:S(2)}) %collective-permute-start.11) | collective-permute-done | bytes 786464 | tf_op jit(solution)/shard_map/ppermute | solution.py:365
  77.8 1.9 %collective-permute-start.8 = (bf16[256,1664]{1,0:T(8,128)(2,1)}, bf16[256,1664]{1,0:T(8,128)(2,1)}, u32[]{:S(2)}, u32[]{:S(2)}) collective-permute-start(bf16[256,1664]{1,0:T(8,128)(2,1)} %collective-permute-done.3.refs_4_), channel_id=1, source_target_pairs={{224,192},{64,224},{32,0},{0,32},{96,64},{192,96},{160,128},{128,1... | collective-permute-start | bytes 2555912 | tf_op jit(solution)/shard_map/ppermute | solution.py:365
  79.7 16.1 %collective-permute-done.10 = bf16[384,1024]{1,0:T(8,128)(2,1)} collective-permute-done((bf16[384,1024]{1,0:T(8,128)(2,1)}, bf16[384,1024]{1,0:T(8,128)(2,1)}, u32[]{:S(2)}, u32[]{:S(2)}) %collective-permute-start.10) | collective-permute-done | bytes 786464 | tf_op jit(solution)/shard_map/ppermute | solution.py:365
  95.9 2.4 %broadcast_select_fusion = (bf16[384,1024]{1,0:T(8,128)(2,1)S(1)}, bf16[384,1024]{1,0:T(8,128)(2,1)}) fusion(bf16[384,1024]{1,0:T(8,128)(2,1)} %collective-permute-done.10, bf16[384,1024]{1,0:T(8,128)(2,1)} %collective-permute-done.11, pred[]{:T(512)S(6)} %eq.7, bf16[384,1024]{1,0:T(8,128)(2,1)} %collective-permute-done.6), kind=kLoop, calls=%fused_computation | loop fusion | flops 786432 | bytes 3932161 | tf_op jit(solution)/shard_map/jit(_where)/select_n | solution.py:391
  98.2 2.9 %collective-permute-start.16 = (bf16[384,1024]{1,0:T(8,128)(2,1)S(1)}, bf16[384,1024]{1,0:T(8,128)(2,1)S(1)}, u32[]{:S(2)}, u32[]{:S(2)}) collective-permute-start(bf16[384,1024]{1,0:T(8,128)(2,1)S(1)} %get-tuple-element.31.refs_9_.refs_13_), channel_id=1, source_target_pairs={{2,0},{3,1},{4,2},{5,3},{6,4},{7,5},{8,6},{9,7},{10,8},{11,9},{12,... | collective-permute-start | bytes 2359304 | tf_op jit(solution)/shard_map/ppermute | solution.py:365
  101.2 0.9 copy-done.1
  102.1 1.7 collective-permute-start.12
  103.7 10.9 %collective-permute-start.9 = (bf16[256,1664]{1,0:T(8,128)(2,1)}, bf16[256,1664]{1,0:T(8,128)(2,1)}, u32[]{:S(2)}, u32[]{:S(2)}) collective-permute-start(bf16[256,1664]{1,0:T(8,128)(2,1)} %collective-permute-done.4.refs_5_), channel_id=1, source_target_pairs={{224,192},{0,224},{32,0},{64,32},{96,64},{128,96},{160,128},{192,1... | collective-permute-start | bytes 2555912 | tf_op jit(solution)/shard_map/ppermute | solution.py:365
  114.6 1.6 collective-permute-start.13
  116.3 2.2 %collective-permute-start.14 = (bf16[256,1664]{1,0:T(8,128)(2,1)}, bf16[256,1664]{1,0:T(8,128)(2,1)}, u32[]{:S(2)}, u32[]{:S(2)}) collective-permute-start(bf16[256,1664]{1,0:T(8,128)(2,1)} %collective-permute-done.8.refs_8_), channel_id=1, source_target_pairs={{224,0},{32,64},{96,128},{160,192},{241,209},{145,241},{49,17},{20... | collective-permute-start | bytes 2555912 | tf_op jit(solution)/shard_map/ppermute | solution.py:365
  118.5 0.9 copy-done.3
  119.4 0.7 dynamic-slice_bitcast_fusion.index
  120.1 1.1 copy-done.2
  121.2 3.4 %shard_map.37.refs_15_ = f32[384,1664]{1,0:T(8,128)S(1)} custom-call(s32[12]{0:T(128)S(1)} %dynamic-slice_bitcast_fusion.index, bf16[1024,1664]{1,0:T(8,128)(2,1)S(1)} %copy-done, bf16[256,1664]{1,0:T(8,128)(2,1)} %collective-permute-done.refs_1_, bf16[256,1664]{1,0:T(8,128)(2,1)} %collective-permute-done.1.refs_2_, ...), custom_call_target="tpu_custom_call" | custom-call | flops 1308622848 | bytes 8519680 | tf_op jit(solution)/shard_map/pallas_call | solution.py:331
  124.6 4.1 %shard_map.38.refs_15_ = f32[384,1664]{1,0:T(8,128)S(1)} custom-call(s32[12]{0:T(128)S(1)} %dynamic-slice_bitcast_fusion.index, bf16[1024,1664]{1,0:T(8,128)(2,1)S(1)} %copy-done, bf16[256,1664]{1,0:T(8,128)(2,1)} %collective-permute-done.refs_1_, bf16[256,1664]{1,0:T(8,128)(2,1)} %collective-permute-done.1.refs_2_, ...), custom_call_target="tpu_custom_call" | custom-call | flops 1308622848 | bytes 8519680 | tf_op jit(solution)/shard_map/pallas_call | solution.py:331
  128.6 14.9 %collective-permute-done.15.refs_14_ = bf16[384,1024]{1,0:T(8,128)(2,1)} collective-permute-done((bf16[384,1024]{1,0:T(8,128)(2,1)}, bf16[384,1024]{1,0:T(8,128)(2,1)}, u32[]{:S(2)}, u32[]{:S(2)}) %collective-permute-start.15) | collective-permute-done | bytes 786464 | tf_op jit(solution)/shard_map/ppermute | solution.py:365
  143.6 4.7 %shard_map.40 = f32[384,1664]{1,0:T(8,128)S(1)} custom-call(s32[12]{0:T(128)S(1)} %dynamic-slice_bitcast_fusion.index, bf16[1024,1664]{1,0:T(8,128)(2,1)} %refs_0_.7, bf16[256,1664]{1,0:T(8,128)(2,1)} %collective-permute-done.refs_1_, bf16[256,1664]{1,0:T(8,128)(2,1)} %collective-permute-done.1.refs_2_, ...), custom_call_target="tpu_custom_call", output_to_operand_aliasing={{}: (16, {})} | custom-call | flops 1308622848 | bytes 8519680 | tf_op jit(solution)/shard_map/pallas_call | solution.py:331
  148.2 27.7 %collective-permute-start.17 = (f32[384,1664]{1,0:T(8,128)S(1)}, f32[384,1664]{1,0:T(8,128)S(1)}, u32[]{:S(2)}, u32[]{:S(2)}) collective-permute-start(f32[384,1664]{1,0:T(8,128)S(1)} %shard_map.40), channel_id=1, source_target_pairs={{0,16},{1,17},{2,18},{3,19},{4,20},{5,21},{6,22},{7,23},{8,24},{9,... | collective-permute-start | bytes 7667720 | tf_op jit(solution)/shard_map/ppermute | solution.py:365
  175.9 5.3 %shard_map.39 = f32[384,1664]{1,0:T(8,128)S(1)} custom-call(s32[12]{0:T(128)S(1)} %dynamic-slice_bitcast_fusion.index, bf16[1024,1664]{1,0:T(8,128)(2,1)} %refs_0_.7, bf16[256,1664]{1,0:T(8,128)(2,1)} %collective-permute-done.refs_1_, bf16[256,1664]{1,0:T(8,128)(2,1)} %collective-permute-done.1.refs_2_, ...), custom_call_target="tpu_custom_call", output_to_operand_aliasing={{}: (16, {})} | custom-call | flops 1308622848 | bytes 8519680 | tf_op jit(solution)/shard_map/pallas_call | solution.py:331
  181.3 1.7 add.21
  (24 shorter events, 0.1 us)
Async XLA Ops:
  0.0 5.1 %copy-start.5 = (bf16[384,1024]{1,0:T(8,128)(2,1)S(1)}, bf16[384,1024]{1,0:T(8,128)(2,1)}, u32[]{:S(2)}) copy-start(bf16[384,1024]{1,0:T(8,128)(2,1)} %param.3) | copy-start | bytes 2359300
  3.4 116.6 %copy-start = (bf16[1024,1664]{1,0:T(8,128)(2,1)S(1)}, bf16[1024,1664]{1,0:T(8,128)(2,1)}, u32[]{:S(2)}) copy-start(bf16[1024,1664]{1,0:T(8,128)(2,1)} %refs_0_.7) | copy-start | bytes 10223620
  3.4 33.8 %collective-permute-start = (bf16[256,1664]{1,0:T(8,128)(2,1)S(1)}, bf16[256,1664]{1,0:T(8,128)(2,1)}, u32[]{:S(2)}, u32[]{:S(2)}) collective-permute-start(bf16[256,1664]{1,0:T(8,128)(2,1)S(1)} %get-tuple-element.16), channel_id=1, source_target_pairs={{0,32},{32,64},{64,96},{96,0},{128,160},{160,192},{192,224},{224,1... | collective-permute-start | bytes 2555912 | tf_op jit(solution)/shard_map/ppermute | solution.py:365
  3.9 33.3 %collective-permute-start.1 = (bf16[256,1664]{1,0:T(8,128)(2,1)S(1)}, bf16[256,1664]{1,0:T(8,128)(2,1)}, u32[]{:S(2)}, u32[]{:S(2)}) collective-permute-start(bf16[256,1664]{1,0:T(8,128)(2,1)S(1)} %get-tuple-element.17), channel_id=1, source_target_pairs={{0,160},{32,0},{64,96},{96,64},{128,32},{160,128},{192,224},{224,1... | collective-permute-start | bytes 2555912 | tf_op jit(solution)/shard_map/ppermute | solution.py:365
  5.1 32.1 %collective-permute-start.6 = (bf16[384,1024]{1,0:T(8,128)(2,1)S(1)}, bf16[384,1024]{1,0:T(8,128)(2,1)}, u32[]{:S(2)}, u32[]{:S(2)}) collective-permute-start(bf16[384,1024]{1,0:T(8,128)(2,1)S(1)} %copy-done.5), channel_id=1, source_target_pairs={{0,14},{1,15},{2,0},{3,1},{4,2},{5,3},{6,4},{7,5},{8,6},{9,7},{10,... | collective-permute-start | bytes 2359304 | tf_op jit(solution)/shard_map/ppermute | solution.py:365
  8.1 37.0 %collective-permute-start.2 = (bf16[256,1664]{1,0:T(8,128)(2,1)}, bf16[256,1664]{1,0:T(8,128)(2,1)}, u32[]{:S(2)}, u32[]{:S(2)}) collective-permute-start(bf16[256,1664]{1,0:T(8,128)(2,1)} %get-tuple-element.18), channel_id=1, source_target_pairs={{0,32},{32,64},{64,96},{96,0},{128,160},{160,192},{192,224},{224,1... | collective-permute-start | bytes 2555912 | tf_op jit(solution)/shard_map/ppermute | solution.py:365
  13.7 57.0 %collective-permute-start.3 = (bf16[256,1664]{1,0:T(8,128)(2,1)}, bf16[256,1664]{1,0:T(8,128)(2,1)}, u32[]{:S(2)}, u32[]{:S(2)}) collective-permute-start(bf16[256,1664]{1,0:T(8,128)(2,1)} %get-tuple-element.19), channel_id=1, source_target_pairs={{0,224},{32,64},{64,32},{96,0},{128,96},{160,192},{192,160},{224,1... | collective-permute-start | bytes 2555912 | tf_op jit(solution)/shard_map/ppermute | solution.py:365
  37.2 40.6 %collective-permute-start.11 = (bf16[384,1024]{1,0:T(8,128)(2,1)}, bf16[384,1024]{1,0:T(8,128)(2,1)}, u32[]{:S(2)}, u32[]{:S(2)}) collective-permute-start(bf16[384,1024]{1,0:T(8,128)(2,1)} %collective-permute-done.6), channel_id=1, source_target_pairs={{1,16},{3,18},{5,20},{7,22},{9,24},{11,26},{13,28},{15,30},{16,1},... | collective-permute-start | bytes 2359304 | tf_op jit(solution)/shard_map/ppermute | solution.py:365
  41.3 54.5 %collective-permute-start.10 = (bf16[384,1024]{1,0:T(8,128)(2,1)}, bf16[384,1024]{1,0:T(8,128)(2,1)}, u32[]{:S(2)}, u32[]{:S(2)}) collective-permute-start(bf16[384,1024]{1,0:T(8,128)(2,1)} %collective-permute-done.6), channel_id=1, source_target_pairs={{0,1},{1,17},{2,3},{3,19},{4,5},{5,21},{6,7},{7,23},{8,9},{9,25},{... | collective-permute-start | bytes 2359304 | tf_op jit(solution)/shard_map/ppermute | solution.py:365
  45.1 69.5 %collective-permute-start.7 = (bf16[256,1664]{1,0:T(8,128)(2,1)}, bf16[256,1664]{1,0:T(8,128)(2,1)}, u32[]{:S(2)}, u32[]{:S(2)}) collective-permute-start(bf16[256,1664]{1,0:T(8,128)(2,1)} %collective-permute-done.2.refs_3_), channel_id=1, source_target_pairs={{32,192},{64,224},{96,0},{0,32},{160,64},{192,96},{224,128},{128,1... | collective-permute-start | bytes 2555912 | tf_op jit(solution)/shard_map/ppermute | solution.py:365
  68.7 35.0 %collective-permute-start.4 = (bf16[256,1664]{1,0:T(8,128)(2,1)}, bf16[256,1664]{1,0:T(8,128)(2,1)}, u32[]{:S(2)}, u32[]{:S(2)}) collective-permute-start(bf16[256,1664]{1,0:T(8,128)(2,1)} %collective-permute-done.refs_1_), channel_id=1, source_target_pairs={{32,224},{64,0},{96,32},{0,64},{160,96},{192,128},{224,160},{128,1... | collective-permute-start | bytes 2555912 | tf_op jit(solution)/shard_map/ppermute | solution.py:365
  70.7 31.4 %collective-permute-start.5 = (bf16[256,1664]{1,0:T(8,128)(2,1)}, bf16[256,1664]{1,0:T(8,128)(2,1)}, u32[]{:S(2)}, u32[]{:S(2)}) collective-permute-start(bf16[256,1664]{1,0:T(8,128)(2,1)} %collective-permute-done.1.refs_2_), channel_id=1, source_target_pairs={{160,192},{0,224},{96,0},{64,32},{32,64},{128,96},{224,128},{192,1... | collective-permute-start | bytes 2555912 | tf_op jit(solution)/shard_map/ppermute | solution.py:365
  77.8 38.5 %collective-permute-start.8 = (bf16[256,1664]{1,0:T(8,128)(2,1)}, bf16[256,1664]{1,0:T(8,128)(2,1)}, u32[]{:S(2)}, u32[]{:S(2)}) collective-permute-start(bf16[256,1664]{1,0:T(8,128)(2,1)} %collective-permute-done.3.refs_4_), channel_id=1, source_target_pairs={{224,192},{64,224},{32,0},{0,32},{96,64},{192,96},{160,128},{128,1... | collective-permute-start | bytes 2555912 | tf_op jit(solution)/shard_map/ppermute | solution.py:365
  98.2 20.2 %collective-permute-start.16 = (bf16[384,1024]{1,0:T(8,128)(2,1)S(1)}, bf16[384,1024]{1,0:T(8,128)(2,1)S(1)}, u32[]{:S(2)}, u32[]{:S(2)}) collective-permute-start(bf16[384,1024]{1,0:T(8,128)(2,1)S(1)} %get-tuple-element.31.refs_9_.refs_13_), channel_id=1, source_target_pairs={{2,0},{3,1},{4,2},{5,3},{6,4},{7,5},{8,6},{9,7},{10,8},{11,9},{12,... | collective-permute-start | bytes 2359304 | tf_op jit(solution)/shard_map/ppermute | solution.py:365
  101.2 0.9 copy-start.1
  102.1 41.5 %collective-permute-start.12 = (bf16[256,1664]{1,0:T(8,128)(2,1)}, bf16[256,1664]{1,0:T(8,128)(2,1)}, u32[]{:S(2)}, u32[]{:S(2)}) collective-permute-start(bf16[256,1664]{1,0:T(8,128)(2,1)} %collective-permute-done.5.refs_6_), channel_id=1, source_target_pairs={{192,224},{0,32},{64,96},{128,160},{193,225},{225,1},{1,33},{33,65... | collective-permute-start | bytes 2555912 | tf_op jit(solution)/shard_map/ppermute | solution.py:365
  103.7 39.8 %collective-permute-start.9 = (bf16[256,1664]{1,0:T(8,128)(2,1)}, bf16[256,1664]{1,0:T(8,128)(2,1)}, u32[]{:S(2)}, u32[]{:S(2)}) collective-permute-start(bf16[256,1664]{1,0:T(8,128)(2,1)} %collective-permute-done.4.refs_5_), channel_id=1, source_target_pairs={{224,192},{0,224},{32,0},{64,32},{96,64},{128,96},{160,128},{192,1... | collective-permute-start | bytes 2555912 | tf_op jit(solution)/shard_map/ppermute | solution.py:365
  114.6 28.9 %collective-permute-start.13 = (bf16[256,1664]{1,0:T(8,128)(2,1)}, bf16[256,1664]{1,0:T(8,128)(2,1)}, u32[]{:S(2)}, u32[]{:S(2)}) collective-permute-start(bf16[256,1664]{1,0:T(8,128)(2,1)} %collective-permute-done.7.refs_7_), channel_id=1, source_target_pairs={{192,224},{224,0},{0,32},{32,64},{64,96},{96,128},{128,160},{160,1... | collective-permute-start | bytes 2555912 | tf_op jit(solution)/shard_map/ppermute | solution.py:365
  116.3 27.3 %collective-permute-start.14 = (bf16[256,1664]{1,0:T(8,128)(2,1)}, bf16[256,1664]{1,0:T(8,128)(2,1)}, u32[]{:S(2)}, u32[]{:S(2)}) collective-permute-start(bf16[256,1664]{1,0:T(8,128)(2,1)} %collective-permute-done.8.refs_8_), channel_id=1, source_target_pairs={{224,0},{32,64},{96,128},{160,192},{241,209},{145,241},{49,17},{20... | collective-permute-start | bytes 2555912 | tf_op jit(solution)/shard_map/ppermute | solution.py:365
  118.5 0.9 copy-start.3
  119.4 24.2 %collective-permute-start.15 = (bf16[384,1024]{1,0:T(8,128)(2,1)}, bf16[384,1024]{1,0:T(8,128)(2,1)}, u32[]{:S(2)}, u32[]{:S(2)}) collective-permute-start(bf16[384,1024]{1,0:T(8,128)(2,1)} %get-tuple-element.32.refs_9_.refs_13_), channel_id=1, source_target_pairs={{14,0},{3,1},{0,2},{5,3},{2,4},{7,5},{4,6},{9,7},{6,8},{11,9},{8,1... | collective-permute-start | bytes 2359304 | tf_op jit(solution)/shard_map/ppermute | solution.py:365
  120.1 1.1 copy-start.2
  124.6 19.0 %copy-start.4 = (bf16[384,1024]{1,0:T(8,128)(2,1)S(1)}, bf16[384,1024]{1,0:T(8,128)(2,1)}, u32[]{:S(2)}) copy-start(bf16[384,1024]{1,0:T(8,128)(2,1)} %copy-done.3) | copy-start | bytes 2359300
  148.2 33.1 %collective-permute-start.17 = (f32[384,1664]{1,0:T(8,128)S(1)}, f32[384,1664]{1,0:T(8,128)S(1)}, u32[]{:S(2)}, u32[]{:S(2)}) collective-permute-start(f32[384,1664]{1,0:T(8,128)S(1)} %shard_map.40), channel_id=1, source_target_pairs={{0,16},{1,17},{2,18},{3,19},{4,20},{5,21},{6,22},{7,23},{8,24},{9,... | collective-permute-start | bytes 7667720 | tf_op jit(solution)/shard_map/ppermute | solution.py:365

commit v3 on v2

v3 whole, which is shorter than its diff:
```python
import functools

import jax
import jax.numpy as jnp
import numpy as np
from jax import lax
from jax.experimental import pallas as pl
from jax.experimental.pallas import tpu as pltpu
from jax.sharding import PartitionSpec as P

XS, YS, ZS = 2, 4, 8
BOTH = ("row", "col")
ROUNDS = 4
PARTS = 4
WHEN = ((0, 1, 2), (0, 1, 3), (0, 2, 3), (1, 2, 3))

ROUTES = {
    (0, 0, 3): (
        ((1, 6, 7), (1, 6, 7), (6, 7), (7, 6)),
        ((2, 7, 0), (2, 7, 0), (5, 0, 7), (0, 7)),
        ((3, 0, 1), (3, 0, 1), (3, 1, 0), (1, 0)),
        ((0, 1, 2), (0, 1, 2), (0, 2, 1), (2, 1)),
    ),
    (0, 0, 2): (
        ((3, 7), (7,), (7,), (7,)),
        ((0,), (0,), (0,), (0,)),
        ((1,), (1,), (1,), (1,)),
        ((2,), (2,), (2,), (2,)),
    ),
    (0, 1, 3): (
        ((1, 6, 7), (1, 6, 7), (7, 6), (7, 6)),
        ((6, 7, 0), (7, 3, 0), (0, 3, 7), (0, 7)),
        ((3, 0, 1), (6, 0, 1), (1, 0), (1, 0)),
        ((0, 1, 2), (0, 1, 2), (2, 1), (2, 1)),
    ),
    (0, 1, 2): (
        ((1, 6, 7), (7, 6), (4, 7, 6), (7, 6)),
        ((2, 7, 0), (0, 7), (2, 0, 7), (0, 7)),
        ((3, 0, 1), (1, 0), (3, 1, 0), (1, 0)),
        ((0, 1, 2), (2, 1), (1, 2), (2, 1)),
    ),
    (1, 0, 3): (
        ((5, 6, 7), (7, 6, 5), (7, 6, 5), (7, 6, 5)),
        ((6, 7, 0), (6, 7, 0), (0, 7, 6), (6, 7, 0)),
        ((7, 0, 1), (1, 0, 7), (1, 0, 7), (1, 0, 7)),
        ((0, 1, 2), (0, 1, 2), (2, 1, 0), (0, 1, 2)),
    ),
    (1, 0, 2): (
        ((3, 6, 7), (1, 6, 7), (1, 6, 7), (7, 6)),
        ((2, 7, 0), (0, 7), (0, 7), (0, 3, 7)),
        ((1, 0), (3, 0, 1), (3, 0, 1), (1, 0)),
        ((0, 1, 2), (2, 1), (2, 1), (2, 1)),
    ),
    (1, 1, 3): (
        ((7, 6, 5), (5, 6, 7), (7, 6, 5), (5, 6, 7)),
        ((0, 7, 6), (0, 7, 6), (6, 7, 0), (0, 7, 6)),
        ((1, 0, 7), (7, 0, 1), (1, 0, 7), (7, 0, 1)),
        ((2, 1, 0), (2, 1, 0), (0, 1, 2), (2, 1, 0)),
    ),
    (1, 1, 2): (
        ((1, 6, 5), (2, 5, 6), (5, 6), (1, 6, 5)),
        ((6, 7), (7, 6), (6, 7), (6, 7)),
        ((7, 0), (0, 3, 7), (7, 0), (3, 0, 7)),
        ((0, 1), (1, 0), (0, 1), (0, 1)),
    ),
    (2, 0, 3): (
        ((6, 5, 4), (4, 5, 6), (4, 5, 6), (4, 5, 6)),
        ((7, 6, 5), (5, 6, 7), (5, 6, 7), (5, 6, 7)),
        ((0, 7, 6), (6, 7, 0), (6, 7, 0), (6, 7, 0)),
        ((1, 0, 7), (7, 0, 1), (7, 0, 1), (7, 0, 1)),
    ),
    (2, 0, 2): (
        ((3, 6, 5), (1, 6, 5), (1, 6, 5), (2, 6, 5)),
        ((0, 7, 6), (2, 7, 6), (2, 7, 6), (4, 7, 6)),
        ((1, 0, 7), (7, 4, 0), (3, 0, 7), (7, 5, 0)),
        ((2, 1, 0), (0, 1), (0, 1), (1, 0)),
    ),
    (2, 1, 3): (
        ((5, 4, 6), (4, 5, 6), (6, 5, 4), (4, 5, 6)),
        ((6, 7, 5), (5, 6, 7), (5, 6, 7), (7, 6, 5)),
        ((7, 6, 0), (6, 7, 0), (0, 7, 6), (6, 7, 0)),
        ((0, 1, 7), (7, 0, 1), (7, 0, 1), (1, 0, 7)),
    ),
    (2, 1, 2): (
        ((1, 4, 5), (4, 5), (1, 5, 4), (4, 5)),
        ((2, 5, 6), (5, 6), (2, 6, 5), (5, 6)),
        ((7, 6), (6, 7), (3, 7, 6), (6, 7)),
        ((0, 7), (7, 0), (0, 4, 7), (7, 4, 0)),
    ),
    (3, 0, 3): (
        ((4, 5, 3), (3, 4, 5), (5, 4, 3), (3, 4, 5)),
        ((5, 4, 6), (4, 5, 6), (4, 5, 6), (6, 5, 4)),
        ((6, 7, 5), (5, 6, 7), (7, 6, 5), (5, 6, 7)),
        ((7, 6, 0), (6, 7, 0), (6, 7, 0), (0, 7, 6)),
    ),
    (3, 0, 2): (
        ((4, 5), (5, 4), (1, 5, 4), (4, 5)),
        ((2, 6, 5), (6, 5), (2, 6, 5), (5, 6)),
        ((1, 7, 6), (7, 6), (3, 7, 6), (6, 7)),
        ((7, 0), (0, 7), (0, 4, 7), (7, 4, 0)),
    ),
    (3, 1, 3): (
        ((4, 5, 3), (5, 4, 3), (5, 4, 3), (3, 4, 5)),
        ((5, 4, 6), (6, 5, 4), (4, 5, 6), (6, 5, 4)),
        ((6, 7, 5), (7, 6, 5), (7, 6, 5), (5, 6, 7)),
        ((7, 6, 0), (0, 7, 6), (6, 7, 0), (0, 7, 6)),
    ),
    (3, 1, 2): (
        ((3, 7, 4), (3, 4), (3, 7, 4), (4, 7, 3)),
        ((0, 4, 5), (4, 5), (0, 4, 5), (5, 4)),
        ((1, 5, 6), (5, 6), (1, 5, 6), (6, 5)),
        ((2, 6, 7), (6, 7), (2, 6, 7), (7, 6)),
    ),
    (4, 0, 3): (
        ((3, 2, 4), (4, 3, 2), (4, 3, 2), (2, 3, 4)),
        ((4, 5, 3), (5, 4, 3), (3, 4, 5), (5, 4, 3)),
        ((6, 4, 5), (6, 5, 4), (6, 5, 4), (4, 5, 6)),
        ((5, 7, 6), (7, 6, 5), (5, 6, 7), (7, 6, 5)),
    ),
    (4, 0, 2): (
        ((3, 4), (4, 3), (3, 7, 4), (4, 7, 3)),
        ((4, 5), (5, 4), (0, 4, 5), (5, 4)),
        ((1, 6, 5), (6, 5), (1, 5, 6), (6, 5)),
        ((2, 7, 6), (7, 6), (2, 6, 7), (7, 6)),
    ),
    (4, 1, 3): (
        ((2, 3, 4), (4, 3, 2), (2, 3, 4), (4, 3, 2)),
        ((5, 4, 3), (3, 4, 5), (5, 4, 3), (5, 4, 3)),
        ((4, 5, 6), (6, 5, 4), (4, 5, 6), (6, 5, 4)),
        ((7, 6, 5), (5, 6, 7), (7, 6, 5), (7, 6, 5)),
    ),
    (4, 1, 2): (
        ((1, 2, 3), (3, 2), (3, 2), (2, 3)),
        ((2, 3, 4), (0, 3, 4), (4, 7, 3), (3, 0, 4)),
        ((3, 4, 5), (1, 4, 5), (1, 4, 5), (4, 5)),
        ((0, 5, 6), (2, 5, 6), (2, 5, 6), (1, 6, 5)),
    ),
    (5, 0, 3): (
        ((1, 2, 3), (1, 2, 3), (3, 2, 1), (1, 2, 3)),
        ((2, 3, 4), (4, 3, 2), (2, 3, 4), (4, 3, 2)),
        ((3, 4, 5), (3, 4, 5), (5, 4, 3), (3, 4, 5)),
        ((4, 5, 6), (6, 5, 4), (4, 5, 6), (6, 5, 4)),
    ),
    (5, 0, 2): (
        ((3, 2), (2, 3), (3, 2), (3, 2)),
        ((4, 3), (3, 0, 4), (4, 3), (0, 3, 4)),
        ((5, 4), (4, 5), (5, 4), (5, 4)),
        ((2, 5, 6), (1, 6, 5), (6, 5), (2, 5, 6)),
    ),
    (5, 1, 3): (
        ((3, 2, 1), (3, 2, 1), (1, 2, 3), (3, 2, 1)),
        ((4, 3, 2), (2, 3, 4), (2, 3, 4), (2, 3, 4)),
        ((5, 4, 3), (5, 4, 3), (3, 4, 5), (5, 4, 3)),
        ((6, 5, 4), (4, 5, 6), (4, 5, 6), (4, 5, 6)),
    ),
    (5, 1, 2): (
        ((3, 2, 1), (1, 2), (1, 2), (1, 2)),
        ((0, 3, 2), (2, 3), (0, 3, 2), (2, 3)),
        ((5, 4, 3), (3, 4), (3, 4), (3, 0, 4)),
        ((2, 5, 4), (0, 5, 4), (2, 5, 4), (4, 5)),
    ),
    (6, 0, 3): (
        ((3, 2, 1), (1, 2), (1, 2), (1, 2)),
        ((0, 3, 2), (2, 3), (2, 3), (2, 3)),
        ((5, 4, 3), (3, 4), (3, 4), (3, 0, 4)),
        ((2, 5, 4), (4, 5), (4, 5), (4, 5)),
    ),
    (6, 0, 2): (
        ((3, 2, 1), (3, 2, 1), (2, 1), (1, 2)),
        ((0, 3, 2), (5, 3, 2), (0, 2, 3), (2, 3)),
        ((1, 4, 3), (4, 0, 3), (1, 3, 4), (3, 4)),
        ((2, 5, 4), (2, 5, 4), (7, 4, 5), (4, 5)),
    ),
    (6, 1, 3): (
        ((3, 2, 1), (3, 2, 1), (3, 1, 2), (1, 2)),
        ((0, 3, 2), (0, 3, 2), (0, 2, 3), (2, 3)),
        ((1, 4, 3), (1, 4, 3), (6, 3, 4), (3, 4)),
        ((2, 5, 4), (2, 5, 4), (5, 4), (4, 5)),
    ),
    (6, 1, 2): (
        ((1,), (1,), (1,), (1,)),
        ((2,), (2,), (2,), (2,)),
        ((3,), (3,), (3,), (3,)),
        ((0, 4), (4,), (4,), (4,)),
    ),
    (7, 0, 3): (
        ((7, 3, 1), (7, 1), (7, 1), (7, 1)),
        ((4, 0, 2), (0, 2), (0, 2), (0, 2)),
        ((1, 5, 3), (1, 3), (1, 3), (1, 3)),
        ((2, 6, 4), (2, 4), (2, 4), (2, 4)),
    ),
    (7, 0, 2): (
        ((1,), (1,), (1,), (1,)),
        ((2,), (2,), (2,), (2,)),
        ((3,), (3,), (3,), (3,)),
        ((4,), (4,), (4,), (0, 4)),
    ),
    (7, 1, 3): (
        ((1, 5, 7), (1, 7), (1, 7), (1, 7)),
        ((6, 2, 0), (2, 0), (2, 0), (2, 0)),
        ((7, 3, 1), (3, 1), (3, 1), (3, 1)),
        ((4, 0, 2), (4, 2), (4, 2), (4, 2)),
    ),
    (7, 1, 2): (
        ((7,), (7,), (7,), (3, 7)),
        ((0,), (0,), (0,), (0,)),
        ((1,), (1,), (1,), (1,)),
        ((2,), (2,), (2,), (2,)),
    ),
}


def place(x, y, core, z, half):
    return (x % XS * 8 + y % YS * 2 + core) * 16 + z % ZS * 2 + half


def everywhere():
    for x in range(XS):
        for y in range(YS):
            for core in range(2):
                for z in range(ZS):
                    for half in range(2):
                        yield x, y, core, z, half


def weight_plan():
    moves = {}
    found = {}
    for (z, half, kept), by_y in ROUTES.items():
        core = half if kept == 3 else 1 - half
        for x in range(XS):
            for y in range(YS):
                for part in range(PARTS):
                    at = place(x, y, core, z, half)
                    for step, chip in zip(WHEN[part], by_y[y][part]):
                        to = place(x + chip // 4, chip % 4, core, z, half)
                        moves.setdefault((step, part), []).append((at, to))
                        found[to, part, x * 4 + y] = (step, part)
                        at = to
    keys = sorted(moves)
    table = np.zeros((256, PARTS, 3), np.int32)
    for x, y, core, z, half in everywhere():
        me = place(x, y, core, z, half)
        chip = 4 * x + y
        first = 2 if (half, core) == (1, 0) else 0
        second = 0 if (half, core) == (0, 1) else 2
        ends = (first, second) if core == 0 else (second, first)
        for part in range(PARTS):
            for slot, offset in enumerate((1,) + ends):
                source = (chip + z + offset) % 8
                if source != chip:
                    table[me, part, slot] = 1 + keys.index(found[me, part, source])
    return {key: moves[key] for key in keys}, table


def token_plan():
    start, shift, first, second, keep, send = [], [], [], [], [], []
    for x, y, core, z, half in everywhere():
        me = place(x, y, core, z, half)
        whole = (-4 * x - y - 1) % ZS
        whole -= ZS if whole > 4 or (whole == 4 and core) else 0
        some = {3: 2, 4: 2, 2: 1, 1: 1, 0: 0}[abs(whole)] * (1 if whole > 0 else -1)
        start.append((me, place(x, y, core, z + some, half)))
        shift.append((me, place(x, y, core, z + whole - some, half)))
        if core == half:
            first.append((me, place(x, y, core, z, 1 - half)))
        else:
            first.append((me, place(x, y, 1 - core, z, half)))
            second.append((me, place(x, y, 1 - core, z, 1 - half)))
        keep.append((place(x, y, core, z + (1 if half else -1), half), me))
        send.append((place(x, y, core, z + (-1 if core else 1), half), me))
    return start, shift, first, second, keep, send


def product_kernel(slots, last, rows, held_at, index, *refs):
    buffers = refs[: 1 + len(held_at)]
    tokens, out, held, sems = refs[1 + len(held_at) : -3 - last], refs[-3], refs[-2], refs[-1]
    jobs = [(part, side) for part in range(PARTS) for side in range(1 + last)]
    early = sum(step < ROUNDS - 1 for step, _ in held_at)

    def fetch(part, side, source):
        return pltpu.make_async_copy(source, held.at[side, part], sems.at[side, part])

    def own(part):
        return buffers[0].at[pl.ds(part * rows, rows)]

    def due(part, side):
        which = index[part * 3 + slots[side]]
        came_late = which > early
        if side:
            return which, which >= 0
        return which, came_late if last else jnp.logical_not(came_late)

    for part, side in jobs:
        which, wanted = due(part, side)
        if not last or side:

            @pl.when(which == 0)
            def _():
                fetch(part, side, own(part)).start()

        for number, (step, of) in enumerate(held_at, 1):
            if of == part and (side or last == (step == ROUNDS - 1)):

                @pl.when(which == number)
                def _():
                    fetch(part, side, buffers[number]).start()

    if not last:
        out[...] = jnp.zeros_like(out)
    width = out.shape[1]
    for part, side in jobs:

        @pl.when(due(part, side)[1])
        def _():
            fetch(part, side, own(part)).wait()
            for low in range(0, width, 256):
                high = min(low + 256, width)
                out[:, low:high] += jnp.dot(
                    tokens[side][:, part * rows : (part + 1) * rows],
                    held[side, part, :, low:high],
                    preferred_element_type=jnp.float32,
                )


def product(slots, index, own, got, mid, *more):
    last = bool(more)
    rows = own.shape[0] // PARTS
    held_at = sorted(key for key in got if last or key[0] < ROUNDS - 1)
    buffers = [own] + [got[key] for key in held_at]
    tokens, width = mid.shape[0], own.shape[1]
    anywhere = pl.BlockSpec(memory_space=pl.ANY)
    whole = pl.BlockSpec(memory_space=pltpu.VMEM)
    return pl.pallas_call(
        functools.partial(product_kernel, slots, last, rows, held_at),
        out_shape=jax.ShapeDtypeStruct((tokens, width), jnp.float32),
        in_specs=[pl.BlockSpec(memory_space=pltpu.SMEM)] + [anywhere] * len(buffers) + [whole] * (1 + len(more)),
        out_specs=whole,
        input_output_aliases={len(buffers) + 3: 0} if last else {},
        scratch_shapes=[
            pltpu.VMEM((1 + last, PARTS, rows, width), jnp.bfloat16),
            pltpu.SemaphoreType.DMA((1 + last, PARTS)),
        ],
        compiler_params=pltpu.CompilerParams(vmem_limit_bytes=40 * 2**20),
        cost_estimate=pl.CostEstimate(
            flops=2 * tokens * own.shape[0] * width,
            bytes_accessed=2 * own.shape[0] * width + 8 * tokens * width,
            transcendentals=0,
        ),
    )(index, *buffers, mid, *more)


def on_device(tokens, gate_weight):
    me = lax.axis_index("row") * 16 + lax.axis_index("col")
    core = lax.axis_index("row") % 2
    half = lax.axis_index("col") % 2
    moves, table = weight_plan()
    index = lax.dynamic_index_in_dim(jnp.asarray(table.reshape(256, -1)), me, 0, keepdims=False)
    rows = gate_weight.shape[0] // PARTS
    parts = [gate_weight[part * rows : (part + 1) * rows] for part in range(PARTS)]

    start, shift, first, second, near_keep, near_send = token_plan()

    def after(value, *others):
        return lax.optimization_barrier((value,) + others)[0]

    def send(value, pairs):
        return lax.ppermute(value, BOTH, pairs)

    got = {}

    def weights(step, part, *others):
        hop = WHEN[part].index(step)
        value = got[WHEN[part][hop - 1], part] if hop else parts[part]
        got[step, part] = send(after(value, *others) if others else value, moves[step, part])
        return got[step, part]

    def product_of(slots, *operands):
        return product(slots, index, gate_weight, *operands)

    shifted = send(tokens, start)
    parts = [after(value, tokens) for value in parts]
    a, b, c = weights(0, 0), weights(0, 1), weights(0, 2)
    a, b, c, shifted = weights(1, 0), weights(1, 1), weights(1, 3, c, shifted), send(after(shifted, a), shift)
    crossed, also = send(after(shifted, a), first), send(after(shifted, b), second)
    a, b, c = weights(2, 0), weights(2, 2, b), weights(2, 3, shifted)
    keep_mid = jnp.where(core == half, shifted, crossed)
    send_mid = jnp.where(core == half, crossed, also)
    keep_end, send_end = send(keep_mid, near_keep), send(send_mid, near_send)
    a, b, c = weights(3, 1, a, crossed, also), weights(3, 2), weights(3, 3)
    early = {key: value for key, value in got.items() if key[0] < ROUNDS - 1}
    sent = product_of((0, 2), early, send_mid)
    kept = product_of((0, 1), early, keep_mid)
    keep_end, send_end, sent, kept = lax.optimization_barrier((keep_end, send_end, sent, kept))
    sent = product_of((0, 2), got, send_mid, send_end, sent)
    swap = [(place(x, y, c, z, h), place(x, y, 1 - c, z, h)) for x, y, c, z, h in everywhere()]
    arrived = send(sent, swap)
    kept = product_of((0, 1), got, keep_mid, keep_end, kept)
    return kept + arrived

def solution(mesh):
    placed = (P("row", "col"), P("row", "col"))
    return jax.shard_map(
        on_device, mesh=mesh, in_specs=placed, out_specs=P("row", "col"), check_vma=False
    )
```

time: 184 us -> 175 us (0.951)
  the two profiles are of different devices: /device:TPU:108 before, /device:TPU:73 now
where the time goes in v3:
time: 175 us; the launch traced here: 174 us
  starting transfers between devices  80.5 us (46%)
  waiting for transfers between devices  61 us (35%)
  Pallas kernels  18.7 us (11%)
  local copies, waits for them, and re-layouts  9.25 us (5%)
  other arithmetic  4.46 us (3%)
    ppermute x19, starting transfers between devices, send(): return lax.ppermute(value, BOTH, pairs)  80.5 us
    ppermute x19, waiting for transfers between devices, send(): return lax.ppermute(value, BOTH, pairs)  61 us
    pallas_call x4, Pallas kernels, product(): pl.pallas_call(functools.partial(product_kernel, slots, last, rows, held_...  18.7 us
    unnamed x18, local copies, waits for them, and re-layouts  6.31 us
  transfers between devices with their start and end apart: 19, of which 6 were waited for; matrix products, arithmetic and copies ran while one was open for 2% of the time, Pallas kernels for 7%

profile of v3, /device:TPU:73, one launch (start us, length us, event | category | flops | bytes accessed | tf_op | source)
XLA Modules:
  0.0 174.2 jit_solution(7442831429581296854)
XLA Ops:
  0.0 2.2 %fusion = (bf16[256,1664]{1,0:T(8,128)(2,1)S(1)}, bf16[256,1664]{1,0:T(8,128)(2,1)S(1)}, bf16[256,1664]{1,0:T(8,128)(2,1)S(1)}, bf16[256,1664]{1,0:T(8,128)(2,1)S(1)}) fusion(bf16[1024,1664]{1,0:T(8,128)(2,1)} %refs_0_.7), kind=kLoop, calls=%fused_computation.3 | loop fusion | bytes 6815744 | tf_op jit(solution)/shard_map/slice | solution.py:360
  2.5 1.3 collective-permute-start.1
  3.8 2.2 %collective-permute-start.2 = (bf16[256,1664]{1,0:T(8,128)(2,1)S(1)}, bf16[256,1664]{1,0:T(8,128)(2,1)}, u32[]{:S(2)}, u32[]{:S(2)}) collective-permute-start(bf16[256,1664]{1,0:T(8,128)(2,1)S(1)} %get-tuple-element.22), channel_id=1, source_target_pairs={{0,192},{32,160},{64,96},{96,0},{128,64},{160,32},{192,224},{224,1... | collective-permute-start | bytes 2555912 | tf_op jit(solution)/shard_map/ppermute | solution.py:368
  6.0 1.9 %collective-permute-start.5 = (bf16[384,1024]{1,0:T(8,128)(2,1)S(1)}, bf16[384,1024]{1,0:T(8,128)(2,1)S(1)}, u32[]{:S(2)}, u32[]{:S(2)}) collective-permute-start(bf16[384,1024]{1,0:T(8,128)(2,1)S(1)} %copy-done.8), channel_id=1, source_target_pairs={{0,14},{1,15},{2,0},{3,1},{4,2},{5,3},{6,4},{7,5},{8,6},{9,7},{10,... | collective-permute-start | bytes 2359304 | tf_op jit(solution)/shard_map/ppermute | solution.py:368
  8.0 13.3 %collective-permute-done.refs_1_ = bf16[256,1664]{1,0:T(8,128)(2,1)S(1)} collective-permute-done((bf16[256,1664]{1,0:T(8,128)(2,1)S(1)}, bf16[256,1664]{1,0:T(8,128)(2,1)S(1)}, u32[]{:S(2)}, u32[]{:S(2)}) %collective-permute-start) | collective-permute-done | bytes 852000 | tf_op jit(solution)/shard_map/ppermute | solution.py:368
  21.3 4.6 %collective-permute-start.3 = (bf16[256,1664]{1,0:T(8,128)(2,1)S(1)}, bf16[256,1664]{1,0:T(8,128)(2,1)}, u32[]{:S(2)}, u32[]{:S(2)}) collective-permute-start(bf16[256,1664]{1,0:T(8,128)(2,1)S(1)} %collective-permute-done.refs_1_), channel_id=1, source_target_pairs={{32,192},{64,224},{96,0},{0,32},{160,64},{192,96},{224,128},{128,1... | collective-permute-start | bytes 2555912 | tf_op jit(solution)/shard_map/ppermute | solution.py:368
  26.8 1.9 %collective-permute-start.4 = (bf16[256,1664]{1,0:T(8,128)(2,1)S(1)}, bf16[256,1664]{1,0:T(8,128)(2,1)S(1)}, u32[]{:S(2)}, u32[]{:S(2)}) collective-permute-start(bf16[256,1664]{1,0:T(8,128)(2,1)S(1)} %collective-permute-done.1.refs_2_), channel_id=1, source_target_pairs={{32,192},{64,224},{96,0},{0,32},{160,64},{192,96},{224,128},{128,1... | collective-permute-start | bytes 2555912 | tf_op jit(solution)/shard_map/ppermute | solution.py:368
  29.7 4.3 %collective-permute-done.2.refs_3_ = bf16[256,1664]{1,0:T(8,128)(2,1)} collective-permute-done((bf16[256,1664]{1,0:T(8,128)(2,1)S(1)}, bf16[256,1664]{1,0:T(8,128)(2,1)}, u32[]{:S(2)}, u32[]{:S(2)}) %collective-permute-start.2) | collective-permute-done | bytes 852000 | tf_op jit(solution)/shard_map/ppermute | solution.py:368
  34.0 12.4 %collective-permute-start.6 = (bf16[256,1664]{1,0:T(8,128)(2,1)S(1)}, bf16[256,1664]{1,0:T(8,128)(2,1)}, u32[]{:S(2)}, u32[]{:S(2)}) collective-permute-start(bf16[256,1664]{1,0:T(8,128)(2,1)S(1)} %get-tuple-element.24), channel_id=1, source_target_pairs={{0,224},{32,0},{64,32},{96,64},{128,96},{160,128},{192,160},{224,1... | collective-permute-start | bytes 2555912 | tf_op jit(solution)/shard_map/ppermute | solution.py:368
  46.4 4.8 %collective-permute-start.9 = (bf16[384,1024]{1,0:T(8,128)(2,1)S(1)}, bf16[384,1024]{1,0:T(8,128)(2,1)}, u32[]{:S(2)}, u32[]{:S(2)}) collective-permute-start(bf16[384,1024]{1,0:T(8,128)(2,1)S(1)} %collective-permute-done.5), channel_id=1, source_target_pairs={{0,0},{1,1},{2,2},{3,3},{4,4},{5,5},{6,6},{7,7},{8,8},{9,9},{10,10... | collective-permute-start | bytes 2359304 | tf_op jit(solution)/shard_map/ppermute | solution.py:368
  52.2 5.3 %collective-permute-start.7 = (bf16[256,1664]{1,0:T(8,128)(2,1)}, bf16[256,1664]{1,0:T(8,128)(2,1)}, u32[]{:S(2)}, u32[]{:S(2)}) collective-permute-start(bf16[256,1664]{1,0:T(8,128)(2,1)} %collective-permute-done.3.refs_4_), channel_id=1, source_target_pairs={{192,224},{224,0},{0,32},{32,64},{64,96},{96,128},{128,160},{160,1... | collective-permute-start | bytes 2555912 | tf_op jit(solution)/shard_map/ppermute | solution.py:368
  57.5 8.6 %collective-permute-done.9 = bf16[384,1024]{1,0:T(8,128)(2,1)} collective-permute-done((bf16[384,1024]{1,0:T(8,128)(2,1)S(1)}, bf16[384,1024]{1,0:T(8,128)(2,1)}, u32[]{:S(2)}, u32[]{:S(2)}) %collective-permute-start.9) | collective-permute-done | bytes 786464 | tf_op jit(solution)/shard_map/ppermute | solution.py:368
  66.1 1.9 %collective-permute-start.10 = (bf16[256,1664]{1,0:T(8,128)(2,1)}, bf16[256,1664]{1,0:T(8,128)(2,1)}, u32[]{:S(2)}, u32[]{:S(2)}) collective-permute-start(bf16[256,1664]{1,0:T(8,128)(2,1)} %collective-permute-done.6.refs_6_), channel_id=1, source_target_pairs={{224,192},{0,224},{32,0},{64,32},{96,64},{128,96},{160,128},{192,1... | collective-permute-start | bytes 2555912 | tf_op jit(solution)/shard_map/ppermute | solution.py:368
  68.1 4.8 %collective-permute-start.8 = (bf16[256,1664]{1,0:T(8,128)(2,1)}, bf16[256,1664]{1,0:T(8,128)(2,1)}, u32[]{:S(2)}, u32[]{:S(2)}) collective-permute-start(bf16[256,1664]{1,0:T(8,128)(2,1)} %collective-permute-done.2.refs_3_), channel_id=1, source_target_pairs={{192,224},{160,0},{96,32},{0,64},{64,96},{32,128},{224,160},{128,1... | collective-permute-start | bytes 2555912 | tf_op jit(solution)/shard_map/ppermute | solution.py:368
  72.8 9.4 %collective-permute-start.11 = (bf16[384,1024]{1,0:T(8,128)(2,1)}, bf16[384,1024]{1,0:T(8,128)(2,1)}, u32[]{:S(2)}, u32[]{:S(2)}) collective-permute-start(bf16[384,1024]{1,0:T(8,128)(2,1)} %collective-permute-done.9), channel_id=1, source_target_pairs={{0,1},{1,17},{2,3},{3,19},{4,5},{5,21},{6,7},{7,23},{8,9},{9,25},{... | collective-permute-start | bytes 2359304 | tf_op jit(solution)/shard_map/ppermute | solution.py:368
  82.3 6.4 %collective-permute-start.12 = (bf16[384,1024]{1,0:T(8,128)(2,1)}, bf16[384,1024]{1,0:T(8,128)(2,1)}, u32[]{:S(2)}, u32[]{:S(2)}) collective-permute-start(bf16[384,1024]{1,0:T(8,128)(2,1)} %collective-permute-done.9), channel_id=1, source_target_pairs={{1,16},{3,18},{5,20},{7,22},{9,24},{11,26},{13,28},{15,30},{16,1},... | collective-permute-start | bytes 2359304 | tf_op jit(solution)/shard_map/ppermute | solution.py:368
  88.7 19.5 %collective-permute-done.11 = bf16[384,1024]{1,0:T(8,128)(2,1)} collective-permute-done((bf16[384,1024]{1,0:T(8,128)(2,1)}, bf16[384,1024]{1,0:T(8,128)(2,1)}, u32[]{:S(2)}, u32[]{:S(2)}) %collective-permute-start.11) | collective-permute-done | bytes 786464 | tf_op jit(solution)/shard_map/ppermute | solution.py:368
  108.2 6.9 %collective-permute-done.12 = bf16[384,1024]{1,0:T(8,128)(2,1)} collective-permute-done((bf16[384,1024]{1,0:T(8,128)(2,1)}, bf16[384,1024]{1,0:T(8,128)(2,1)}, u32[]{:S(2)}, u32[]{:S(2)}) %collective-permute-start.12) | collective-permute-done | bytes 786464 | tf_op jit(solution)/shard_map/ppermute | solution.py:368
  115.1 1.3 collective-permute-start.13
  116.4 11.0 %collective-permute-start.15 = (bf16[256,1664]{1,0:T(8,128)(2,1)}, bf16[256,1664]{1,0:T(8,128)(2,1)}, u32[]{:S(2)}, u32[]{:S(2)}) collective-permute-start(bf16[256,1664]{1,0:T(8,128)(2,1)} %collective-permute-done.10.refs_9_), channel_id=1, source_target_pairs={{194,162},{226,2},{2,226},{34,66},{66,34},{98,130},{130,98},{162,1... | collective-permute-start | bytes 2555912 | tf_op jit(solution)/shard_map/ppermute | solution.py:368
  127.5 1.3 collective-permute-start.14
  128.8 2.7 %broadcast_select_fusion = (bf16[384,1024]{1,0:T(8,128)(2,1)}, bf16[384,1024]{1,0:T(8,128)(2,1)}) fusion(bf16[384,1024]{1,0:T(8,128)(2,1)} %collective-permute-done.11, bf16[384,1024]{1,0:T(8,128)(2,1)} %collective-permute-done.12, pred[]{:T(512)S(6)} %eq.7, bf16[384,1024]{1,0:T(8,128)(2,1)} %collective-permute-done.9), kind=kLoop, calls=%fused_computation | loop fusion | flops 786432 | bytes 3932161 | tf_op jit(solution)/shard_map/jit(_where)/select_n | solution.py:388
  131.4 9.5 %collective-permute-start.16 = (bf16[384,1024]{1,0:T(8,128)(2,1)}, bf16[384,1024]{1,0:T(8,128)(2,1)}, u32[]{:S(2)}, u32[]{:S(2)}) collective-permute-start(bf16[384,1024]{1,0:T(8,128)(2,1)} %get-tuple-element.40.refs_10_.refs_13_), channel_id=1, source_target_pairs={{14,0},{3,1},{0,2},{5,3},{2,4},{7,5},{4,6},{9,7},{6,8},{11,9},{8,1... | collective-permute-start | bytes 2359304 | tf_op jit(solution)/shard_map/ppermute | solution.py:368
  141.7 1.2 copy-done.2
  142.8 1.2 copy-done.4
  144.0 1.2 copy-done.6
  145.1 2.9 %shard_map.37.refs_15_ = f32[384,1664]{1,0:T(8,128)S(1)} custom-call(s32[12]{0:T(128)S(1)} %dynamic-slice_bitcast_fusion.index, bf16[1024,1664]{1,0:T(8,128)(2,1)S(1)} %copy-done, bf16[256,1664]{1,0:T(8,128)(2,1)S(1)} %copy-done.2, bf16[256,1664]{1,0:T(8,128)(2,1)S(1)} %copy-done.4, bf16[256,1664]{1,0:T(8,128)(2,1)} %collective-permute-done.2.refs_3_, ...), custom_call_target="tpu_custom_call" | custom-call | flops 1308622848 | bytes 8519680 | tf_op jit(solution)/shard_map/pallas_call | solution.py:334
  148.0 3.0 %shard_map.38.refs_15_ = f32[384,1664]{1,0:T(8,128)S(1)} custom-call(s32[12]{0:T(128)S(1)} %dynamic-slice_bitcast_fusion.index, bf16[1024,1664]{1,0:T(8,128)(2,1)S(1)} %copy-done, bf16[256,1664]{1,0:T(8,128)(2,1)S(1)} %copy-done.2, bf16[256,1664]{1,0:T(8,128)(2,1)S(1)} %copy-done.4, bf16[256,1664]{1,0:T(8,128)(2,1)} %collective-permute-done.2.refs_3_, ...), custom_call_target="tpu_custom_call" | custom-call | flops 1308622848 | bytes 8519680 | tf_op jit(solution)/shard_map/pallas_call | solution.py:334
  151.0 8.4 %collective-permute-done.16.refs_14_ = bf16[384,1024]{1,0:T(8,128)(2,1)} collective-permute-done((bf16[384,1024]{1,0:T(8,128)(2,1)}, bf16[384,1024]{1,0:T(8,128)(2,1)}, u32[]{:S(2)}, u32[]{:S(2)}) %collective-permute-start.16) | collective-permute-done | bytes 786464 | tf_op jit(solution)/shard_map/ppermute | solution.py:368
  159.4 6.4 %shard_map.40 = f32[384,1664]{1,0:T(8,128)S(1)} custom-call(s32[12]{0:T(128)S(1)} %dynamic-slice_bitcast_fusion.index, bf16[1024,1664]{1,0:T(8,128)(2,1)} %refs_0_.7, bf16[256,1664]{1,0:T(8,128)(2,1)S(1)} %copy-done.2, bf16[256,1664]{1,0:T(8,128)(2,1)S(1)} %copy-done.4, ...), custom_call_target="tpu_custom_call", output_to_operand_aliasing={{}: (16, {})} | custom-call | flops 1308622848 | bytes 8519680 | tf_op jit(solution)/shard_map/pallas_call | solution.py:334
  166.0 6.4 %shard_map.39 = f32[384,1664]{1,0:T(8,128)S(1)} custom-call(s32[12]{0:T(128)S(1)} %dynamic-slice_bitcast_fusion.index, bf16[1024,1664]{1,0:T(8,128)(2,1)} %refs_0_.7, bf16[256,1664]{1,0:T(8,128)(2,1)S(1)} %copy-done.2, bf16[256,1664]{1,0:T(8,128)(2,1)S(1)} %copy-done.4, ...), custom_call_target="tpu_custom_call", output_to_operand_aliasing={{}: (16, {})} | custom-call | flops 1308622848 | bytes 8519680 | tf_op jit(solution)/shard_map/pallas_call | solution.py:334
  172.4 1.8 %add.21 = f32[384,1664]{1,0:T(8,128)} add(f32[384,1664]{1,0:T(8,128)S(1)} %shard_map.39, f32[384,1664]{1,0:T(8,128)S(1)} %collective-permute-done.18) | non-fusion elementwise | flops 638976 | bytes 7667712 | tf_op jit(solution)/shard_map/add | solution.py:399
  (32 shorter events, 3.9 us)
Async XLA Ops:
  0.0 6.0 %copy-start.8 = (bf16[384,1024]{1,0:T(8,128)(2,1)S(1)}, bf16[384,1024]{1,0:T(8,128)(2,1)}, u32[]{:S(2)}) copy-start(bf16[384,1024]{1,0:T(8,128)(2,1)} %param.3) | copy-start | bytes 2359300
  2.3 139.4 %copy-start = (bf16[1024,1664]{1,0:T(8,128)(2,1)S(1)}, bf16[1024,1664]{1,0:T(8,128)(2,1)}, u32[]{:S(2)}) copy-start(bf16[1024,1664]{1,0:T(8,128)(2,1)} %refs_0_.7) | copy-start | bytes 10223620
  2.3 19.0 %collective-permute-start = (bf16[256,1664]{1,0:T(8,128)(2,1)S(1)}, bf16[256,1664]{1,0:T(8,128)(2,1)S(1)}, u32[]{:S(2)}, u32[]{:S(2)}) collective-permute-start(bf16[256,1664]{1,0:T(8,128)(2,1)S(1)} %get-tuple-element.20), channel_id=1, source_target_pairs={{0,32},{32,64},{64,96},{96,0},{128,160},{160,192},{192,224},{224,1... | collective-permute-start | bytes 2555912 | tf_op jit(solution)/shard_map/ppermute | solution.py:368
  2.5 24.3 %collective-permute-start.1 = (bf16[256,1664]{1,0:T(8,128)(2,1)S(1)}, bf16[256,1664]{1,0:T(8,128)(2,1)S(1)}, u32[]{:S(2)}, u32[]{:S(2)}) collective-permute-start(bf16[256,1664]{1,0:T(8,128)(2,1)S(1)} %get-tuple-element.21), channel_id=1, source_target_pairs={{0,32},{32,64},{64,96},{96,0},{128,160},{160,192},{192,224},{224,1... | collective-permute-start | bytes 2555912 | tf_op jit(solution)/shard_map/ppermute | solution.py:368
  3.8 30.2 %collective-permute-start.2 = (bf16[256,1664]{1,0:T(8,128)(2,1)S(1)}, bf16[256,1664]{1,0:T(8,128)(2,1)}, u32[]{:S(2)}, u32[]{:S(2)}) collective-permute-start(bf16[256,1664]{1,0:T(8,128)(2,1)S(1)} %get-tuple-element.22), channel_id=1, source_target_pairs={{0,192},{32,160},{64,96},{96,0},{128,64},{160,32},{192,224},{224,1... | collective-permute-start | bytes 2555912 | tf_op jit(solution)/shard_map/ppermute | solution.py:368
  6.0 23.7 %collective-permute-start.5 = (bf16[384,1024]{1,0:T(8,128)(2,1)S(1)}, bf16[384,1024]{1,0:T(8,128)(2,1)S(1)}, u32[]{:S(2)}, u32[]{:S(2)}) collective-permute-start(bf16[384,1024]{1,0:T(8,128)(2,1)S(1)} %copy-done.8), channel_id=1, source_target_pairs={{0,14},{1,15},{2,0},{3,1},{4,2},{5,3},{6,4},{7,5},{8,6},{9,7},{10,... | collective-permute-start | bytes 2359304 | tf_op jit(solution)/shard_map/ppermute | solution.py:368
  21.3 29.9 %collective-permute-start.3 = (bf16[256,1664]{1,0:T(8,128)(2,1)S(1)}, bf16[256,1664]{1,0:T(8,128)(2,1)}, u32[]{:S(2)}, u32[]{:S(2)}) collective-permute-start(bf16[256,1664]{1,0:T(8,128)(2,1)S(1)} %collective-permute-done.refs_1_), channel_id=1, source_target_pairs={{32,192},{64,224},{96,0},{0,32},{160,64},{192,96},{224,128},{128,1... | collective-permute-start | bytes 2555912 | tf_op jit(solution)/shard_map/ppermute | solution.py:368
  25.9 0.9 copy-start.1
  26.8 24.4 %collective-permute-start.4 = (bf16[256,1664]{1,0:T(8,128)(2,1)S(1)}, bf16[256,1664]{1,0:T(8,128)(2,1)S(1)}, u32[]{:S(2)}, u32[]{:S(2)}) collective-permute-start(bf16[256,1664]{1,0:T(8,128)(2,1)S(1)} %collective-permute-done.1.refs_2_), channel_id=1, source_target_pairs={{32,192},{64,224},{96,0},{0,32},{160,64},{192,96},{224,128},{128,1... | collective-permute-start | bytes 2555912 | tf_op jit(solution)/shard_map/ppermute | solution.py:368
  28.7 1.0 copy-start.3
  34.0 32.2 %collective-permute-start.6 = (bf16[256,1664]{1,0:T(8,128)(2,1)S(1)}, bf16[256,1664]{1,0:T(8,128)(2,1)}, u32[]{:S(2)}, u32[]{:S(2)}) collective-permute-start(bf16[256,1664]{1,0:T(8,128)(2,1)S(1)} %get-tuple-element.24), channel_id=1, source_target_pairs={{0,224},{32,0},{64,32},{96,64},{128,96},{160,128},{192,160},{224,1... | collective-permute-start | bytes 2555912 | tf_op jit(solution)/shard_map/ppermute | solution.py:368
  46.4 19.7 %collective-permute-start.9 = (bf16[384,1024]{1,0:T(8,128)(2,1)S(1)}, bf16[384,1024]{1,0:T(8,128)(2,1)}, u32[]{:S(2)}, u32[]{:S(2)}) collective-permute-start(bf16[384,1024]{1,0:T(8,128)(2,1)S(1)} %collective-permute-done.5), channel_id=1, source_target_pairs={{0,0},{1,1},{2,2},{3,3},{4,4},{5,5},{6,6},{7,7},{8,8},{9,9},{10,10... | collective-permute-start | bytes 2359304 | tf_op jit(solution)/shard_map/ppermute | solution.py:368
  51.2 1.0 copy-start.5
  52.2 63.0 %collective-permute-start.7 = (bf16[256,1664]{1,0:T(8,128)(2,1)}, bf16[256,1664]{1,0:T(8,128)(2,1)}, u32[]{:S(2)}, u32[]{:S(2)}) collective-permute-start(bf16[256,1664]{1,0:T(8,128)(2,1)} %collective-permute-done.3.refs_4_), channel_id=1, source_target_pairs={{192,224},{224,0},{0,32},{32,64},{64,96},{96,128},{128,160},{160,1... | collective-permute-start | bytes 2555912 | tf_op jit(solution)/shard_map/ppermute | solution.py:368
  66.1 50.3 %collective-permute-start.10 = (bf16[256,1664]{1,0:T(8,128)(2,1)}, bf16[256,1664]{1,0:T(8,128)(2,1)}, u32[]{:S(2)}, u32[]{:S(2)}) collective-permute-start(bf16[256,1664]{1,0:T(8,128)(2,1)} %collective-permute-done.6.refs_6_), channel_id=1, source_target_pairs={{224,192},{0,224},{32,0},{64,32},{96,64},{128,96},{160,128},{192,1... | collective-permute-start | bytes 2555912 | tf_op jit(solution)/shard_map/ppermute | solution.py:368
  68.1 59.4 %collective-permute-start.8 = (bf16[256,1664]{1,0:T(8,128)(2,1)}, bf16[256,1664]{1,0:T(8,128)(2,1)}, u32[]{:S(2)}, u32[]{:S(2)}) collective-permute-start(bf16[256,1664]{1,0:T(8,128)(2,1)} %collective-permute-done.2.refs_3_), channel_id=1, source_target_pairs={{192,224},{160,0},{96,32},{0,64},{64,96},{32,128},{224,160},{128,1... | collective-permute-start | bytes 2555912 | tf_op jit(solution)/shard_map/ppermute | solution.py:368
  72.8 35.4 %collective-permute-start.11 = (bf16[384,1024]{1,0:T(8,128)(2,1)}, bf16[384,1024]{1,0:T(8,128)(2,1)}, u32[]{:S(2)}, u32[]{:S(2)}) collective-permute-start(bf16[384,1024]{1,0:T(8,128)(2,1)} %collective-permute-done.9), channel_id=1, source_target_pairs={{0,1},{1,17},{2,3},{3,19},{4,5},{5,21},{6,7},{7,23},{8,9},{9,25},{... | collective-permute-start | bytes 2359304 | tf_op jit(solution)/shard_map/ppermute | solution.py:368
  82.3 32.9 %collective-permute-start.12 = (bf16[384,1024]{1,0:T(8,128)(2,1)}, bf16[384,1024]{1,0:T(8,128)(2,1)}, u32[]{:S(2)}, u32[]{:S(2)}) collective-permute-start(bf16[384,1024]{1,0:T(8,128)(2,1)} %collective-permute-done.9), channel_id=1, source_target_pairs={{1,16},{3,18},{5,20},{7,22},{9,24},{11,26},{13,28},{15,30},{16,1},... | collective-permute-start | bytes 2359304 | tf_op jit(solution)/shard_map/ppermute | solution.py:368
  115.1 44.3 %collective-permute-start.13 = (bf16[256,1664]{1,0:T(8,128)(2,1)}, bf16[256,1664]{1,0:T(8,128)(2,1)}, u32[]{:S(2)}, u32[]{:S(2)}) collective-permute-start(bf16[256,1664]{1,0:T(8,128)(2,1)} %copy-done.5), channel_id=1, source_target_pairs={{192,224},{224,0},{0,32},{32,64},{64,96},{96,128},{128,160},{160,1... | collective-permute-start | bytes 2555912 | tf_op jit(solution)/shard_map/ppermute | solution.py:368
  116.4 43.0 %collective-permute-start.15 = (bf16[256,1664]{1,0:T(8,128)(2,1)}, bf16[256,1664]{1,0:T(8,128)(2,1)}, u32[]{:S(2)}, u32[]{:S(2)}) collective-permute-start(bf16[256,1664]{1,0:T(8,128)(2,1)} %collective-permute-done.10.refs_9_), channel_id=1, source_target_pairs={{194,162},{226,2},{2,226},{34,66},{66,34},{98,130},{130,98},{162,1... | collective-permute-start | bytes 2555912 | tf_op jit(solution)/shard_map/ppermute | solution.py:368
  127.5 32.0 %collective-permute-start.14 = (bf16[256,1664]{1,0:T(8,128)(2,1)}, bf16[256,1664]{1,0:T(8,128)(2,1)}, u32[]{:S(2)}, u32[]{:S(2)}) collective-permute-start(bf16[256,1664]{1,0:T(8,128)(2,1)} %collective-permute-done.8.refs_8_), channel_id=1, source_target_pairs={{0,224},{32,0},{64,32},{128,96},{160,128},{192,160},{113,241},{241... | collective-permute-start | bytes 2555912 | tf_op jit(solution)/shard_map/ppermute | solution.py:368
  131.4 19.6 %collective-permute-start.17 = (bf16[384,1024]{1,0:T(8,128)(2,1)}, bf16[384,1024]{1,0:T(8,128)(2,1)}, u32[]{:S(2)}, u32[]{:S(2)}) collective-permute-start(bf16[384,1024]{1,0:T(8,128)(2,1)} %get-tuple-element.39.refs_10_.refs_13_), channel_id=1, source_target_pairs={{2,0},{3,1},{4,2},{5,3},{6,4},{7,5},{8,6},{9,7},{10,8},{11,9},{12,... | collective-permute-start | bytes 2359304 | tf_op jit(solution)/shard_map/ppermute | solution.py:368
  131.4 28.0 %collective-permute-start.16 = (bf16[384,1024]{1,0:T(8,128)(2,1)}, bf16[384,1024]{1,0:T(8,128)(2,1)}, u32[]{:S(2)}, u32[]{:S(2)}) collective-permute-start(bf16[384,1024]{1,0:T(8,128)(2,1)} %get-tuple-element.40.refs_10_.refs_13_), channel_id=1, source_target_pairs={{14,0},{3,1},{0,2},{5,3},{2,4},{7,5},{4,6},{9,7},{6,8},{11,9},{8,1... | collective-permute-start | bytes 2359304 | tf_op jit(solution)/shard_map/ppermute | solution.py:368
  141.7 1.2 copy-start.2
  142.8 1.2 copy-start.4
  144.0 1.2 copy-start.6
  148.0 11.4 %copy-start.7 = (bf16[256,1664]{1,0:T(8,128)(2,1)S(1)}, bf16[256,1664]{1,0:T(8,128)(2,1)}, u32[]{:S(2)}) copy-start(bf16[256,1664]{1,0:T(8,128)(2,1)} %copy-done.5) | copy-start | bytes 2555908
  165.9 6.5 %collective-permute-start.18 = (f32[384,1664]{1,0:T(8,128)S(1)}, f32[384,1664]{1,0:T(8,128)S(1)}, u32[]{:S(2)}, u32[]{:S(2)}) collective-permute-start(f32[384,1664]{1,0:T(8,128)S(1)} %shard_map.40), channel_id=1, source_target_pairs={{0,16},{1,17},{2,18},{3,19},{4,20},{5,21},{6,22},{7,23},{8,24},{9,... | collective-permute-start | bytes 7667720 | tf_op jit(solution)/shard_map/ppermute | solution.py:368

commit v4 on v3

--- a/solution.py
+++ b/solution.py
@@ -11,6 +11,7 @@
 XS, YS, ZS = 2, 4, 8
 BOTH = ("row", "col")
 ROUNDS = 4
+SPARE = 0
 PARTS = 4
 WHEN = ((0, 1, 2), (0, 1, 3), (0, 2, 3), (1, 2, 3))
 
@@ -40,15 +41,15 @@
         ((0, 1, 2), (2, 1), (1, 2), (2, 1)),
     ),
     (1, 0, 3): (
-        ((5, 6, 7), (7, 6, 5), (7, 6, 5), (7, 6, 5)),
+        ((5, 6, 7), (5, 6, 7), (7, 6, 5), (7, 6, 5)),
         ((6, 7, 0), (6, 7, 0), (0, 7, 6), (6, 7, 0)),
-        ((7, 0, 1), (1, 0, 7), (1, 0, 7), (1, 0, 7)),
+        ((7, 0, 1), (7, 0, 1), (1, 0, 7), (1, 0, 7)),
         ((0, 1, 2), (0, 1, 2), (2, 1, 0), (0, 1, 2)),
     ),
     (1, 0, 2): (
-        ((3, 6, 7), (1, 6, 7), (1, 6, 7), (7, 6)),
-        ((2, 7, 0), (0, 7), (0, 7), (0, 3, 7)),
-        ((1, 0), (3, 0, 1), (3, 0, 1), (1, 0)),
+        ((2, 6, 7), (7, 6), (3, 7, 6), (7, 6)),
+        ((7, 3, 0), (0, 7), (0, 2, 7), (0, 7)),
+        ((1, 0), (1, 0), (1, 0), (1, 0)),
         ((0, 1, 2), (2, 1), (2, 1), (2, 1)),
     ),
     (1, 1, 3): (
@@ -76,16 +77,16 @@
         ((2, 1, 0), (0, 1), (0, 1), (1, 0)),
     ),
     (2, 1, 3): (
-        ((5, 4, 6), (4, 5, 6), (6, 5, 4), (4, 5, 6)),
+        ((4, 5, 6), (4, 5, 6), (6, 5, 4), (4, 5, 6)),
         ((6, 7, 5), (5, 6, 7), (5, 6, 7), (7, 6, 5)),
         ((7, 6, 0), (6, 7, 0), (0, 7, 6), (6, 7, 0)),
-        ((0, 1, 7), (7, 0, 1), (7, 0, 1), (1, 0, 7)),
+        ((1, 0, 7), (7, 0, 1), (7, 0, 1), (1, 0, 7)),
     ),
     (2, 1, 2): (
-        ((1, 4, 5), (4, 5), (1, 5, 4), (4, 5)),
-        ((2, 5, 6), (5, 6), (2, 6, 5), (5, 6)),
-        ((7, 6), (6, 7), (3, 7, 6), (6, 7)),
-        ((0, 7), (7, 0), (0, 4, 7), (7, 4, 0)),
+        ((1, 5, 4), (4, 5), (1, 5, 4), (4, 5)),
+        ((2, 6, 5), (5, 6), (2, 6, 5), (5, 6)),
+        ((3, 7, 6), (6, 7), (3, 7, 6), (6, 7)),
+        ((0, 4, 7), (7, 4, 0), (0, 4, 7), (7, 0)),
     ),
     (3, 0, 3): (
         ((4, 5, 3), (3, 4, 5), (5, 4, 3), (3, 4, 5)),
@@ -114,8 +115,8 @@
     (4, 0, 3): (
         ((3, 2, 4), (4, 3, 2), (4, 3, 2), (2, 3, 4)),
         ((4, 5, 3), (5, 4, 3), (3, 4, 5), (5, 4, 3)),
-        ((6, 4, 5), (6, 5, 4), (6, 5, 4), (4, 5, 6)),
-        ((5, 7, 6), (7, 6, 5), (5, 6, 7), (7, 6, 5)),
+        ((5, 4, 6), (6, 5, 4), (6, 5, 4), (4, 5, 6)),
+        ((6, 7, 5), (7, 6, 5), (5, 6, 7), (7, 6, 5)),
     ),
     (4, 0, 2): (
         ((3, 4), (4, 3), (3, 7, 4), (4, 7, 3)),
@@ -149,15 +150,15 @@
     ),
     (5, 1, 3): (
         ((3, 2, 1), (3, 2, 1), (1, 2, 3), (3, 2, 1)),
-        ((4, 3, 2), (2, 3, 4), (2, 3, 4), (2, 3, 4)),
+        ((4, 3, 2), (4, 3, 2), (2, 3, 4), (2, 3, 4)),
         ((5, 4, 3), (5, 4, 3), (3, 4, 5), (5, 4, 3)),
-        ((6, 5, 4), (4, 5, 6), (4, 5, 6), (4, 5, 6)),
+        ((6, 5, 4), (6, 5, 4), (4, 5, 6), (4, 5, 6)),
     ),
     (5, 1, 2): (
         ((3, 2, 1), (1, 2), (1, 2), (1, 2)),
-        ((0, 3, 2), (2, 3), (0, 3, 2), (2, 3)),
-        ((5, 4, 3), (3, 4), (3, 4), (3, 0, 4)),
-        ((2, 5, 4), (0, 5, 4), (2, 5, 4), (4, 5)),
+        ((2, 3), (2, 3), (2, 3), (2, 3)),
+        ((4, 0, 3), (3, 4), (3, 1, 4), (3, 4)),
+        ((1, 5, 4), (4, 5), (0, 4, 5), (4, 5)),
     ),
     (6, 0, 3): (
         ((3, 2, 1), (1, 2), (1, 2), (1, 2)),
@@ -272,11 +273,10 @@
     return start, shift, first, second, keep, send
 
 
-def product_kernel(slots, last, rows, held_at, index, *refs):
-    buffers = refs[: 1 + len(held_at)]
-    tokens, out, held, sems = refs[1 + len(held_at) : -3 - last], refs[-3], refs[-2], refs[-1]
-    jobs = [(part, side) for part in range(PARTS) for side in range(1 + last)]
-    early = sum(step < ROUNDS - 1 for step, _ in held_at)
+def product_kernel(slots, last, rows, early, held_at, index, *refs):
+    buffers, (mid, end) = refs[: 1 + len(held_at)], refs[1 + len(held_at) : 3 + len(held_at)]
+    out, held, sems = refs[-3:]
+    jobs = [(part, side) for part in range(PARTS) for side in range(2)]
 
     def fetch(part, side, source):
         return pltpu.make_async_copy(source, held.at[side, part], sems.at[side, part])
@@ -286,25 +286,22 @@
 
     def due(part, side):
         which = index[part * 3 + slots[side]]
-        came_late = which > early
-        if side:
-            return which, which >= 0
-        return which, came_late if last else jnp.logical_not(came_late)
+        return which, which > early if last else which <= early
 
     for part, side in jobs:
-        which, wanted = due(part, side)
-        if not last or side:
+        which = due(part, side)[0]
+        if not last:
 
             @pl.when(which == 0)
             def _():
                 fetch(part, side, own(part)).start()
 
-        for number, (step, of) in enumerate(held_at, 1):
-            if of == part and (side or last == (step == ROUNDS - 1)):
+        for number, (_, of) in enumerate(held_at, 1 + early if last else 1):
+            if of == part:
 
                 @pl.when(which == number)
                 def _():
-                    fetch(part, side, buffers[number]).start()
+                    fetch(part, side, buffers[number - early if last else number]).start()
 
     if not last:
         out[...] = jnp.zeros_like(out)
@@ -317,37 +314,38 @@
             for low in range(0, width, 256):
                 high = min(low + 256, width)
                 out[:, low:high] += jnp.dot(
-                    tokens[side][:, part * rows : (part + 1) * rows],
+                    (mid, end)[side][: out.shape[0], part * rows : (part + 1) * rows],
                     held[side, part, :, low:high],
                     preferred_element_type=jnp.float32,
                 )
 
 
-def product(slots, index, own, got, mid, *more):
-    last = bool(more)
+def product(slots, index, own, got, mid, end, *before):
+    last = bool(before)
     rows = own.shape[0] // PARTS
-    held_at = sorted(key for key in got if last or key[0] < ROUNDS - 1)
+    early = sum(key[0] < ROUNDS - 1 for key in got)
+    held_at = sorted(key for key in got if last == (key[0] == ROUNDS - 1))
     buffers = [own] + [got[key] for key in held_at]
-    tokens, width = mid.shape[0], own.shape[1]
+    count, width = mid.shape[0] - SPARE, own.shape[1]
     anywhere = pl.BlockSpec(memory_space=pl.ANY)
     whole = pl.BlockSpec(memory_space=pltpu.VMEM)
     return pl.pallas_call(
-        functools.partial(product_kernel, slots, last, rows, held_at),
-        out_shape=jax.ShapeDtypeStruct((tokens, width), jnp.float32),
-        in_specs=[pl.BlockSpec(memory_space=pltpu.SMEM)] + [anywhere] * len(buffers) + [whole] * (1 + len(more)),
+        functools.partial(product_kernel, slots, last, rows, early, held_at),
+        out_shape=jax.ShapeDtypeStruct((count, width), jnp.float32),
+        in_specs=[pl.BlockSpec(memory_space=pltpu.SMEM)] + [anywhere] * len(buffers) + [whole] * (2 + last),
         out_specs=whole,
         input_output_aliases={len(buffers) + 3: 0} if last else {},
         scratch_shapes=[
-            pltpu.VMEM((1 + last, PARTS, rows, width), jnp.bfloat16),
-            pltpu.SemaphoreType.DMA((1 + last, PARTS)),
+            pltpu.VMEM((2, PARTS, rows, width), jnp.bfloat16),
+            pltpu.SemaphoreType.DMA((2, PARTS)),
         ],
-        compiler_params=pltpu.CompilerParams(vmem_limit_bytes=40 * 2**20),
+        compiler_params=pltpu.CompilerParams(vmem_limit_bytes=24 * 2**20),
         cost_estimate=pl.CostEstimate(
-            flops=2 * tokens * own.shape[0] * width,
-            bytes_accessed=2 * own.shape[0] * width + 8 * tokens * width,
+            flops=2 * count * own.shape[0] * width,
+            bytes_accessed=2 * own.shape[0] * width + 8 * count * width,
             transcendentals=0,
         ),
-    )(index, *buffers, mid, *more)
+    )(index, *buffers, mid, end, *before)
 
 
 def on_device(tokens, gate_weight):
@@ -376,7 +374,7 @@
         return got[step, part]
 
     def product_of(slots, *operands):
-        return product(slots, index, gate_weight, *operands)
+        return product(slots, index, gate_weight, got, *operands)
 
     shifted = send(tokens, start)
     parts = [after(value, tokens) for value in parts]
@@ -387,15 +385,14 @@
     keep_mid = jnp.where(core == half, shifted, crossed)
     send_mid = jnp.where(core == half, crossed, also)
     keep_end, send_end = send(keep_mid, near_keep), send(send_mid, near_send)
-    a, b, c = weights(3, 1, a, crossed, also), weights(3, 2), weights(3, 3)
-    early = {key: value for key, value in got.items() if key[0] < ROUNDS - 1}
-    sent = product_of((0, 2), early, send_mid)
-    kept = product_of((0, 1), early, keep_mid)
-    keep_end, send_end, sent, kept = lax.optimization_barrier((keep_end, send_end, sent, kept))
-    sent = product_of((0, 2), got, send_mid, send_end, sent)
+    a, b, c = weights(3, 1, a, keep_mid, send_mid), weights(3, 2, keep_mid, send_mid), weights(3, 3, keep_mid, send_mid)
+    sent = product_of((0, 2), send_mid, send_end)
+    kept = product_of((0, 1), keep_mid, keep_end)
+    got = dict(zip(got, lax.optimization_barrier((sent, kept) + tuple(got.values()))[2:]))
+    sent = product_of((0, 2), send_mid, send_end, sent)
     swap = [(place(x, y, c, z, h), place(x, y, 1 - c, z, h)) for x, y, c, z, h in everywhere()]
     arrived = send(sent, swap)
-    kept = product_of((0, 1), got, keep_mid, keep_end, kept)
+    kept = product_of((0, 1), keep_mid, keep_end, kept)
     return kept + arrived
 
 def solution(mesh):

time: 175 us -> 158 us (0.903)
  the two profiles are of different devices: /device:TPU:73 before, /device:TPU:71 now
where the time goes in v4:
time: 158 us; the launch traced here: 157 us
  waiting for transfers between devices  64.2 us (41%)
  starting transfers between devices  60.1 us (38%)
  Pallas kernels  19.3 us (12%)
  local copies, waits for them, and re-layouts  9.12 us (6%)
  other arithmetic  4.37 us (3%)
    ppermute x19, waiting for transfers between devices, send(): return lax.ppermute(value, BOTH, pairs)  64.2 us
    ppermute x19, starting transfers between devices, send(): return lax.ppermute(value, BOTH, pairs)  60.1 us
    pallas_call x4, Pallas kernels, product(): pl.pallas_call(functools.partial(product_kernel, slots, last, rows, early...  19.3 us
    unnamed x18, local copies, waits for them, and re-layouts  6.17 us
  transfers between devices with their start and end apart: 19, of which 8 were waited for; matrix products, arithmetic and copies ran while one was open for 2% of the time, Pallas kernels for 10%

profile of v4, /device:TPU:71, one launch (start us, length us, event | category | flops | bytes accessed | tf_op | source)
XLA Modules:
  0.0 157.3 jit_solution(5834882102523272751)
XLA Ops:
  0.0 2.2 %fusion = (bf16[256,1664]{1,0:T(8,128)(2,1)S(1)}, bf16[256,1664]{1,0:T(8,128)(2,1)S(1)}, bf16[256,1664]{1,0:T(8,128)(2,1)S(1)}, bf16[256,1664]{1,0:T(8,128)(2,1)S(1)}) fusion(bf16[1024,1664]{1,0:T(8,128)(2,1)} %refs_0_.7), kind=kLoop, calls=%fused_computation.3 | loop fusion | bytes 6815744 | tf_op jit(solution)/shard_map/slice | solution.py:358
  3.8 8.1 %collective-permute-start.5 = (bf16[384,1024]{1,0:T(8,128)(2,1)S(1)}, bf16[384,1024]{1,0:T(8,128)(2,1)S(1)}, u32[]{:S(2)}, u32[]{:S(2)}) collective-permute-start(bf16[384,1024]{1,0:T(8,128)(2,1)S(1)} %copy-done.8), channel_id=1, source_target_pairs={{0,14},{1,15},{2,0},{3,1},{4,2},{5,3},{6,4},{7,5},{8,6},{9,7},{10,... | collective-permute-start | bytes 2359304 | tf_op jit(solution)/shard_map/ppermute | solution.py:366
  12.0 8.6 %collective-permute-done.refs_1_ = bf16[256,1664]{1,0:T(8,128)(2,1)S(1)} collective-permute-done((bf16[256,1664]{1,0:T(8,128)(2,1)S(1)}, bf16[256,1664]{1,0:T(8,128)(2,1)S(1)}, u32[]{:S(2)}, u32[]{:S(2)}) %collective-permute-start) | collective-permute-done | bytes 852000 | tf_op jit(solution)/shard_map/ppermute | solution.py:366
  20.6 3.5 %collective-permute-start.3 = (bf16[256,1664]{1,0:T(8,128)(2,1)S(1)}, bf16[256,1664]{1,0:T(8,128)(2,1)}, u32[]{:S(2)}, u32[]{:S(2)}) collective-permute-start(bf16[256,1664]{1,0:T(8,128)(2,1)S(1)} %collective-permute-done.refs_1_), channel_id=1, source_target_pairs={{32,192},{64,224},{96,0},{0,32},{160,64},{192,96},{224,128},{128,1... | collective-permute-start | bytes 2555912 | tf_op jit(solution)/shard_map/ppermute | solution.py:366
  25.0 13.9 %collective-permute-done.1.refs_2_ = bf16[256,1664]{1,0:T(8,128)(2,1)S(1)} collective-permute-done((bf16[256,1664]{1,0:T(8,128)(2,1)S(1)}, bf16[256,1664]{1,0:T(8,128)(2,1)S(1)}, u32[]{:S(2)}, u32[]{:S(2)}) %collective-permute-start.1) | collective-permute-done | bytes 852000 | tf_op jit(solution)/shard_map/ppermute | solution.py:366
  38.9 2.5 %collective-permute-start.4 = (bf16[256,1664]{1,0:T(8,128)(2,1)S(1)}, bf16[256,1664]{1,0:T(8,128)(2,1)S(1)}, u32[]{:S(2)}, u32[]{:S(2)}) collective-permute-start(bf16[256,1664]{1,0:T(8,128)(2,1)S(1)} %collective-permute-done.1.refs_2_), channel_id=1, source_target_pairs={{32,192},{64,224},{96,0},{0,32},{160,64},{192,96},{224,128},{128,1... | collective-permute-start | bytes 2555912 | tf_op jit(solution)/shard_map/ppermute | solution.py:366
  42.3 3.4 %collective-permute-done.5 = bf16[384,1024]{1,0:T(8,128)(2,1)S(1)} collective-permute-done((bf16[384,1024]{1,0:T(8,128)(2,1)S(1)}, bf16[384,1024]{1,0:T(8,128)(2,1)S(1)}, u32[]{:S(2)}, u32[]{:S(2)}) %collective-permute-start.5) | collective-permute-done | bytes 786464 | tf_op jit(solution)/shard_map/ppermute | solution.py:366
  45.7 1.9 %collective-permute-start.9 = (bf16[384,1024]{1,0:T(8,128)(2,1)S(1)}, bf16[384,1024]{1,0:T(8,128)(2,1)}, u32[]{:S(2)}, u32[]{:S(2)}) collective-permute-start(bf16[384,1024]{1,0:T(8,128)(2,1)S(1)} %collective-permute-done.5), channel_id=1, source_target_pairs={{0,0},{1,1},{2,2},{3,3},{4,4},{5,5},{6,6},{7,7},{8,8},{9,9},{10,10... | collective-permute-start | bytes 2359304 | tf_op jit(solution)/shard_map/ppermute | solution.py:366
  47.6 1.4 collective-permute-done.2.refs_3_
  50.0 14.2 %collective-permute-done.9 = bf16[384,1024]{1,0:T(8,128)(2,1)} collective-permute-done((bf16[384,1024]{1,0:T(8,128)(2,1)S(1)}, bf16[384,1024]{1,0:T(8,128)(2,1)}, u32[]{:S(2)}, u32[]{:S(2)}) %collective-permute-start.9) | collective-permute-done | bytes 786464 | tf_op jit(solution)/shard_map/ppermute | solution.py:366
  64.2 2.0 %collective-permute-start.11 = (bf16[384,1024]{1,0:T(8,128)(2,1)}, bf16[384,1024]{1,0:T(8,128)(2,1)}, u32[]{:S(2)}, u32[]{:S(2)}) collective-permute-start(bf16[384,1024]{1,0:T(8,128)(2,1)} %collective-permute-done.9), channel_id=1, source_target_pairs={{0,1},{1,17},{2,3},{3,19},{4,5},{5,21},{6,7},{7,23},{8,9},{9,25},{... | collective-permute-start | bytes 2359304 | tf_op jit(solution)/shard_map/ppermute | solution.py:366
  67.1 1.6 %collective-permute-start.12 = (bf16[384,1024]{1,0:T(8,128)(2,1)}, bf16[384,1024]{1,0:T(8,128)(2,1)}, u32[]{:S(2)}, u32[]{:S(2)}) collective-permute-start(bf16[384,1024]{1,0:T(8,128)(2,1)} %collective-permute-done.9), channel_id=1, source_target_pairs={{1,16},{3,18},{5,20},{7,22},{9,24},{11,26},{13,28},{15,30},{16,1},... | collective-permute-start | bytes 2359304 | tf_op jit(solution)/shard_map/ppermute | solution.py:366
  68.8 8.6 %collective-permute-start.7 = (bf16[256,1664]{1,0:T(8,128)(2,1)}, bf16[256,1664]{1,0:T(8,128)(2,1)}, u32[]{:S(2)}, u32[]{:S(2)}) collective-permute-start(bf16[256,1664]{1,0:T(8,128)(2,1)} %collective-permute-done.3.refs_4_), channel_id=1, source_target_pairs={{192,224},{224,0},{0,32},{32,64},{64,96},{96,128},{128,160},{160,1... | collective-permute-start | bytes 2555912 | tf_op jit(solution)/shard_map/ppermute | solution.py:366
  77.4 1.9 %collective-permute-start.10 = (bf16[256,1664]{1,0:T(8,128)(2,1)}, bf16[256,1664]{1,0:T(8,128)(2,1)}, u32[]{:S(2)}, u32[]{:S(2)}) collective-permute-start(bf16[256,1664]{1,0:T(8,128)(2,1)} %collective-permute-done.6.refs_6_), channel_id=1, source_target_pairs={{224,192},{0,224},{32,0},{64,32},{96,64},{128,96},{160,128},{192,1... | collective-permute-start | bytes 2555912 | tf_op jit(solution)/shard_map/ppermute | solution.py:366
  79.3 1.9 %collective-permute-start.8 = (bf16[256,1664]{1,0:T(8,128)(2,1)}, bf16[256,1664]{1,0:T(8,128)(2,1)}, u32[]{:S(2)}, u32[]{:S(2)}) collective-permute-start(bf16[256,1664]{1,0:T(8,128)(2,1)} %collective-permute-done.2.refs_3_), channel_id=1, source_target_pairs={{192,224},{160,0},{96,32},{0,64},{64,96},{32,128},{224,160},{128,1... | collective-permute-start | bytes 2555912 | tf_op jit(solution)/shard_map/ppermute | solution.py:366
  81.3 2.6 %broadcast_select_fusion = (bf16[384,1024]{1,0:T(8,128)(2,1)}, bf16[384,1024]{1,0:T(8,128)(2,1)}) fusion(bf16[384,1024]{1,0:T(8,128)(2,1)} %collective-permute-done.9, bf16[384,1024]{1,0:T(8,128)(2,1)} %collective-permute-done.11, pred[]{:T(512)S(6)} %eq.7, bf16[384,1024]{1,0:T(8,128)(2,1)} %collective-permute-done.12), kind=kLoop, calls=%fused_computation | loop fusion | flops 786432 | bytes 3932161 | tf_op jit(solution)/shard_map/jit(_where)/select_n | solution.py:385
  84.0 8.5 %collective-permute-start.14 = (bf16[384,1024]{1,0:T(8,128)(2,1)}, bf16[384,1024]{1,0:T(8,128)(2,1)}, u32[]{:S(2)}, u32[]{:S(2)}) collective-permute-start(bf16[384,1024]{1,0:T(8,128)(2,1)} %get-tuple-element.41.refs_10_.refs_4_), channel_id=1, source_target_pairs={{14,0},{3,1},{0,2},{5,3},{2,4},{7,5},{4,6},{9,7},{6,8},{11,9},{8,1... | collective-permute-start | bytes 2359304 | tf_op jit(solution)/shard_map/ppermute | solution.py:366
  92.5 15.0 %collective-permute-done.7.refs_7_ = bf16[256,1664]{1,0:T(8,128)(2,1)} collective-permute-done((bf16[256,1664]{1,0:T(8,128)(2,1)}, bf16[256,1664]{1,0:T(8,128)(2,1)}, u32[]{:S(2)}, u32[]{:S(2)}) %collective-permute-start.7) | collective-permute-done | bytes 852000 | tf_op jit(solution)/shard_map/ppermute | solution.py:366
  107.5 1.9 %collective-permute-start.15 = (bf16[256,1664]{1,0:T(8,128)(2,1)}, bf16[256,1664]{1,0:T(8,128)(2,1)}, u32[]{:S(2)}, u32[]{:S(2)}) collective-permute-start(bf16[256,1664]{1,0:T(8,128)(2,1)} %copy-done.5), channel_id=1, source_target_pairs={{192,224},{224,0},{0,32},{32,64},{64,96},{96,128},{128,160},{160,1... | collective-permute-start | bytes 2555912 | tf_op jit(solution)/shard_map/ppermute | solution.py:366
  109.4 5.5 %collective-permute-start.17 = (bf16[256,1664]{1,0:T(8,128)(2,1)}, bf16[256,1664]{1,0:T(8,128)(2,1)}, u32[]{:S(2)}, u32[]{:S(2)}) collective-permute-start(bf16[256,1664]{1,0:T(8,128)(2,1)} %collective-permute-done.10.refs_9_), channel_id=1, source_target_pairs={{194,162},{226,2},{2,226},{34,66},{66,34},{98,130},{130,98},{162,1... | collective-permute-start | bytes 2555912 | tf_op jit(solution)/shard_map/ppermute | solution.py:366
  114.9 1.9 %collective-permute-start.16 = (bf16[256,1664]{1,0:T(8,128)(2,1)}, bf16[256,1664]{1,0:T(8,128)(2,1)}, u32[]{:S(2)}, u32[]{:S(2)}) collective-permute-start(bf16[256,1664]{1,0:T(8,128)(2,1)} %collective-permute-done.8.refs_8_), channel_id=1, source_target_pairs={{0,224},{32,0},{64,32},{128,96},{160,128},{192,160},{113,241},{241... | collective-permute-start | bytes 2555912 | tf_op jit(solution)/shard_map/ppermute | solution.py:366
  117.5 1.1 copy-done.2
  118.7 1.2 copy-done.4
  119.8 1.2 copy-done.6
  121.0 6.5 %shard_map.38.refs_6_ = f32[384,1664]{1,0:T(8,128)S(1)} custom-call(s32[12]{0:T(128)S(1)} %dynamic-slice_bitcast_fusion.index, bf16[1024,1664]{1,0:T(8,128)(2,1)S(1)} %copy-done, bf16[256,1664]{1,0:T(8,128)(2,1)S(1)} %copy-done.2, bf16[256,1664]{1,0:T(8,128)(2,1)S(1)} %copy-done.4, bf16[256,1664]{1,0:T(8,128)(2,1)} %collective-permute-done.2.refs_3_, ...), custom_call_target="tpu_custom_call" | custom-call | flops 1308622848 | bytes 8519680 | tf_op jit(solution)/shard_map/pallas_call | solution.py:332
  127.5 5.9 %shard_map.37.refs_6_ = f32[384,1664]{1,0:T(8,128)S(1)} custom-call(s32[12]{0:T(128)S(1)} %dynamic-slice_bitcast_fusion.index, bf16[1024,1664]{1,0:T(8,128)(2,1)S(1)} %copy-done, bf16[256,1664]{1,0:T(8,128)(2,1)S(1)} %copy-done.2, bf16[256,1664]{1,0:T(8,128)(2,1)S(1)} %copy-done.4, bf16[256,1664]{1,0:T(8,128)(2,1)} %collective-permute-done.2.refs_3_, ...), custom_call_target="tpu_custom_call" | custom-call | flops 1308622848 | bytes 8519680 | tf_op jit(solution)/shard_map/pallas_call | solution.py:332
  133.4 6.4 %collective-permute-done.17.refs_3_ = bf16[256,1664]{1,0:T(8,128)(2,1)} collective-permute-done((bf16[256,1664]{1,0:T(8,128)(2,1)}, bf16[256,1664]{1,0:T(8,128)(2,1)}, u32[]{:S(2)}, u32[]{:S(2)}) %collective-permute-start.17) | collective-permute-done | bytes 852000 | tf_op jit(solution)/shard_map/ppermute | solution.py:366
  139.8 3.7 %shard_map.40 = f32[384,1664]{1,0:T(8,128)S(1)} custom-call(s32[12]{0:T(128)S(1)} %dynamic-slice_bitcast_fusion.index, bf16[1024,1664]{1,0:T(8,128)(2,1)S(1)} %copy-done, bf16[256,1664]{1,0:T(8,128)(2,1)} %collective-permute-done.15.refs_1_, bf16[256,1664]{1,0:T(8,128)(2,1)} %collective-permute-done.16.refs_2_, ...), custom_call_target="tpu_custom_call", output_to_operand_aliasing={{}: (7, {})} | custom-call | flops 1308622848 | bytes 8519680 | tf_op jit(solution)/shard_map/pallas_call | solution.py:332
  143.5 7.6 %collective-permute-start.18 = (f32[384,1664]{1,0:T(8,128)S(1)}, f32[384,1664]{1,0:T(8,128)S(1)}, u32[]{:S(2)}, u32[]{:S(2)}) collective-permute-start(f32[384,1664]{1,0:T(8,128)S(1)} %shard_map.40), channel_id=1, source_target_pairs={{0,16},{1,17},{2,18},{3,19},{4,20},{5,21},{6,22},{7,23},{8,24},{9,... | collective-permute-start | bytes 7667720 | tf_op jit(solution)/shard_map/ppermute | solution.py:366
  151.1 3.2 %shard_map.39 = f32[384,1664]{1,0:T(8,128)S(1)} custom-call(s32[12]{0:T(128)S(1)} %dynamic-slice_bitcast_fusion.index, bf16[1024,1664]{1,0:T(8,128)(2,1)S(1)} %copy-done, bf16[256,1664]{1,0:T(8,128)(2,1)} %collective-permute-done.15.refs_1_, bf16[256,1664]{1,0:T(8,128)(2,1)} %collective-permute-done.16.refs_2_, ...), custom_call_target="tpu_custom_call", output_to_operand_aliasing={{}: (7, {})} | custom-call | flops 1308622848 | bytes 8519680 | tf_op jit(solution)/shard_map/pallas_call | solution.py:332
  154.3 1.3 collective-permute-done.18
  155.6 1.7 %add.21 = f32[384,1664]{1,0:T(8,128)} add(f32[384,1664]{1,0:T(8,128)S(1)} %shard_map.39, f32[384,1664]{1,0:T(8,128)S(1)} %collective-permute-done.18) | non-fusion elementwise | flops 638976 | bytes 7667712 | tf_op jit(solution)/shard_map/add | solution.py:396
  (32 shorter events, 6.0 us)
Async XLA Ops:
  0.0 3.8 %copy-start.8 = (bf16[384,1024]{1,0:T(8,128)(2,1)S(1)}, bf16[384,1024]{1,0:T(8,128)(2,1)}, u32[]{:S(2)}) copy-start(bf16[384,1024]{1,0:T(8,128)(2,1)} %param.3) | copy-start | bytes 2359300
  2.3 115.3 %copy-start = (bf16[1024,1664]{1,0:T(8,128)(2,1)S(1)}, bf16[1024,1664]{1,0:T(8,128)(2,1)}, u32[]{:S(2)}) copy-start(bf16[1024,1664]{1,0:T(8,128)(2,1)} %refs_0_.7) | copy-start | bytes 10223620
  2.3 18.4 %collective-permute-start = (bf16[256,1664]{1,0:T(8,128)(2,1)S(1)}, bf16[256,1664]{1,0:T(8,128)(2,1)S(1)}, u32[]{:S(2)}, u32[]{:S(2)}) collective-permute-start(bf16[256,1664]{1,0:T(8,128)(2,1)S(1)} %get-tuple-element.21), channel_id=1, source_target_pairs={{0,32},{32,64},{64,96},{96,0},{128,160},{160,192},{192,224},{224,1... | collective-permute-start | bytes 2555912 | tf_op jit(solution)/shard_map/ppermute | solution.py:366
  2.9 36.0 %collective-permute-start.1 = (bf16[256,1664]{1,0:T(8,128)(2,1)S(1)}, bf16[256,1664]{1,0:T(8,128)(2,1)S(1)}, u32[]{:S(2)}, u32[]{:S(2)}) collective-permute-start(bf16[256,1664]{1,0:T(8,128)(2,1)S(1)} %get-tuple-element.22), channel_id=1, source_target_pairs={{0,32},{32,64},{64,96},{96,0},{128,160},{160,192},{192,224},{224,1... | collective-permute-start | bytes 2555912 | tf_op jit(solution)/shard_map/ppermute | solution.py:366
  3.8 41.9 %collective-permute-start.5 = (bf16[384,1024]{1,0:T(8,128)(2,1)S(1)}, bf16[384,1024]{1,0:T(8,128)(2,1)S(1)}, u32[]{:S(2)}, u32[]{:S(2)}) collective-permute-start(bf16[384,1024]{1,0:T(8,128)(2,1)S(1)} %copy-done.8), channel_id=1, source_target_pairs={{0,14},{1,15},{2,0},{3,1},{4,2},{5,3},{6,4},{7,5},{8,6},{9,7},{10,... | collective-permute-start | bytes 2359304 | tf_op jit(solution)/shard_map/ppermute | solution.py:366
  11.9 37.2 %collective-permute-start.2 = (bf16[256,1664]{1,0:T(8,128)(2,1)S(1)}, bf16[256,1664]{1,0:T(8,128)(2,1)}, u32[]{:S(2)}, u32[]{:S(2)}) collective-permute-start(bf16[256,1664]{1,0:T(8,128)(2,1)S(1)} %get-tuple-element.23), channel_id=1, source_target_pairs={{0,192},{32,160},{64,96},{96,0},{128,64},{160,32},{192,224},{224,1... | collective-permute-start | bytes 2555912 | tf_op jit(solution)/shard_map/ppermute | solution.py:366
  20.6 43.6 %collective-permute-start.3 = (bf16[256,1664]{1,0:T(8,128)(2,1)S(1)}, bf16[256,1664]{1,0:T(8,128)(2,1)}, u32[]{:S(2)}, u32[]{:S(2)}) collective-permute-start(bf16[256,1664]{1,0:T(8,128)(2,1)S(1)} %collective-permute-done.refs_1_), channel_id=1, source_target_pairs={{32,192},{64,224},{96,0},{0,32},{160,64},{192,96},{224,128},{128,1... | collective-permute-start | bytes 2555912 | tf_op jit(solution)/shard_map/ppermute | solution.py:366
  24.1 0.9 copy-start.1
  38.9 27.3 %collective-permute-start.4 = (bf16[256,1664]{1,0:T(8,128)(2,1)S(1)}, bf16[256,1664]{1,0:T(8,128)(2,1)S(1)}, u32[]{:S(2)}, u32[]{:S(2)}) collective-permute-start(bf16[256,1664]{1,0:T(8,128)(2,1)S(1)} %collective-permute-done.1.refs_2_), channel_id=1, source_target_pairs={{32,192},{64,224},{96,0},{0,32},{160,64},{192,96},{224,128},{128,1... | collective-permute-start | bytes 2555912 | tf_op jit(solution)/shard_map/ppermute | solution.py:366
  41.4 0.9 copy-start.3
  45.7 18.5 %collective-permute-start.9 = (bf16[384,1024]{1,0:T(8,128)(2,1)S(1)}, bf16[384,1024]{1,0:T(8,128)(2,1)}, u32[]{:S(2)}, u32[]{:S(2)}) collective-permute-start(bf16[384,1024]{1,0:T(8,128)(2,1)S(1)} %collective-permute-done.5), channel_id=1, source_target_pairs={{0,0},{1,1},{2,2},{3,3},{4,4},{5,5},{6,6},{7,7},{8,8},{9,9},{10,10... | collective-permute-start | bytes 2359304 | tf_op jit(solution)/shard_map/ppermute | solution.py:366
  49.1 28.3 %collective-permute-start.6 = (bf16[256,1664]{1,0:T(8,128)(2,1)S(1)}, bf16[256,1664]{1,0:T(8,128)(2,1)}, u32[]{:S(2)}, u32[]{:S(2)}) collective-permute-start(bf16[256,1664]{1,0:T(8,128)(2,1)S(1)} %get-tuple-element.25), channel_id=1, source_target_pairs={{0,224},{32,0},{64,32},{96,64},{128,96},{160,128},{192,160},{224,1... | collective-permute-start | bytes 2555912 | tf_op jit(solution)/shard_map/ppermute | solution.py:366
  64.2 17.1 %collective-permute-start.11 = (bf16[384,1024]{1,0:T(8,128)(2,1)}, bf16[384,1024]{1,0:T(8,128)(2,1)}, u32[]{:S(2)}, u32[]{:S(2)}) collective-permute-start(bf16[384,1024]{1,0:T(8,128)(2,1)} %collective-permute-done.9), channel_id=1, source_target_pairs={{0,1},{1,17},{2,3},{3,19},{4,5},{5,21},{6,7},{7,23},{8,9},{9,25},{... | collective-permute-start | bytes 2359304 | tf_op jit(solution)/shard_map/ppermute | solution.py:366
  66.2 0.9 copy-start.5
  67.1 14.2 %collective-permute-start.12 = (bf16[384,1024]{1,0:T(8,128)(2,1)}, bf16[384,1024]{1,0:T(8,128)(2,1)}, u32[]{:S(2)}, u32[]{:S(2)}) collective-permute-start(bf16[384,1024]{1,0:T(8,128)(2,1)} %collective-permute-done.9), channel_id=1, source_target_pairs={{1,16},{3,18},{5,20},{7,22},{9,24},{11,26},{13,28},{15,30},{16,1},... | collective-permute-start | bytes 2359304 | tf_op jit(solution)/shard_map/ppermute | solution.py:366
  68.8 38.7 %collective-permute-start.7 = (bf16[256,1664]{1,0:T(8,128)(2,1)}, bf16[256,1664]{1,0:T(8,128)(2,1)}, u32[]{:S(2)}, u32[]{:S(2)}) collective-permute-start(bf16[256,1664]{1,0:T(8,128)(2,1)} %collective-permute-done.3.refs_4_), channel_id=1, source_target_pairs={{192,224},{224,0},{0,32},{32,64},{64,96},{96,128},{128,160},{160,1... | collective-permute-start | bytes 2555912 | tf_op jit(solution)/shard_map/ppermute | solution.py:366
  77.4 32.0 %collective-permute-start.10 = (bf16[256,1664]{1,0:T(8,128)(2,1)}, bf16[256,1664]{1,0:T(8,128)(2,1)}, u32[]{:S(2)}, u32[]{:S(2)}) collective-permute-start(bf16[256,1664]{1,0:T(8,128)(2,1)} %collective-permute-done.6.refs_6_), channel_id=1, source_target_pairs={{224,192},{0,224},{32,0},{64,32},{96,64},{128,96},{160,128},{192,1... | collective-permute-start | bytes 2555912 | tf_op jit(solution)/shard_map/ppermute | solution.py:366
  79.3 35.5 %collective-permute-start.8 = (bf16[256,1664]{1,0:T(8,128)(2,1)}, bf16[256,1664]{1,0:T(8,128)(2,1)}, u32[]{:S(2)}, u32[]{:S(2)}) collective-permute-start(bf16[256,1664]{1,0:T(8,128)(2,1)} %collective-permute-done.2.refs_3_), channel_id=1, source_target_pairs={{192,224},{160,0},{96,32},{0,64},{64,96},{32,128},{224,160},{128,1... | collective-permute-start | bytes 2555912 | tf_op jit(solution)/shard_map/ppermute | solution.py:366
  84.0 33.6 %collective-permute-start.14 = (bf16[384,1024]{1,0:T(8,128)(2,1)}, bf16[384,1024]{1,0:T(8,128)(2,1)}, u32[]{:S(2)}, u32[]{:S(2)}) collective-permute-start(bf16[384,1024]{1,0:T(8,128)(2,1)} %get-tuple-element.41.refs_10_.refs_4_), channel_id=1, source_target_pairs={{14,0},{3,1},{0,2},{5,3},{2,4},{7,5},{4,6},{9,7},{6,8},{11,9},{8,1... | collective-permute-start | bytes 2359304 | tf_op jit(solution)/shard_map/ppermute | solution.py:366
  92.5 35.0 %collective-permute-start.13 = (bf16[384,1024]{1,0:T(8,128)(2,1)}, bf16[384,1024]{1,0:T(8,128)(2,1)}, u32[]{:S(2)}, u32[]{:S(2)}) collective-permute-start(bf16[384,1024]{1,0:T(8,128)(2,1)} %get-tuple-element.42.refs_10_.refs_4_), channel_id=1, source_target_pairs={{2,0},{3,1},{4,2},{5,3},{6,4},{7,5},{8,6},{9,7},{10,8},{11,9},{12,... | collective-permute-start | bytes 2359304 | tf_op jit(solution)/shard_map/ppermute | solution.py:366
  107.5 26.0 %collective-permute-start.15 = (bf16[256,1664]{1,0:T(8,128)(2,1)}, bf16[256,1664]{1,0:T(8,128)(2,1)}, u32[]{:S(2)}, u32[]{:S(2)}) collective-permute-start(bf16[256,1664]{1,0:T(8,128)(2,1)} %copy-done.5), channel_id=1, source_target_pairs={{192,224},{224,0},{0,32},{32,64},{64,96},{96,128},{128,160},{160,1... | collective-permute-start | bytes 2555912 | tf_op jit(solution)/shard_map/ppermute | solution.py:366
  109.4 30.4 %collective-permute-start.17 = (bf16[256,1664]{1,0:T(8,128)(2,1)}, bf16[256,1664]{1,0:T(8,128)(2,1)}, u32[]{:S(2)}, u32[]{:S(2)}) collective-permute-start(bf16[256,1664]{1,0:T(8,128)(2,1)} %collective-permute-done.10.refs_9_), channel_id=1, source_target_pairs={{194,162},{226,2},{2,226},{34,66},{66,34},{98,130},{130,98},{162,1... | collective-permute-start | bytes 2555912 | tf_op jit(solution)/shard_map/ppermute | solution.py:366
  114.9 24.9 %collective-permute-start.16 = (bf16[256,1664]{1,0:T(8,128)(2,1)}, bf16[256,1664]{1,0:T(8,128)(2,1)}, u32[]{:S(2)}, u32[]{:S(2)}) collective-permute-start(bf16[256,1664]{1,0:T(8,128)(2,1)} %collective-permute-done.8.refs_8_), channel_id=1, source_target_pairs={{0,224},{32,0},{64,32},{128,96},{160,128},{192,160},{113,241},{241... | collective-permute-start | bytes 2555912 | tf_op jit(solution)/shard_map/ppermute | solution.py:366
  117.5 1.2 copy-start.2
  118.7 1.2 copy-start.4
  119.8 1.2 copy-start.6
  121.0 6.5 %copy-start.7 = (bf16[256,1664]{1,0:T(8,128)(2,1)S(1)}, bf16[256,1664]{1,0:T(8,128)(2,1)}, u32[]{:S(2)}) copy-start(bf16[256,1664]{1,0:T(8,128)(2,1)} %copy-done.5) | copy-start | bytes 2555908
  143.5 12.0 %collective-permute-start.18 = (f32[384,1664]{1,0:T(8,128)S(1)}, f32[384,1664]{1,0:T(8,128)S(1)}, u32[]{:S(2)}, u32[]{:S(2)}) collective-permute-start(f32[384,1664]{1,0:T(8,128)S(1)} %shard_map.40), channel_id=1, source_target_pairs={{0,16},{1,17},{2,18},{3,19},{4,20},{5,21},{6,22},{7,23},{8,24},{9,... | collective-permute-start | bytes 7667720 | tf_op jit(solution)/shard_map/ppermute | solution.py:366

commit v5 on v4

--- a/solution.py
+++ b/solution.py
@@ -339,7 +339,7 @@
             pltpu.VMEM((2, PARTS, rows, width), jnp.bfloat16),
             pltpu.SemaphoreType.DMA((2, PARTS)),
         ],
-        compiler_params=pltpu.CompilerParams(vmem_limit_bytes=24 * 2**20),
+        compiler_params=pltpu.CompilerParams(vmem_limit_bytes=16 * 2**20),
         cost_estimate=pl.CostEstimate(
             flops=2 * count * own.shape[0] * width,
             bytes_accessed=2 * own.shape[0] * width + 8 * count * width,

time: 158 us -> 158 us (level)
    unnamed x18 -> x22, local copies, waits for them, and re-layouts: 6.17 us -> 6.18 us
where the time goes in v5:
time: 158 us; the launch traced here: 157 us
  waiting for transfers between devices  64.1 us (41%)
  starting transfers between devices  60.1 us (38%)
  Pallas kernels  19.3 us (12%)
  local copies, waits for them, and re-layouts  9.12 us (6%)
  other arithmetic  4.38 us (3%)
    ppermute x19, waiting for transfers between devices, send(): return lax.ppermute(value, BOTH, pairs)  64.1 us
    ppermute x19, starting transfers between devices, send(): return lax.ppermute(value, BOTH, pairs)  60.1 us
    pallas_call x4, Pallas kernels, product(): pl.pallas_call(functools.partial(product_kernel, slots, last, rows, early...  19.3 us
    unnamed x22, local copies, waits for them, and re-layouts  6.18 us
  transfers between devices with their start and end apart: 19, of which 8 were waited for; matrix products, arithmetic and copies ran while one was open for 2% of the time, Pallas kernels for 10%

profile of v5, /device:TPU:71, one launch (start us, length us, event | category | flops | bytes accessed | tf_op | source)
XLA Modules:
  0.0 157.3 jit_solution(14811407548859609131)
XLA Ops:
  0.0 2.2 %fusion = (bf16[256,1664]{1,0:T(8,128)(2,1)S(1)}, bf16[256,1664]{1,0:T(8,128)(2,1)S(1)}, bf16[256,1664]{1,0:T(8,128)(2,1)S(1)}, bf16[256,1664]{1,0:T(8,128)(2,1)S(1)}) fusion(bf16[1024,1664]{1,0:T(8,128)(2,1)} %refs_0_.7), kind=kLoop, calls=%fused_computation.3 | loop fusion | bytes 6815744 | tf_op jit(solution)/shard_map/slice | solution.py:358
  3.8 8.1 %collective-permute-start.5 = (bf16[384,1024]{1,0:T(8,128)(2,1)S(1)}, bf16[384,1024]{1,0:T(8,128)(2,1)S(1)}, u32[]{:S(2)}, u32[]{:S(2)}) collective-permute-start(bf16[384,1024]{1,0:T(8,128)(2,1)S(1)} %copy-done.10), channel_id=1, source_target_pairs={{0,14},{1,15},{2,0},{3,1},{4,2},{5,3},{6,4},{7,5},{8,6},{9,7},{10,... | collective-permute-start | bytes 2359304 | tf_op jit(solution)/shard_map/ppermute | solution.py:366
  12.0 8.6 %collective-permute-done.refs_1_ = bf16[256,1664]{1,0:T(8,128)(2,1)S(1)} collective-permute-done((bf16[256,1664]{1,0:T(8,128)(2,1)S(1)}, bf16[256,1664]{1,0:T(8,128)(2,1)S(1)}, u32[]{:S(2)}, u32[]{:S(2)}) %collective-permute-start) | collective-permute-done | bytes 852000 | tf_op jit(solution)/shard_map/ppermute | solution.py:366
  20.6 3.5 %collective-permute-start.3 = (bf16[256,1664]{1,0:T(8,128)(2,1)S(1)}, bf16[256,1664]{1,0:T(8,128)(2,1)}, u32[]{:S(2)}, u32[]{:S(2)}) collective-permute-start(bf16[256,1664]{1,0:T(8,128)(2,1)S(1)} %collective-permute-done.refs_1_), channel_id=1, source_target_pairs={{32,192},{64,224},{96,0},{0,32},{160,64},{192,96},{224,128},{128,1... | collective-permute-start | bytes 2555912 | tf_op jit(solution)/shard_map/ppermute | solution.py:366
  25.0 13.9 %collective-permute-done.1.refs_2_ = bf16[256,1664]{1,0:T(8,128)(2,1)S(1)} collective-permute-done((bf16[256,1664]{1,0:T(8,128)(2,1)S(1)}, bf16[256,1664]{1,0:T(8,128)(2,1)S(1)}, u32[]{:S(2)}, u32[]{:S(2)}) %collective-permute-start.1) | collective-permute-done | bytes 852000 | tf_op jit(solution)/shard_map/ppermute | solution.py:366
  38.9 2.5 %collective-permute-start.4 = (bf16[256,1664]{1,0:T(8,128)(2,1)S(1)}, bf16[256,1664]{1,0:T(8,128)(2,1)S(1)}, u32[]{:S(2)}, u32[]{:S(2)}) collective-permute-start(bf16[256,1664]{1,0:T(8,128)(2,1)S(1)} %collective-permute-done.1.refs_2_), channel_id=1, source_target_pairs={{32,192},{64,224},{96,0},{0,32},{160,64},{192,96},{224,128},{128,1... | collective-permute-start | bytes 2555912 | tf_op jit(solution)/shard_map/ppermute | solution.py:366
  42.3 3.4 %collective-permute-done.5 = bf16[384,1024]{1,0:T(8,128)(2,1)S(1)} collective-permute-done((bf16[384,1024]{1,0:T(8,128)(2,1)S(1)}, bf16[384,1024]{1,0:T(8,128)(2,1)S(1)}, u32[]{:S(2)}, u32[]{:S(2)}) %collective-permute-start.5) | collective-permute-done | bytes 786464 | tf_op jit(solution)/shard_map/ppermute | solution.py:366
  45.7 1.9 %collective-permute-start.9 = (bf16[384,1024]{1,0:T(8,128)(2,1)S(1)}, bf16[384,1024]{1,0:T(8,128)(2,1)}, u32[]{:S(2)}, u32[]{:S(2)}) collective-permute-start(bf16[384,1024]{1,0:T(8,128)(2,1)S(1)} %collective-permute-done.5), channel_id=1, source_target_pairs={{0,0},{1,1},{2,2},{3,3},{4,4},{5,5},{6,6},{7,7},{8,8},{9,9},{10,10... | collective-permute-start | bytes 2359304 | tf_op jit(solution)/shard_map/ppermute | solution.py:366
  47.6 1.4 collective-permute-done.2.refs_3_
  50.0 14.2 %collective-permute-done.9 = bf16[384,1024]{1,0:T(8,128)(2,1)} collective-permute-done((bf16[384,1024]{1,0:T(8,128)(2,1)S(1)}, bf16[384,1024]{1,0:T(8,128)(2,1)}, u32[]{:S(2)}, u32[]{:S(2)}) %collective-permute-start.9) | collective-permute-done | bytes 786464 | tf_op jit(solution)/shard_map/ppermute | solution.py:366
  64.2 2.0 %collective-permute-start.11 = (bf16[384,1024]{1,0:T(8,128)(2,1)}, bf16[384,1024]{1,0:T(8,128)(2,1)}, u32[]{:S(2)}, u32[]{:S(2)}) collective-permute-start(bf16[384,1024]{1,0:T(8,128)(2,1)} %collective-permute-done.9), channel_id=1, source_target_pairs={{0,1},{1,17},{2,3},{3,19},{4,5},{5,21},{6,7},{7,23},{8,9},{9,25},{... | collective-permute-start | bytes 2359304 | tf_op jit(solution)/shard_map/ppermute | solution.py:366
  67.1 1.6 %collective-permute-start.12 = (bf16[384,1024]{1,0:T(8,128)(2,1)}, bf16[384,1024]{1,0:T(8,128)(2,1)}, u32[]{:S(2)}, u32[]{:S(2)}) collective-permute-start(bf16[384,1024]{1,0:T(8,128)(2,1)} %collective-permute-done.9), channel_id=1, source_target_pairs={{1,16},{3,18},{5,20},{7,22},{9,24},{11,26},{13,28},{15,30},{16,1},... | collective-permute-start | bytes 2359304 | tf_op jit(solution)/shard_map/ppermute | solution.py:366
  68.8 8.6 %collective-permute-start.7 = (bf16[256,1664]{1,0:T(8,128)(2,1)}, bf16[256,1664]{1,0:T(8,128)(2,1)}, u32[]{:S(2)}, u32[]{:S(2)}) collective-permute-start(bf16[256,1664]{1,0:T(8,128)(2,1)} %collective-permute-done.3.refs_4_), channel_id=1, source_target_pairs={{192,224},{224,0},{0,32},{32,64},{64,96},{96,128},{128,160},{160,1... | collective-permute-start | bytes 2555912 | tf_op jit(solution)/shard_map/ppermute | solution.py:366
  77.4 1.9 %collective-permute-start.10 = (bf16[256,1664]{1,0:T(8,128)(2,1)}, bf16[256,1664]{1,0:T(8,128)(2,1)}, u32[]{:S(2)}, u32[]{:S(2)}) collective-permute-start(bf16[256,1664]{1,0:T(8,128)(2,1)} %collective-permute-done.6.refs_6_), channel_id=1, source_target_pairs={{224,192},{0,224},{32,0},{64,32},{96,64},{128,96},{160,128},{192,1... | collective-permute-start | bytes 2555912 | tf_op jit(solution)/shard_map/ppermute | solution.py:366
  79.3 1.9 %collective-permute-start.8 = (bf16[256,1664]{1,0:T(8,128)(2,1)}, bf16[256,1664]{1,0:T(8,128)(2,1)}, u32[]{:S(2)}, u32[]{:S(2)}) collective-permute-start(bf16[256,1664]{1,0:T(8,128)(2,1)} %collective-permute-done.2.refs_3_), channel_id=1, source_target_pairs={{192,224},{160,0},{96,32},{0,64},{64,96},{32,128},{224,160},{128,1... | collective-permute-start | bytes 2555912 | tf_op jit(solution)/shard_map/ppermute | solution.py:366
  81.3 2.7 %broadcast_select_fusion = (bf16[384,1024]{1,0:T(8,128)(2,1)}, bf16[384,1024]{1,0:T(8,128)(2,1)}) fusion(bf16[384,1024]{1,0:T(8,128)(2,1)} %collective-permute-done.9, bf16[384,1024]{1,0:T(8,128)(2,1)} %collective-permute-done.11, pred[]{:T(512)S(6)} %eq.7, bf16[384,1024]{1,0:T(8,128)(2,1)} %collective-permute-done.12), kind=kLoop, calls=%fused_computation | loop fusion | flops 786432 | bytes 3932161 | tf_op jit(solution)/shard_map/jit(_where)/select_n | solution.py:385
  83.9 8.5 %collective-permute-start.14 = (bf16[384,1024]{1,0:T(8,128)(2,1)}, bf16[384,1024]{1,0:T(8,128)(2,1)}, u32[]{:S(2)}, u32[]{:S(2)}) collective-permute-start(bf16[384,1024]{1,0:T(8,128)(2,1)} %get-tuple-element.41.refs_10_.refs_4_), channel_id=1, source_target_pairs={{14,0},{3,1},{0,2},{5,3},{2,4},{7,5},{4,6},{9,7},{6,8},{11,9},{8,1... | collective-permute-start | bytes 2359304 | tf_op jit(solution)/shard_map/ppermute | solution.py:366
  92.5 15.0 %collective-permute-done.7.refs_7_ = bf16[256,1664]{1,0:T(8,128)(2,1)} collective-permute-done((bf16[256,1664]{1,0:T(8,128)(2,1)}, bf16[256,1664]{1,0:T(8,128)(2,1)}, u32[]{:S(2)}, u32[]{:S(2)}) %collective-permute-start.7) | collective-permute-done | bytes 852000 | tf_op jit(solution)/shard_map/ppermute | solution.py:366
  107.5 1.9 %collective-permute-start.15 = (bf16[256,1664]{1,0:T(8,128)(2,1)}, bf16[256,1664]{1,0:T(8,128)(2,1)}, u32[]{:S(2)}, u32[]{:S(2)}) collective-permute-start(bf16[256,1664]{1,0:T(8,128)(2,1)} %copy-done.7), channel_id=1, source_target_pairs={{192,224},{224,0},{0,32},{32,64},{64,96},{96,128},{128,160},{160,1... | collective-permute-start | bytes 2555912 | tf_op jit(solution)/shard_map/ppermute | solution.py:366
  109.4 5.5 %collective-permute-start.17 = (bf16[256,1664]{1,0:T(8,128)(2,1)}, bf16[256,1664]{1,0:T(8,128)(2,1)}, u32[]{:S(2)}, u32[]{:S(2)}) collective-permute-start(bf16[256,1664]{1,0:T(8,128)(2,1)} %collective-permute-done.10.refs_9_), channel_id=1, source_target_pairs={{194,162},{226,2},{2,226},{34,66},{66,34},{98,130},{130,98},{162,1... | collective-permute-start | bytes 2555912 | tf_op jit(solution)/shard_map/ppermute | solution.py:366
  114.9 1.9 %collective-permute-start.16 = (bf16[256,1664]{1,0:T(8,128)(2,1)}, bf16[256,1664]{1,0:T(8,128)(2,1)}, u32[]{:S(2)}, u32[]{:S(2)}) collective-permute-start(bf16[256,1664]{1,0:T(8,128)(2,1)} %collective-permute-done.8.refs_8_), channel_id=1, source_target_pairs={{0,224},{32,0},{64,32},{128,96},{160,128},{192,160},{113,241},{241... | collective-permute-start | bytes 2555912 | tf_op jit(solution)/shard_map/ppermute | solution.py:366
  117.5 1.1 copy-done.2
  118.7 1.2 copy-done.5
  119.8 1.2 copy-done.8
  121.0 6.6 %shard_map.38.refs_6_ = f32[384,1664]{1,0:T(8,128)S(1)} custom-call(s32[12]{0:T(128)S(1)} %dynamic-slice_bitcast_fusion.index, bf16[1024,1664]{1,0:T(8,128)(2,1)S(1)} %copy-done, bf16[256,1664]{1,0:T(8,128)(2,1)S(1)} %copy-done.2, bf16[256,1664]{1,0:T(8,128)(2,1)S(1)} %copy-done.5, bf16[256,1664]{1,0:T(8,128)(2,1)} %collective-permute-done.2.refs_3_, ...), custom_call_target="tpu_custom_call" | custom-call | flops 1308622848 | bytes 8519680 | tf_op jit(solution)/shard_map/pallas_call | solution.py:332
  127.6 5.8 %shard_map.37.refs_6_ = f32[384,1664]{1,0:T(8,128)S(1)} custom-call(s32[12]{0:T(128)S(1)} %dynamic-slice_bitcast_fusion.index, bf16[1024,1664]{1,0:T(8,128)(2,1)S(1)} %copy-done, bf16[256,1664]{1,0:T(8,128)(2,1)S(1)} %copy-done.3, bf16[256,1664]{1,0:T(8,128)(2,1)S(1)} %copy-done.6, bf16[256,1664]{1,0:T(8,128)(2,1)} %collective-permute-done.2.refs_3_, ...), custom_call_target="tpu_custom_call" | custom-call | flops 1308622848 | bytes 8519680 | tf_op jit(solution)/shard_map/pallas_call | solution.py:332
  133.5 6.3 %collective-permute-done.17.refs_3_ = bf16[256,1664]{1,0:T(8,128)(2,1)} collective-permute-done((bf16[256,1664]{1,0:T(8,128)(2,1)}, bf16[256,1664]{1,0:T(8,128)(2,1)}, u32[]{:S(2)}, u32[]{:S(2)}) %collective-permute-start.17) | collective-permute-done | bytes 852000 | tf_op jit(solution)/shard_map/ppermute | solution.py:366
  139.8 3.7 %shard_map.40 = f32[384,1664]{1,0:T(8,128)S(1)} custom-call(s32[12]{0:T(128)S(1)} %dynamic-slice_bitcast_fusion.index, bf16[1024,1664]{1,0:T(8,128)(2,1)S(1)} %copy-done, bf16[256,1664]{1,0:T(8,128)(2,1)} %collective-permute-done.15.refs_1_, bf16[256,1664]{1,0:T(8,128)(2,1)} %collective-permute-done.16.refs_2_, ...), custom_call_target="tpu_custom_call", output_to_operand_aliasing={{}: (7, {})} | custom-call | flops 1308622848 | bytes 8519680 | tf_op jit(solution)/shard_map/pallas_call | solution.py:332
  143.5 7.6 %collective-permute-start.18 = (f32[384,1664]{1,0:T(8,128)S(1)}, f32[384,1664]{1,0:T(8,128)S(1)}, u32[]{:S(2)}, u32[]{:S(2)}) collective-permute-start(f32[384,1664]{1,0:T(8,128)S(1)} %shard_map.40), channel_id=1, source_target_pairs={{0,16},{1,17},{2,18},{3,19},{4,20},{5,21},{6,22},{7,23},{8,24},{9,... | collective-permute-start | bytes 7667720 | tf_op jit(solution)/shard_map/ppermute | solution.py:366
  151.1 3.2 %shard_map.39 = f32[384,1664]{1,0:T(8,128)S(1)} custom-call(s32[12]{0:T(128)S(1)} %dynamic-slice_bitcast_fusion.index, bf16[1024,1664]{1,0:T(8,128)(2,1)S(1)} %copy-done, bf16[256,1664]{1,0:T(8,128)(2,1)} %collective-permute-done.15.refs_1_, bf16[256,1664]{1,0:T(8,128)(2,1)} %collective-permute-done.16.refs_2_, ...), custom_call_target="tpu_custom_call", output_to_operand_aliasing={{}: (7, {})} | custom-call | flops 1308622848 | bytes 8519680 | tf_op jit(solution)/shard_map/pallas_call | solution.py:332
  154.3 1.3 collective-permute-done.18
  155.6 1.7 %add.21 = f32[384,1664]{1,0:T(8,128)} add(f32[384,1664]{1,0:T(8,128)S(1)} %shard_map.39, f32[384,1664]{1,0:T(8,128)S(1)} %collective-permute-done.18) | non-fusion elementwise | flops 638976 | bytes 7667712 | tf_op jit(solution)/shard_map/add | solution.py:396
  (36 shorter events, 6.0 us)
Async XLA Ops:
  0.0 3.8 %copy-start.10 = (bf16[384,1024]{1,0:T(8,128)(2,1)S(1)}, bf16[384,1024]{1,0:T(8,128)(2,1)}, u32[]{:S(2)}) copy-start(bf16[384,1024]{1,0:T(8,128)(2,1)} %param.3) | copy-start | bytes 2359300
  2.3 115.3 %copy-start = (bf16[1024,1664]{1,0:T(8,128)(2,1)S(1)}, bf16[1024,1664]{1,0:T(8,128)(2,1)}, u32[]{:S(2)}) copy-start(bf16[1024,1664]{1,0:T(8,128)(2,1)} %refs_0_.7) | copy-start | bytes 10223620
  2.3 18.4 %collective-permute-start = (bf16[256,1664]{1,0:T(8,128)(2,1)S(1)}, bf16[256,1664]{1,0:T(8,128)(2,1)S(1)}, u32[]{:S(2)}, u32[]{:S(2)}) collective-permute-start(bf16[256,1664]{1,0:T(8,128)(2,1)S(1)} %get-tuple-element.21), channel_id=1, source_target_pairs={{0,32},{32,64},{64,96},{96,0},{128,160},{160,192},{192,224},{224,1... | collective-permute-start | bytes 2555912 | tf_op jit(solution)/shard_map/ppermute | solution.py:366
  2.9 36.0 %collective-permute-start.1 = (bf16[256,1664]{1,0:T(8,128)(2,1)S(1)}, bf16[256,1664]{1,0:T(8,128)(2,1)S(1)}, u32[]{:S(2)}, u32[]{:S(2)}) collective-permute-start(bf16[256,1664]{1,0:T(8,128)(2,1)S(1)} %get-tuple-element.22), channel_id=1, source_target_pairs={{0,32},{32,64},{64,96},{96,0},{128,160},{160,192},{192,224},{224,1... | collective-permute-start | bytes 2555912 | tf_op jit(solution)/shard_map/ppermute | solution.py:366
  3.8 41.9 %collective-permute-start.5 = (bf16[384,1024]{1,0:T(8,128)(2,1)S(1)}, bf16[384,1024]{1,0:T(8,128)(2,1)S(1)}, u32[]{:S(2)}, u32[]{:S(2)}) collective-permute-start(bf16[384,1024]{1,0:T(8,128)(2,1)S(1)} %copy-done.10), channel_id=1, source_target_pairs={{0,14},{1,15},{2,0},{3,1},{4,2},{5,3},{6,4},{7,5},{8,6},{9,7},{10,... | collective-permute-start | bytes 2359304 | tf_op jit(solution)/shard_map/ppermute | solution.py:366
  11.9 37.2 %collective-permute-start.2 = (bf16[256,1664]{1,0:T(8,128)(2,1)S(1)}, bf16[256,1664]{1,0:T(8,128)(2,1)}, u32[]{:S(2)}, u32[]{:S(2)}) collective-permute-start(bf16[256,1664]{1,0:T(8,128)(2,1)S(1)} %get-tuple-element.23), channel_id=1, source_target_pairs={{0,192},{32,160},{64,96},{96,0},{128,64},{160,32},{192,224},{224,1... | collective-permute-start | bytes 2555912 | tf_op jit(solution)/shard_map/ppermute | solution.py:366
  20.6 43.6 %collective-permute-start.3 = (bf16[256,1664]{1,0:T(8,128)(2,1)S(1)}, bf16[256,1664]{1,0:T(8,128)(2,1)}, u32[]{:S(2)}, u32[]{:S(2)}) collective-permute-start(bf16[256,1664]{1,0:T(8,128)(2,1)S(1)} %collective-permute-done.refs_1_), channel_id=1, source_target_pairs={{32,192},{64,224},{96,0},{0,32},{160,64},{192,96},{224,128},{128,1... | collective-permute-start | bytes 2555912 | tf_op jit(solution)/shard_map/ppermute | solution.py:366
  24.1 0.9 copy-start.1
  38.9 27.3 %collective-permute-start.4 = (bf16[256,1664]{1,0:T(8,128)(2,1)S(1)}, bf16[256,1664]{1,0:T(8,128)(2,1)S(1)}, u32[]{:S(2)}, u32[]{:S(2)}) collective-permute-start(bf16[256,1664]{1,0:T(8,128)(2,1)S(1)} %collective-permute-done.1.refs_2_), channel_id=1, source_target_pairs={{32,192},{64,224},{96,0},{0,32},{160,64},{192,96},{224,128},{128,1... | collective-permute-start | bytes 2555912 | tf_op jit(solution)/shard_map/ppermute | solution.py:366
  41.4 0.9 copy-start.4
  45.7 18.5 %collective-permute-start.9 = (bf16[384,1024]{1,0:T(8,128)(2,1)S(1)}, bf16[384,1024]{1,0:T(8,128)(2,1)}, u32[]{:S(2)}, u32[]{:S(2)}) collective-permute-start(bf16[384,1024]{1,0:T(8,128)(2,1)S(1)} %collective-permute-done.5), channel_id=1, source_target_pairs={{0,0},{1,1},{2,2},{3,3},{4,4},{5,5},{6,6},{7,7},{8,8},{9,9},{10,10... | collective-permute-start | bytes 2359304 | tf_op jit(solution)/shard_map/ppermute | solution.py:366
  49.1 28.3 %collective-permute-start.6 = (bf16[256,1664]{1,0:T(8,128)(2,1)S(1)}, bf16[256,1664]{1,0:T(8,128)(2,1)}, u32[]{:S(2)}, u32[]{:S(2)}) collective-permute-start(bf16[256,1664]{1,0:T(8,128)(2,1)S(1)} %get-tuple-element.25), channel_id=1, source_target_pairs={{0,224},{32,0},{64,32},{96,64},{128,96},{160,128},{192,160},{224,1... | collective-permute-start | bytes 2555912 | tf_op jit(solution)/shard_map/ppermute | solution.py:366
  64.2 17.1 %collective-permute-start.11 = (bf16[384,1024]{1,0:T(8,128)(2,1)}, bf16[384,1024]{1,0:T(8,128)(2,1)}, u32[]{:S(2)}, u32[]{:S(2)}) collective-permute-start(bf16[384,1024]{1,0:T(8,128)(2,1)} %collective-permute-done.9), channel_id=1, source_target_pairs={{0,1},{1,17},{2,3},{3,19},{4,5},{5,21},{6,7},{7,23},{8,9},{9,25},{... | collective-permute-start | bytes 2359304 | tf_op jit(solution)/shard_map/ppermute | solution.py:366
  66.2 0.9 copy-start.7
  67.1 14.1 %collective-permute-start.12 = (bf16[384,1024]{1,0:T(8,128)(2,1)}, bf16[384,1024]{1,0:T(8,128)(2,1)}, u32[]{:S(2)}, u32[]{:S(2)}) collective-permute-start(bf16[384,1024]{1,0:T(8,128)(2,1)} %collective-permute-done.9), channel_id=1, source_target_pairs={{1,16},{3,18},{5,20},{7,22},{9,24},{11,26},{13,28},{15,30},{16,1},... | collective-permute-start | bytes 2359304 | tf_op jit(solution)/shard_map/ppermute | solution.py:366
  68.8 38.7 %collective-permute-start.7 = (bf16[256,1664]{1,0:T(8,128)(2,1)}, bf16[256,1664]{1,0:T(8,128)(2,1)}, u32[]{:S(2)}, u32[]{:S(2)}) collective-permute-start(bf16[256,1664]{1,0:T(8,128)(2,1)} %collective-permute-done.3.refs_4_), channel_id=1, source_target_pairs={{192,224},{224,0},{0,32},{32,64},{64,96},{96,128},{128,160},{160,1... | collective-permute-start | bytes 2555912 | tf_op jit(solution)/shard_map/ppermute | solution.py:366
  77.4 32.0 %collective-permute-start.10 = (bf16[256,1664]{1,0:T(8,128)(2,1)}, bf16[256,1664]{1,0:T(8,128)(2,1)}, u32[]{:S(2)}, u32[]{:S(2)}) collective-permute-start(bf16[256,1664]{1,0:T(8,128)(2,1)} %collective-permute-done.6.refs_6_), channel_id=1, source_target_pairs={{224,192},{0,224},{32,0},{64,32},{96,64},{128,96},{160,128},{192,1... | collective-permute-start | bytes 2555912 | tf_op jit(solution)/shard_map/ppermute | solution.py:366
  79.3 35.6 %collective-permute-start.8 = (bf16[256,1664]{1,0:T(8,128)(2,1)}, bf16[256,1664]{1,0:T(8,128)(2,1)}, u32[]{:S(2)}, u32[]{:S(2)}) collective-permute-start(bf16[256,1664]{1,0:T(8,128)(2,1)} %collective-permute-done.2.refs_3_), channel_id=1, source_target_pairs={{192,224},{160,0},{96,32},{0,64},{64,96},{32,128},{224,160},{128,1... | collective-permute-start | bytes 2555912 | tf_op jit(solution)/shard_map/ppermute | solution.py:366
  83.9 33.6 %collective-permute-start.14 = (bf16[384,1024]{1,0:T(8,128)(2,1)}, bf16[384,1024]{1,0:T(8,128)(2,1)}, u32[]{:S(2)}, u32[]{:S(2)}) collective-permute-start(bf16[384,1024]{1,0:T(8,128)(2,1)} %get-tuple-element.41.refs_10_.refs_4_), channel_id=1, source_target_pairs={{14,0},{3,1},{0,2},{5,3},{2,4},{7,5},{4,6},{9,7},{6,8},{11,9},{8,1... | collective-permute-start | bytes 2359304 | tf_op jit(solution)/shard_map/ppermute | solution.py:366
  92.5 35.1 %collective-permute-start.13 = (bf16[384,1024]{1,0:T(8,128)(2,1)}, bf16[384,1024]{1,0:T(8,128)(2,1)}, u32[]{:S(2)}, u32[]{:S(2)}) collective-permute-start(bf16[384,1024]{1,0:T(8,128)(2,1)} %get-tuple-element.42.refs_10_.refs_4_), channel_id=1, source_target_pairs={{2,0},{3,1},{4,2},{5,3},{6,4},{7,5},{8,6},{9,7},{10,8},{11,9},{12,... | collective-permute-start | bytes 2359304 | tf_op jit(solution)/shard_map/ppermute | solution.py:366
  107.5 26.0 %collective-permute-start.15 = (bf16[256,1664]{1,0:T(8,128)(2,1)}, bf16[256,1664]{1,0:T(8,128)(2,1)}, u32[]{:S(2)}, u32[]{:S(2)}) collective-permute-start(bf16[256,1664]{1,0:T(8,128)(2,1)} %copy-done.7), channel_id=1, source_target_pairs={{192,224},{224,0},{0,32},{32,64},{64,96},{96,128},{128,160},{160,1... | collective-permute-start | bytes 2555912 | tf_op jit(solution)/shard_map/ppermute | solution.py:366
  109.4 30.4 %collective-permute-start.17 = (bf16[256,1664]{1,0:T(8,128)(2,1)}, bf16[256,1664]{1,0:T(8,128)(2,1)}, u32[]{:S(2)}, u32[]{:S(2)}) collective-permute-start(bf16[256,1664]{1,0:T(8,128)(2,1)} %collective-permute-done.10.refs_9_), channel_id=1, source_target_pairs={{194,162},{226,2},{2,226},{34,66},{66,34},{98,130},{130,98},{162,1... | collective-permute-start | bytes 2555912 | tf_op jit(solution)/shard_map/ppermute | solution.py:366
  114.9 24.9 %collective-permute-start.16 = (bf16[256,1664]{1,0:T(8,128)(2,1)}, bf16[256,1664]{1,0:T(8,128)(2,1)}, u32[]{:S(2)}, u32[]{:S(2)}) collective-permute-start(bf16[256,1664]{1,0:T(8,128)(2,1)} %collective-permute-done.8.refs_8_), channel_id=1, source_target_pairs={{0,224},{32,0},{64,32},{128,96},{160,128},{192,160},{113,241},{241... | collective-permute-start | bytes 2555912 | tf_op jit(solution)/shard_map/ppermute | solution.py:366
  117.5 1.2 copy-start.2
  118.7 1.2 copy-start.5
  119.8 1.2 copy-start.8
  121.0 6.6 %copy-start.3 = (bf16[256,1664]{1,0:T(8,128)(2,1)S(1)}, bf16[256,1664]{1,0:T(8,128)(2,1)}, u32[]{:S(2)}) copy-start(bf16[256,1664]{1,0:T(8,128)(2,1)} %copy-done.1) | copy-start | bytes 2555908
  121.0 6.6 %copy-start.6 = (bf16[256,1664]{1,0:T(8,128)(2,1)S(1)}, bf16[256,1664]{1,0:T(8,128)(2,1)}, u32[]{:S(2)}) copy-start(bf16[256,1664]{1,0:T(8,128)(2,1)} %copy-done.4) | copy-start | bytes 2555908
  121.0 6.6 %copy-start.9 = (bf16[256,1664]{1,0:T(8,128)(2,1)S(1)}, bf16[256,1664]{1,0:T(8,128)(2,1)}, u32[]{:S(2)}) copy-start(bf16[256,1664]{1,0:T(8,128)(2,1)} %copy-done.7) | copy-start | bytes 2555908
  143.5 12.1 %collective-permute-start.18 = (f32[384,1664]{1,0:T(8,128)S(1)}, f32[384,1664]{1,0:T(8,128)S(1)}, u32[]{:S(2)}, u32[]{:S(2)}) collective-permute-start(f32[384,1664]{1,0:T(8,128)S(1)} %shard_map.40), channel_id=1, source_target_pairs={{0,16},{1,17},{2,18},{3,19},{4,20},{5,21},{6,22},{7,23},{8,24},{9,... | collective-permute-start | bytes 7667720 | tf_op jit(solution)/shard_map/ppermute | solution.py:366
